TPU v7x, 128 devices: a whole 4x4x4 slice. The times are simulated.
128 devices in a mesh: box: 8 (over y, x_hi), dir: 16 (over z, x_lo, core).
Axes of the slice: x: 4 (x_hi: 2, x_lo: 2; x = x_hi * 2 + x_lo), y: 4, z: 4, core: 2. Of those that a mesh axis runs over, the one named last changes fastest.
Arguments:
- currents: bfloat16 [8192, 512], P(('box', 'dir')), may hold values from -6 to 6
- near_list: int32 [8192, 27], P(('box', 'dir')), may hold values from 0 to 8191, as said below
- far_list: int32 [1024, 20], replicated, may hold values from 0 to 1023, as said below
- far_kind: int32 [1024, 20], replicated, may hold values from 0 to 315
- aggregate: bfloat16 [512, 1024], replicated, may hold values from -0.25 to 0.25
- interp: bfloat16 [1024, 4096], replicated, may hold values from -0.1875 to 0.1875
- receive: bfloat16 [1024, 512], replicated, may hold values from -0.1875 to 0.1875
- shift_angle: float32 [8, 2048], replicated, may hold values from -3.140625 to 3.140625
- translation: float32 [316, 2, 2048], P(None, None, 'dir'), may hold values from -0.6 to 0.6
- near_matrix: bfloat16 [27, 512, 512], replicated, may hold values from -0.0546875 to 0.0546875
Outputs:
- fields: float32 [8192, 512], P(('box', 'dir'))
Inputs may be any that keep to these rules, and one draw needn't show every extreme that they name: `near_list`: entry [l, n] lies within 32 of l. `far_list`: entry [p, j] differs from p by 2 to 64.
All inputs are finite; a program needn't handle non-finite values.
Results may differ from a plain program's by a relative error of at most 0.013.
Values may be sent and summed in bfloat16 or wider, within the bound.
No kernel may reach another device: no remote copies, remote signals or barrier semaphores. Data moves between devices by JAX's collectives and lax.ppermute only.
A program may use at most 128 MiB of HBM per device.

v0:
```python
import jax
import jax.numpy as jnp
from jax import lax
from jax.sharding import PartitionSpec as P


def padded_2(block, sides, width):
    for axis, dim in sides:
        count = lax.axis_size(axis)
        forward = [(i, i + 1) for i in range(count - 1)]
        backward = [(target, source) for source, target in forward]
        low = lax.ppermute(
            lax.slice_in_dim(block, block.shape[dim] - width, None, axis=dim), axis, forward
        )
        high = lax.ppermute(lax.slice_in_dim(block, 0, width, axis=dim), axis, backward)
        block = jnp.concatenate([low, block, high], axis=dim)
    return block


def translate(source_field, row_index, inside, kind_rows, translation):
    rows = row_index.shape[0]
    width = source_field.shape[2]
    real_acc = jnp.zeros((rows, width), jnp.float32)
    imag_acc = jnp.zeros((rows, width), jnp.float32)
    for slot in range(row_index.shape[1]):
        source = jnp.where(inside[:, slot, None, None], source_field[row_index[:, slot]], 0.0)
        operator = translation[kind_rows[:, slot]]
        real_acc = real_acc + operator[:, 0] * source[:, 0] - operator[:, 1] * source[:, 1]
        imag_acc = imag_acc + operator[:, 0] * source[:, 1] + operator[:, 1] * source[:, 0]
    return jnp.stack([real_acc, imag_acc], axis=1)


def on_device(
    currents,
    near_list,
    far_list,
    far_kind,
    aggregate,
    interp,
    receive,
    shift_angle,
    translation,
    near_matrix,
):
    leaf_dev = currents.shape[0]
    directions = shift_angle.shape[1]
    pattern = jnp.dot(currents, aggregate, preferred_element_type=jnp.float32).astype(jnp.bfloat16)
    children = jnp.dot(pattern, interp, preferred_element_type=jnp.float32).reshape(
        leaf_dev // 8, 8, 2, directions
    )
    cosine = jnp.cos(shift_angle)
    sine_part = jnp.sin(shift_angle)
    real_part = jnp.sum(children[:, :, 0] * cosine - children[:, :, 1] * sine_part, axis=1)
    imag_part = jnp.sum(children[:, :, 0] * sine_part + children[:, :, 1] * cosine, axis=1)
    parent = jnp.stack([real_part, imag_part], axis=1)
    upper = lax.all_to_all(
        parent.astype(jnp.bfloat16), "dir", split_axis=2, concat_axis=0, tiled=True
    ).astype(parent.dtype)
    upper_rows = upper.shape[0]
    far_reach = upper_rows // 2
    first_row = lax.axis_index("box") * upper_rows
    my_far = lax.dynamic_slice_in_dim(far_list, first_row, upper_rows, 0)
    my_kind = lax.dynamic_slice_in_dim(far_kind, first_row, upper_rows, 0)
    extended = padded_2(upper.astype(jnp.bfloat16), (("box", 0),), far_reach).astype(upper.dtype)
    local_index = my_far - (first_row - far_reach)
    inside = jnp.ones(my_far.shape, jnp.bool_)
    local_field = translate(extended, local_index, inside, my_kind, translation)
    incoming = lax.all_to_all(
        local_field.astype(jnp.bfloat16), "dir", split_axis=0, concat_axis=2, tiled=True
    ).astype(local_field.dtype)
    rot_real = incoming[:, None, 0] * cosine + incoming[:, None, 1] * sine_part
    rot_imag = incoming[:, None, 1] * cosine - incoming[:, None, 0] * sine_part
    received = (
        jnp.stack([rot_real, rot_imag], axis=2)
        .reshape(leaf_dev, 2 * directions)
        .astype(jnp.bfloat16)
    )
    back_pattern = lax.dot_general(
        received, interp, (((1,), (1,)), ((), ())), preferred_element_type=jnp.float32
    ).astype(jnp.bfloat16)
    fields = jnp.dot(back_pattern, receive, preferred_element_type=jnp.float32)
    near_reach = leaf_dev // 2
    padded = padded_2(currents, ((("box", "dir"), 0),), near_reach)
    local_near = near_list - (lax.axis_index(("box", "dir")) * leaf_dev - near_reach)
    near_rows = padded[local_near].reshape(leaf_dev, -1)
    stacked = near_matrix.reshape(-1, near_matrix.shape[2])
    return fields + jnp.dot(near_rows, stacked, preferred_element_type=jnp.float32)


def solution(mesh):
    placed = (
        P(("box", "dir"), None),
        P(("box", "dir"), None),
        P(),
        P(),
        P(),
        P(),
        P(),
        P(),
        P(None, None, "dir"),
        P(),
    )
    return jax.shard_map(
        on_device, mesh=mesh, in_specs=placed, out_specs=P(("box", "dir"), None), check_vma=False
    )
```

profile of v0, /device:TPU:27, one launch (start us, length us, event | category | flops | bytes accessed | tf_op | source)
XLA Modules:
  0.0 150.7 jit_solution(3382404798901073002)
XLA Ops:
  1.3 5.2 %fusion.2 = f32[64,4096]{1,0:T(8,128)S(1)} fusion(bf16[1024,4096]{1,0:T(8,128)(2,1)} %param.15, bf16[64,512]{1,0:T(8,128)(2,1)} %param.10, bf16[512,1024]{1,0:T(8,128)(2,1)S(1)} %copy-done), kind=kOutput, calls=%fused_computation.45 | convolution fusion | flops 604045312 | bytes 10551296 | tf_op jit(solution)/shard_map/dot_general | solution.py:48
  7.7 1.8 %reshape.367 = bf16[16,2,1024]{2,1,0:T(2,128)(2,1)} reshape(bf16[2048,2,8]{2,1,0:T(2,128)(2,1)S(1)} %bitcast.135) | data formatting | bytes 131072
  9.4 7.1 %all-to-all-start = ((bf16[16,2,1024]{2,1,0:T(2,128)(2,1)}), bf16[16,2,1024]{2,1,0:T(2,128)(2,1)S(1)}, u32[]{:S(2)}, u32[]{:S(2)}) async-start(bf16[16,2,1024]{2,1,0:T(2,128)(2,1)} %reshape.367), calls=%async_computation | async-start | bytes 131072 | tf_op jit(solution)/shard_map/all_to_all | solution.py:56
  16.5 3.3 %collective-permute-start.2 = (bf16[32,512]{1,0:T(8,128)(2,1)S(1)}, bf16[32,512]{1,0:T(8,128)(2,1)S(1)}, u32[]{:S(2)}, u32[]{:S(2)}) collective-permute-start(bf16[32,512]{1,0:T(8,128)(2,1)S(1)} %get-tuple-element.35), channel_id=1, source_target_pairs={{0,1},{1,2},{2,3},{3,4},{4,5},{5,6},{6,7},{7,8},{8,9},{9,10},{10,1... | collective-permute-start | bytes 98312 | tf_op jit(solution)/shard_map/ppermute | solution.py:12
  19.9 1.9 %collective-permute-start.3 = (bf16[32,512]{1,0:T(8,128)(2,1)S(1)}, bf16[32,512]{1,0:T(8,128)(2,1)S(1)}, u32[]{:S(2)}, u32[]{:S(2)}) collective-permute-start(bf16[32,512]{1,0:T(8,128)(2,1)S(1)} %get-tuple-element.36), channel_id=1, source_target_pairs={{1,0},{2,1},{3,2},{4,3},{5,4},{6,5},{7,6},{8,7},{9,8},{10,9},{11,1... | collective-permute-start | bytes 98312 | tf_op jit(solution)/shard_map/ppermute | solution.py:15
  25.4 1.4 gather_fusion.12
  28.1 1.4 gather_fusion.16
  29.5 1.4 gather_fusion.18
  30.9 1.4 gather_fusion.20
  33.7 1.4 gather_fusion.24
  35.1 1.4 gather_fusion.26
  36.5 1.4 gather_fusion.28
  37.9 1.4 gather_fusion.30
  39.3 1.4 gather_fusion.32
  42.1 1.4 gather_fusion.36
  43.4 1.4 gather_fusion.6
  46.2 1.4 gather_fusion.2
  47.6 1.4 gather_fusion.38
  50.4 1.4 gather_fusion
  59.3 3.8 %collective-permute-start = (bf16[64,2,128]{2,1,0:T(2,128)(2,1)S(1)}, bf16[64,2,128]{2,1,0:T(2,128)(2,1)S(1)}, u32[]{:S(2)}, u32[]{:S(2)}) collective-permute-start(bf16[64,2,128]{2,1,0:T(2,128)(2,1)S(1)} %bitcast.145), channel_id=1, source_target_pairs={{0,16},{16,32},{32,48},{48,64},{64,80},{80,96},{96,112},{1,17},{17... | collective-permute-start | bytes 98312 | tf_op jit(solution)/shard_map/ppermute | solution.py:12
  63.1 4.1 %collective-permute-start.1 = (bf16[64,2,128]{2,1,0:T(2,128)(2,1)S(1)}, bf16[64,2,128]{2,1,0:T(2,128)(2,1)S(1)}, u32[]{:S(2)}, u32[]{:S(2)}) collective-permute-start(bf16[64,2,128]{2,1,0:T(2,128)(2,1)S(1)} %bitcast.146), channel_id=1, source_target_pairs={{16,0},{32,16},{48,32},{64,48},{80,64},{96,80},{112,96},{17,1},{33... | collective-permute-start | bytes 98312 | tf_op jit(solution)/shard_map/ppermute | solution.py:15
  67.2 6.1 %gather_fusion.40 = bf16[1728,512]{1,0:T(8,128)(2,1)} fusion(bf16[128,512]{1,0:T(8,128)(2,1)S(1)} %pad_maximum_fusion, s32[2048]{0:T(1024)S(1)} %pad_clamp_fusion), kind=kCustom, calls=%fused_computation.40 | custom fusion | bytes 3545856 | tf_op jit(solution)/shard_map/gather | solution.py:85
  73.3 2.5 %reshape.357 = bf16[64,27,512]{2,1,0:T(8,128)(2,1)S(1)} reshape(bf16[1728,512]{1,0:T(8,128)(2,1)} %gather_fusion.40) | data formatting | bytes 3538944 | tf_op jit(solution)/shard_map/gather | solution.py:85
  78.1 1.5 gather_fusion.1
  79.6 1.5 %gather_fusion.11 = f32[128,2,128]{2,1,0:T(2,128)} fusion(f32[256,2,128]{2,1,0:T(2,128)S(1)} %maximum_convert_fusion, s32[1024]{0:T(1024)} %get-tuple-element.73), kind=kCustom, calls=%fused_computation.11 | custom fusion | bytes 262656 | tf_op jit(solution)/shard_map/gather | solution.py:26
  81.1 1.5 gather_fusion.13
  82.6 1.5 gather_fusion.15
  84.1 1.5 gather_fusion.17
  85.6 1.5 gather_fusion.19
  87.1 1.5 %gather_fusion.21 = f32[128,2,128]{2,1,0:T(2,128)} fusion(f32[256,2,128]{2,1,0:T(2,128)S(1)} %maximum_convert_fusion, s32[1024]{0:T(1024)} %get-tuple-element.68), kind=kCustom, calls=%fused_computation.21 | custom fusion | bytes 262656 | tf_op jit(solution)/shard_map/gather | solution.py:26
  88.6 1.5 gather_fusion.23
  90.1 1.5 gather_fusion.25
  91.6 1.5 %gather_fusion.27 = f32[128,2,128]{2,1,0:T(2,128)} fusion(f32[256,2,128]{2,1,0:T(2,128)S(1)} %maximum_convert_fusion, s32[1024]{0:T(1024)} %get-tuple-element.65), kind=kCustom, calls=%fused_computation.27 | custom fusion | bytes 262656 | tf_op jit(solution)/shard_map/gather | solution.py:26
  93.2 1.5 %gather_fusion.29 = f32[128,2,128]{2,1,0:T(2,128)} fusion(f32[256,2,128]{2,1,0:T(2,128)S(1)} %maximum_convert_fusion, s32[1024]{0:T(1024)} %get-tuple-element.64), kind=kCustom, calls=%fused_computation.29 | custom fusion | bytes 262656 | tf_op jit(solution)/shard_map/gather | solution.py:26
  94.7 1.5 %gather_fusion.31 = f32[128,2,128]{2,1,0:T(2,128)} fusion(f32[256,2,128]{2,1,0:T(2,128)S(1)} %maximum_convert_fusion, s32[1024]{0:T(1024)} %get-tuple-element.63), kind=kCustom, calls=%fused_computation.31 | custom fusion | bytes 262656 | tf_op jit(solution)/shard_map/gather | solution.py:26
  96.2 1.5 gather_fusion.33
  97.7 1.5 %gather_fusion.35 = f32[128,2,128]{2,1,0:T(2,128)} fusion(f32[256,2,128]{2,1,0:T(2,128)S(1)} %maximum_convert_fusion, s32[1024]{0:T(1024)} %get-tuple-element.61), kind=kCustom, calls=%fused_computation.35 | custom fusion | bytes 262656 | tf_op jit(solution)/shard_map/gather | solution.py:26
  99.2 1.5 %gather_fusion.37 = f32[128,2,128]{2,1,0:T(2,128)} fusion(f32[256,2,128]{2,1,0:T(2,128)S(1)} %maximum_convert_fusion, s32[1024]{0:T(1024)} %get-tuple-element.60), kind=kCustom, calls=%fused_computation.37 | custom fusion | bytes 262656 | tf_op jit(solution)/shard_map/gather | solution.py:26
  100.7 1.4 gather_fusion.7
  102.1 1.4 gather_fusion.9
  103.5 1.5 %gather_fusion.39 = f32[128,2,128]{2,1,0:T(2,128)} fusion(f32[256,2,128]{2,1,0:T(2,128)S(1)} %maximum_convert_fusion, s32[1024]{0:T(1024)} %get-tuple-element.59), kind=kCustom, calls=%fused_computation.39 | custom fusion | bytes 262656 | tf_op jit(solution)/shard_map/gather | solution.py:26
  105.0 1.4 gather_fusion.3
  106.4 1.4 gather_fusion.5
  107.8 8.0 %subtract_convert_fusion.1 = bf16[128,1,128]{2,1,0:T(2,128)(2,1)S(1)} fusion(f32[128,2,128]{2,1,0:T(2,128)} %gather_fusion.39, f32[128,2,128]{2,1,0:T(2,128)} %gather_fusion.38, f32[128,2,128]{2,1,0:T(2,128)} %gather_fusion.37, f32[128,2,128]{2,1,0:T(2,128)} %gather_fusion.36, f32[128,2,128]{2,1,0:T(2,128)} %gather_fusion.35, ...), kind=kLoop, calls=%fused_computation.63 | loop fusion | flops 1310720 | bytes 5275648 | tf_op jit(solution)/shard_map/convert.5
  115.8 7.9 %add_convert_fusion.1 = bf16[128,1,128]{2,1,0:T(2,128)(2,1)S(1)} fusion(f32[128,2,128]{2,1,0:T(2,128)} %gather_fusion.39, f32[128,2,128]{2,1,0:T(2,128)} %gather_fusion.38, f32[128,2,128]{2,1,0:T(2,128)} %gather_fusion.37, f32[128,2,128]{2,1,0:T(2,128)} %gather_fusion.36, f32[128,2,128]{2,1,0:T(2,128)} %gather_fusion.35, f32[128,2,128]{2,1,0:T(2,128)} %gather_fusion.34, ...), kind=kLoop, calls=%fused_computation.62 | loop fusion | flops 1310720 | bytes 5275648 | tf_op jit(solution)/shard_map/convert.6
  124.5 8.5 %all-to-all-start.1 = ((bf16[128,2,128]{2,1,0:T(2,128)(2,1)}), bf16[128,2,128]{2,1,0:T(2,128)(2,1)S(1)}, u32[]{:S(2)}, u32[]{:S(2)}) async-start(bf16[128,2,128]{2,1,0:T(2,128)(2,1)} %pad_maximum_fusion.2), calls=%async_computation.1 | async-start | bytes 131072 | tf_op jit(solution)/shard_map/all_to_all | solution.py:68
  133.0 8.0 %fusion.3 = f32[64,512]{1,0:T(8,128)S(1)} fusion(bf16[27,512,512]{2,1,0:T(8,128)(2,1)} %param.19, bf16[64,27,512]{2,1,0:T(8,128)(2,1)S(1)} %reshape.357), kind=kOutput, calls=%fused_computation.47 | convolution fusion | flops 905969664 | bytes 16056320 | tf_op jit(solution)/shard_map/dot_general | solution.py:87
  143.6 7.1 %convolution_add_fusion = f32[64,512]{1,0:T(8,128)} fusion(f32[64,512]{1,0:T(8,128)S(1)} %fusion.3, bf16[1024,512]{1,0:T(8,128)(2,1)} %param.16, bf16[64,4096]{1,0:T(8,128)(2,1)S(1)} %bitcast.137, bf16[1024,4096]{1,0:T(8,128)(2,1)} %param.15), kind=kOutput, calls=%fused_computation.46 | convolution fusion | flops 604078080 | bytes 10223616 | tf_op jit(solution)/shard_map/dot_general | solution.py:81
  (83 shorter events, 25.8 us)
Async XLA Ops:
  0.0 1.3 copy-start
  0.0 16.5 %copy-start.2 = (bf16[64,512]{1,0:T(8,128)(2,1)S(1)}, bf16[64,512]{1,0:T(8,128)(2,1)}, u32[]{:S(2)}) copy-start(bf16[64,512]{1,0:T(8,128)(2,1)} %param.10) | copy-start | bytes 196612
  0.0 24.6 %copy-start.1 = (f32[316,2,128]{2,1,0:T(2,128)S(1)}, f32[316,2,128]{2,1,0:T(2,128)}, u32[]{:S(2)}) copy-start(f32[316,2,128]{2,1,0:T(2,128)} %param.18) | copy-start | bytes 970756
  1.3 23.3 %copy-start.3 = (f32[8,2048]{1,0:T(8,128)}, f32[8,2048]{1,0:T(8,128)S(1)}, u32[]{:S(2)}) copy-start(f32[8,2048]{1,0:T(8,128)S(1)} %get-tuple-element.33) | copy-start | bytes 196612
  1.3 23.3 %copy-start.5 = (f32[8,2048]{1,0:T(8,128)}, f32[8,2048]{1,0:T(8,128)S(1)}, u32[]{:S(2)}) copy-start(f32[8,2048]{1,0:T(8,128)S(1)} %get-tuple-element.34) | copy-start | bytes 196612
  1.3 50.5 %copy-start.9 = (s32[64,27]{0,1:T(8,128)S(1)}, s32[64,27]{0,1:T(8,128)}, u32[]{:S(2)}) copy-start(s32[64,27]{0,1:T(8,128)} %param.11) | copy-start | bytes 20740
  9.4 48.0 %all-to-all-start = ((bf16[16,2,1024]{2,1,0:T(2,128)(2,1)}), bf16[16,2,1024]{2,1,0:T(2,128)(2,1)S(1)}, u32[]{:S(2)}, u32[]{:S(2)}) async-start(bf16[16,2,1024]{2,1,0:T(2,128)(2,1)} %reshape.367), calls=%async_computation | async-start | bytes 131072 | tf_op jit(solution)/shard_map/all_to_all | solution.py:56
  16.5 50.7 %collective-permute-start.2 = (bf16[32,512]{1,0:T(8,128)(2,1)S(1)}, bf16[32,512]{1,0:T(8,128)(2,1)S(1)}, u32[]{:S(2)}, u32[]{:S(2)}) collective-permute-start(bf16[32,512]{1,0:T(8,128)(2,1)S(1)} %get-tuple-element.35), channel_id=1, source_target_pairs={{0,1},{1,2},{2,3},{3,4},{4,5},{5,6},{6,7},{7,8},{8,9},{9,10},{10,1... | collective-permute-start | bytes 98312 | tf_op jit(solution)/shard_map/ppermute | solution.py:12
  19.9 47.3 %collective-permute-start.3 = (bf16[32,512]{1,0:T(8,128)(2,1)S(1)}, bf16[32,512]{1,0:T(8,128)(2,1)S(1)}, u32[]{:S(2)}, u32[]{:S(2)}) collective-permute-start(bf16[32,512]{1,0:T(8,128)(2,1)S(1)} %get-tuple-element.36), channel_id=1, source_target_pairs={{1,0},{2,1},{3,2},{4,3},{5,4},{6,5},{7,6},{8,7},{9,8},{10,9},{11,1... | collective-permute-start | bytes 98312 | tf_op jit(solution)/shard_map/ppermute | solution.py:15
  59.3 16.6 %collective-permute-start = (bf16[64,2,128]{2,1,0:T(2,128)(2,1)S(1)}, bf16[64,2,128]{2,1,0:T(2,128)(2,1)S(1)}, u32[]{:S(2)}, u32[]{:S(2)}) collective-permute-start(bf16[64,2,128]{2,1,0:T(2,128)(2,1)S(1)} %bitcast.145), channel_id=1, source_target_pairs={{0,16},{16,32},{32,48},{48,64},{64,80},{80,96},{96,112},{1,17},{17... | collective-permute-start | bytes 98312 | tf_op jit(solution)/shard_map/ppermute | solution.py:12
  63.1 12.9 %collective-permute-start.1 = (bf16[64,2,128]{2,1,0:T(2,128)(2,1)S(1)}, bf16[64,2,128]{2,1,0:T(2,128)(2,1)S(1)}, u32[]{:S(2)}, u32[]{:S(2)}) collective-permute-start(bf16[64,2,128]{2,1,0:T(2,128)(2,1)S(1)} %bitcast.146), channel_id=1, source_target_pairs={{16,0},{32,16},{48,32},{64,48},{80,64},{96,80},{112,96},{17,1},{33... | collective-permute-start | bytes 98312 | tf_op jit(solution)/shard_map/ppermute | solution.py:15
  75.9 0.6 copy-start.7
  76.5 0.6 copy-start.8
  124.5 16.5 %all-to-all-start.1 = ((bf16[128,2,128]{2,1,0:T(2,128)(2,1)}), bf16[128,2,128]{2,1,0:T(2,128)(2,1)S(1)}, u32[]{:S(2)}, u32[]{:S(2)}) async-start(bf16[128,2,128]{2,1,0:T(2,128)(2,1)} %pad_maximum_fusion.2), calls=%async_computation.1 | async-start | bytes 131072 | tf_op jit(solution)/shard_map/all_to_all | solution.py:68
  132.9 8.1 %copy-start.4 = (f32[8,2048]{1,0:T(8,128)S(1)}, f32[8,2048]{1,0:T(8,128)}, u32[]{:S(2)}) copy-start(f32[8,2048]{1,0:T(8,128)} %copy-done.3) | copy-start | bytes 196612
  133.0 8.1 %copy-start.6 = (f32[8,2048]{1,0:T(8,128)S(1)}, f32[8,2048]{1,0:T(8,128)}, u32[]{:S(2)}) copy-start(f32[8,2048]{1,0:T(8,128)} %copy-done.5) | copy-start | bytes 196612
where the time goes:
time: 152 us; the launch traced here: 151 us
  local copies, waits for them, and re-layouts  72.8 us (48%)
  starting transfers between devices  28.7 us (19%)
  other arithmetic  28.4 us (19%)
  matrix products  20.4 us (13%)
    gather x20, local copies, waits for them, and re-layouts, translate(): source_field[row_index[:, slot]]  29.7 us
    gather x20, local copies, waits for them, and re-layouts, translate(): operator = translation[kind_rows[:, slot]]  27.1 us
    another operation x3, other arithmetic  16.9 us
    gather x2, local copies, waits for them, and re-layouts, on_device(): near_rows = padded[local_near].reshape(leaf_dev, -1)  8.59 us
    all_to_all x1, starting transfers between devices, on_device(): lax.all_to_all(local_field.astype(jnp.bfloat16), 'dir', split_axis=0, con...  8.48 us
    dot_general x1, matrix products, on_device(): jnp.dot(near_rows, stacked, preferred_element_type=jnp.float32)  8.04 us
    dot_general x1, matrix products, on_device(): fields = jnp.dot(back_pattern, receive, preferred_element_type=jnp.float32)  7.14 us
    all_to_all x1, starting transfers between devices, on_device(): lax.all_to_all(parent.astype(jnp.bfloat16), 'dir', split_axis=2, concat_a...  7.1 us
  transfers between devices with their start and end apart: 6, of which 0 were waited for; matrix products, arithmetic and copies ran while one was open for 36% of the time, Pallas kernels for 0%

commit v1 on v0

v1 whole, which is shorter than its diff:
```python
import functools

import jax
import jax.numpy as jnp
from jax import lax
from jax.experimental import pallas as pl
from jax.experimental.pallas import tpu as pltpu
from jax.sharding import PartitionSpec as P

BF16, F32, I32 = jnp.bfloat16, jnp.float32, jnp.int32
BOTH = ("box", "dir")
VMEM = pltpu.VMEM


def whole(space=VMEM):
    return pl.BlockSpec(memory_space=space)


def call(body, out, args, specs, scratch, mib, flops, moved):
    return pl.pallas_call(
        body,
        out_shape=out,
        in_specs=specs,
        out_specs=jax.tree.map(lambda _: whole(), out),
        scratch_shapes=scratch,
        compiler_params=pltpu.CompilerParams(vmem_limit_bytes=mib << 20),
        cost_estimate=pl.CostEstimate(flops=flops, bytes_accessed=moved, transcendentals=0),
    )(*args)


def dot(a, b, ca=1, cb=0):
    return lax.dot_general(a, b, (((ca,), (cb,)), ((), ())), preferred_element_type=F32)


def up_kernel(cur_ref, agg_ref, cos_ref, sin_ref, interp, out_ref, buf, sems):
    chunks, width = buf.shape[0] // 2, buf.shape[2]
    copies = []
    for j in range(2 * chunks):
        copies.append(
            pltpu.make_async_copy(interp.at[:, pl.ds(j * width, width)], buf.at[j], sems.at[j])
        )
    for j in range(chunks):
        copies[j].start()
        copies[chunks + j].start()
    rows = cur_ref.shape[0]
    parents = rows // 8
    r = lax.broadcasted_iota(I32, (rows, rows), 0)
    c = lax.broadcasted_iota(I32, (rows, rows), 1)
    pick = jnp.where(c == 8 * (r % parents) + r // parents, 1.0, 0.0).astype(BF16)
    cur = dot(pick, cur_ref[...]).astype(BF16)
    pattern = dot(cur, agg_ref[...]).astype(BF16)
    for j in range(chunks):
        copies[j].wait()
        copies[chunks + j].wait()
        re = dot(pattern, buf[j])
        im = dot(pattern, buf[chunks + j])
        acc_re = jnp.zeros((parents, width), F32)
        acc_im = jnp.zeros((parents, width), F32)
        for k in range(8):
            cosine = cos_ref[pl.ds(k, 1), pl.ds(j * width, width)]
            sine = sin_ref[pl.ds(k, 1), pl.ds(j * width, width)]
            a, b = re[k * parents : (k + 1) * parents], im[k * parents : (k + 1) * parents]
            acc_re += a * cosine - b * sine
            acc_im += a * sine + b * cosine
        for h in range(width // 128):
            s = slice(h * 128, (h + 1) * 128)
            out_ref[j * (width // 128) + h, 0:parents, :] = acc_re[:, s].astype(BF16)
            out_ref[j * (width // 128) + h, parents : 2 * parents, :] = acc_im[:, s].astype(BF16)


def operators_kernel(kind_ref, table_ref, out_ref):
    rows, slots = kind_ref.shape
    lane = lax.broadcasted_iota(I32, (rows, table_ref.shape[0]), 1)
    for j in range(slots):
        hot = jnp.where(lane == kind_ref[:, j : j + 1], 1.0, 0.0).astype(BF16)
        out_ref[j] = dot(hot, table_ref[...]).astype(BF16)


def translate_kernel(upper_ref, index_ref, operator_ref, out_ref):
    sources = upper_ref.shape[0] * 16
    rows, slots = index_ref.shape
    field = jnp.concatenate(
        [
            upper_ref[:, 0:16, :].reshape(sources, 128),
            upper_ref[:, 16:32, :].reshape(sources, 128),
        ],
        axis=1,
    )
    lane = lax.broadcasted_iota(I32, (rows, sources), 1)
    acc_re = jnp.zeros((rows, 128), F32)
    acc_im = jnp.zeros((rows, 128), F32)
    for j in range(slots):
        hot = jnp.where(lane == index_ref[:, j : j + 1], 1.0, 0.0).astype(BF16)
        x = dot(hot, field)
        op = operator_ref[j].astype(F32)
        xr, xi = x[:, :128], x[:, 128:]
        tr, ti = op[:, :128], op[:, 128:]
        acc_re += tr * xr - ti * xi
        acc_im += tr * xi + ti * xr
    blocks = out_ref.shape[0]
    out_ref[:, 0:8, :] = acc_re.reshape(blocks, 8, 128).astype(BF16)
    out_ref[:, 8:16, :] = acc_im.reshape(blocks, 8, 128).astype(BF16)


def down_kernel(inc_ref, cos_ref, sin_ref, receive_ref, near_ref, interp, out_ref, buf, received, sems):
    chunks, width = buf.shape[0], buf.shape[1]
    copies = []
    for j in range(chunks):
        copies.append(
            pltpu.make_async_copy(interp.at[pl.ds(j * width, width)], buf.at[j], sems.at[j])
        )
        copies[j].start()
    leaves = received.shape[0]
    half = received.shape[1] // 2
    for s in range(inc_ref.shape[0]):
        lanes = slice(s * 128, (s + 1) * 128)
        block = inc_ref[s].astype(F32)
        re, im = block[0:8][:, None, :], block[8:16][:, None, :]
        cosine, sine = cos_ref[:, lanes][None], sin_ref[:, lanes][None]
        received[:, s * 128 : (s + 1) * 128] = (
            (re * cosine + im * sine).reshape(leaves, 128).astype(BF16)
        )
        received[:, half + s * 128 : half + (s + 1) * 128] = (
            (im * cosine - re * sine).reshape(leaves, 128).astype(BF16)
        )
    total = near_ref[...]
    for j in range(chunks):
        copies[j].wait()
        back = dot(received[...], buf[j], 1, 1).astype(BF16)
        total += dot(back, receive_ref[pl.ds(j * width, width), :])
    out_ref[...] = total


def near_kernel(cur_ref, col_ref, near_hbm, out_ref, buf, sems):
    slots = col_ref.shape[1]
    copies = []
    for n in range(slots):
        copies.append(pltpu.make_async_copy(near_hbm.at[n], buf.at[n], sems.at[n]))
        copies[n].start()
    rows = col_ref.shape[0]
    lane = lax.broadcasted_iota(I32, (rows, cur_ref.shape[0]), 1)
    total = jnp.zeros(out_ref.shape, F32)
    for n in range(slots):
        hot = jnp.where(lane == col_ref[:, n : n + 1], 1.0, 0.0).astype(BF16)
        picked = dot(hot, cur_ref[...]).astype(BF16)
        copies[n].wait()
        total += dot(picked, buf[n])
    out_ref[...] = total


def halo_partner(i, boxes, dirs):
    b, d = divmod(i, dirs)
    quarter = dirs // 4
    z, r = divmod(d, quarter)
    other = b + 1 if z >= 2 else b - 1
    if other < 0 or other >= boxes:
        return i ^ 1
    return other * dirs + (3 - z) * quarter + r


def on_device(
    boxes,
    dirs,
    currents,
    near_list,
    far_list,
    far_kind,
    aggregate,
    interp,
    receive,
    shift_angle,
    translation,
    near_matrix,
):
    leaves, width = currents.shape
    n = boxes * dirs
    me = lax.axis_index(BOTH)
    box = lax.axis_index("box")
    odd = me % 2
    parents = leaves // 8 * dirs
    directions = shift_angle.shape[1]

    far_half = lax.ppermute(currents, BOTH, [(i, halo_partner(i, boxes, dirs)) for i in range(n)])
    outward = lax.dynamic_slice_in_dim(currents, odd * (leaves // 2), leaves // 2, 0)
    inward = lax.dynamic_slice_in_dim(currents, (1 - odd) * (leaves // 2), leaves // 2, 0)
    cross = [(i, min(max(i + (1 if i % 2 else -1), 0), n - 1)) for i in range(n)]
    from_cross = lax.ppermute(outward, BOTH, cross)
    from_sibling = lax.ppermute(inward, BOTH, [(i, i ^ 1) for i in range(n)])

    cosine, sine = jnp.cos(shift_angle), jnp.sin(shift_angle)

    slots = far_list.shape[1]
    my_far = lax.dynamic_slice_in_dim(far_list, box * parents, parents, 0)
    my_kind = lax.dynamic_slice_in_dim(far_kind, box * parents, parents, 0)
    kinds = translation.shape[0]
    table = jnp.concatenate([translation[:, 0], translation[:, 1]], axis=1).astype(BF16)
    table = jnp.pad(table, ((0, -kinds % 128), (0, 0)))
    operators = call(
        operators_kernel,
        jax.ShapeDtypeStruct((slots, parents, 256), BF16),
        (my_kind, table),
        [whole()] * 2,
        [],
        16,
        2 * slots * parents * 384 * 256,
        4 << 20,
    )
    e = my_far - box * parents + parents // 2
    q = e - parents // 2
    own = (q // 8) * 16 + q % 8
    g = jnp.where(q < 0, e, q - parents)
    low = ((1 - g // 32) * 4 + (g // 8) % 4) * 16 + 8 + g % 8
    high = ((3 - g // 32) * 4 + (g // 8) % 4) * 16 + 8 + g % 8
    index = jnp.where(q < 0, low, jnp.where(q < parents, own, high))

    rows = jnp.concatenate([currents, far_half], axis=0)
    up = call(
        up_kernel,
        jax.ShapeDtypeStruct((dirs, 4 * leaves // 8, 128), BF16),
        (rows, aggregate, cosine, sine, interp),
        [whole()] * 4 + [whole(pl.ANY)],
        [pltpu.VMEM((16, interp.shape[0], 256), BF16), pltpu.SemaphoreType.DMA((16,))],
        20,
        2 * 128 * 1024 * 4608,
        10 << 20,
    )
    upper = lax.all_to_all(up, "dir", split_axis=0, concat_axis=0, tiled=True)

    near_rows = jnp.concatenate([currents, from_sibling, from_cross], axis=0)
    rel = near_list - me * leaves
    reach = leaves // 2
    outside = jnp.where((rel < 0) == (odd == 0), leaves + reach, leaves) + rel % reach
    column = jnp.where((rel >= 0) & (rel < leaves), rel, outside)
    near = call(
        near_kernel,
        jax.ShapeDtypeStruct((leaves, width), F32),
        (near_rows, column, near_matrix),
        [whole()] * 2 + [whole(pl.ANY)],
        [pltpu.VMEM(near_matrix.shape, BF16), pltpu.SemaphoreType.DMA((near_matrix.shape[0],))],
        24,
        2 * leaves * 27 * 512 * 640,
        15 << 20,
    )

    local = call(
        translate_kernel,
        jax.ShapeDtypeStruct((dirs, 2 * leaves // 8, 128), BF16),
        (upper, index, operators),
        [whole()] * 3,
        [],
        16,
        2 * slots * parents * 256 * 256,
        2 << 20,
    )
    incoming = lax.all_to_all(local, "dir", split_axis=0, concat_axis=0, tiled=True)

    return call(
        down_kernel,
        jax.ShapeDtypeStruct((leaves, width), F32),
        (incoming, cosine, sine, receive, near, interp),
        [whole()] * 5 + [whole(pl.ANY)],
        [
            pltpu.VMEM((4, interp.shape[0] // 4, interp.shape[1]), BF16),
            pltpu.VMEM((leaves, 2 * directions), BF16),
            pltpu.SemaphoreType.DMA((4,)),
        ],
        20,
        2 * 64 * 4096 * 1536,
        10 << 20,
    )


def solution(mesh):
    placed = (
        P(BOTH, None),
        P(BOTH, None),
        P(),
        P(),
        P(),
        P(),
        P(),
        P(),
        P(None, None, "dir"),
        P(),
    )
    body = functools.partial(on_device, mesh.shape["box"], mesh.shape["dir"])
    return jax.shard_map(
        body, mesh=mesh, in_specs=placed, out_specs=P(BOTH, None), check_vma=False
    )
```

time: 152 us -> 66.7 us (0.44)
  local copies, waits for them, and re-layouts: 72.8 us -> 17.6 us
  other arithmetic: 28.4 us -> 1.13 us
  Pallas kernels: 0 us -> 21.7 us
  matrix products: 20.4 us -> 0 us
  starting transfers between devices: 28.7 us -> 21.1 us
  waiting for transfers between devices: 0.02 us -> 4.35 us
    gather x42 -> x0, local copies, waits for them, and re-layouts: 65.4 us -> none  [the longest x20 29.7 us: translate(): source_field[row_index[:, slot]]]
    pallas_call x0 -> x5, Pallas kernels: none -> 21.7 us  [call(): pl.pallas_call(body, out_shape=out, in_specs=specs, out_specs=jax.tree.ma...]
    dot_general x3 -> x0, matrix products: 20.4 us -> none  [the longest x1 8.04 us: on_device(): jnp.dot(near_rows, stacked, preferred_element_type=jnp.float32)]
    another operation x5 -> x0, other arithmetic: 17.7 us -> none
    unnamed x23 -> x14, local copies, waits for them, and re-layouts: 4.4 us -> 15 us
    gather x24 -> x0, other arithmetic: 5.46 us -> none  [the longest x11 5.39 us: translate(): source_field[row_index[:, slot]]]
    ppermute x4 -> x3, starting transfers between devices: 13.1 us -> 8.64 us  [the longest x1 5.5 us: on_device(): lax.ppermute(currents, BOTH, [(i, halo_partner(i, boxes, dirs)) for i in...]
    all_to_all x2, waiting for transfers between devices: 0.01 us -> 4.34 us  [the longest x1 4.34 us: on_device(): upper = lax.all_to_all(up, 'dir', split_axis=0, concat_axis=0, tiled=True)]
  transfers between devices with their start and end apart: 6 -> 5, of which waited for: 0 -> 1; matrix products, arithmetic and copies ran while one was open for 36% -> 7% of each run, Pallas kernels for 0% -> 13%
where the time goes in v1:
time: 66.7 us; the launch traced here: 66 us
  Pallas kernels  21.7 us (33%)
  starting transfers between devices  21.1 us (32%)
  local copies, waits for them, and re-layouts  17.6 us (26%)
  waiting for transfers between devices  4.35 us (7%)
  other arithmetic  1.13 us (2%)
    pallas_call x5, Pallas kernels, call(): pl.pallas_call(body, out_shape=out, in_specs=specs, out_specs=jax.tree.ma...  21.7 us
    unnamed x14, local copies, waits for them, and re-layouts  15 us
    all_to_all x1, starting transfers between devices, on_device(): upper = lax.all_to_all(up, 'dir', split_axis=0, concat_axis=0, tiled=True)  7.51 us
    ppermute x1, starting transfers between devices, on_device(): lax.ppermute(currents, BOTH, [(i, halo_partner(i, boxes, dirs)) for i in...  5.5 us
    all_to_all x1, starting transfers between devices, on_device(): lax.all_to_all(local, 'dir', split_axis=0, concat_axis=0, tiled=True)  4.92 us
    all_to_all x1, waiting for transfers between devices, on_device(): upper = lax.all_to_all(up, 'dir', split_axis=0, concat_axis=0, tiled=True)  4.34 us
    ppermute x1, starting transfers between devices, on_device(): from_cross = lax.ppermute(outward, BOTH, cross)  2.19 us
  transfers between devices with their start and end apart: 5, of which 1 were waited for; matrix products, arithmetic and copies ran while one was open for 7% of the time, Pallas kernels for 13%

profile of v1, /device:TPU:27, one launch (start us, length us, event | category | flops | bytes accessed | tf_op | source)
XLA Modules:
  0.0 66.0 jit_solution(16518500841111479362)
XLA Ops:
  0.0 5.5 %collective-permute-start = (bf16[64,512]{1,0:T(8,128)(2,1)}, bf16[64,512]{1,0:T(8,128)(2,1)S(1)}, u32[]{:S(2)}, u32[]{:S(2)}) collective-permute-start(bf16[64,512]{1,0:T(8,128)(2,1)} %param.10), channel_id=1, source_target_pairs={{0,1},{1,0},{2,3},{3,2},{4,5},{5,4},{6,7},{7,6},{8,20},{9,21},{10,... | collective-permute-start | bytes 196616 | tf_op jit(solution)/shard_map/ppermute | solution.py:183
  5.5 0.8 %constant_dynamic-slice_fusion.1 = (bf16[32,512]{1,0:T(8,128)(2,1)S(1)}, bf16[32,512]{1,0:T(8,128)(2,1)S(1)}) fusion(bf16[64,512]{1,0:T(8,128)(2,1)} %param.10, s32[]{:T(128)S(6)} %select_n.82, s32[]{:T(128)S(6)} %select_n.83), kind=kLoop, calls=%fused_computation.50 | loop fusion | bytes 131080 | tf_op jit(solution)/shard_map/dynamic_slice | solution.py:185
  6.3 1.0 %collective-permute-start.1 = (bf16[32,512]{1,0:T(8,128)(2,1)S(1)}, bf16[32,512]{1,0:T(8,128)(2,1)S(1)}, u32[]{:S(2)}, u32[]{:S(2)}) collective-permute-start(bf16[32,512]{1,0:T(8,128)(2,1)S(1)} %get-tuple-element.9), channel_id=1, source_target_pairs={{0,1},{1,0},{2,3},{3,2},{4,5},{5,4},{6,7},{7,6},{8,9},{9,8},{10,11... | collective-permute-start | bytes 98312 | tf_op jit(solution)/shard_map/ppermute | solution.py:188
  7.3 2.2 %collective-permute-start.2 = (bf16[32,512]{1,0:T(8,128)(2,1)S(1)}, bf16[32,512]{1,0:T(8,128)(2,1)S(1)}, u32[]{:S(2)}, u32[]{:S(2)}) collective-permute-start(bf16[32,512]{1,0:T(8,128)(2,1)S(1)} %get-tuple-element.10), channel_id=1, source_target_pairs={{0,0},{1,2},{2,1},{3,4},{4,3},{5,6},{6,5},{7,8},{8,7},{9,10},{10,9... | collective-permute-start | bytes 98312 | tf_op jit(solution)/shard_map/ppermute | solution.py:187
  9.5 0.8 %copy.14 = s32[64,27]{1,0:T(8,128)S(1)} copy(s32[64,27]{0,1:T(8,128)} %param.11) | data formatting | bytes 13824 | tf_op args[1]
  10.3 0.7 %constant_dynamic-slice_fusion.2 = (s32[128,20]{0,1:T(8,128)S(1)}, s32[128,20]{0,1:T(8,128)S(1)}) fusion(s32[1024,20]{0,1:T(8,128)} %param.13, s32[]{:T(128)S(6)} %select_n.71, s32[1024,20]{0,1:T(8,128)} %param.12), kind=kLoop, calls=%fused_computation.51 | loop fusion | bytes 40964 | tf_op jit(solution)/shard_map/dynamic_slice | solution.py:194
  11.0 0.1 copy.15
  11.1 0.2 fusion.9.index_ref
  11.3 1.1 %fusion.20 = (f32[8,2048]{1,0:T(8,128)S(1)}, f32[8,2048]{1,0:T(8,128)S(1)}) fusion(f32[8,2048]{1,0:T(8,128)} %param.17), kind=kLoop, calls=%fused_computation.53 | loop fusion | bytes 196608 | tf_op jit(solution)/shard_map/sin | solution.py:190
  12.4 1.0 %copy.18 = bf16[316,2,128]{2,0,1:T(8,128)(2,1)S(1)} copy(f32[316,2,128]{2,1,0:T(2,128)} %param.18) | data formatting | bytes 485376 | tf_op args[8]
  13.5 0.1 copy.16.kind_ref
  13.6 0.0 collective-permute-done.1
  13.6 0.0 collective-permute-done.2
  13.6 0.0 collective-permute-done
  13.6 0.9 %fusion.3 = (bf16[128,512]{1,0:T(8,128)(2,1)S(1)}, bf16[128,512]{1,0:T(8,128)(2,1)S(1)}) fusion(bf16[64,512]{1,0:T(8,128)(2,1)} %param.10, bf16[32,512]{1,0:T(8,128)(2,1)S(1)} %collective-permute-done.2, bf16[32,512]{1,0:T(8,128)(2,1)S(1)} %collective-permute-done.1, bf16[64,512]{1,0:T(8,128)(2,1)S(1)} %collective-permute-done), kind=kLoop, calls=%fused_computation.7 | loop fusion | flops 589824 | bytes 458752 | tf_op jit(solution)/shard_map/concatenate | solution.py:229
  14.5 0.0 copy-start
  14.5 3.4 %copy-done = bf16[1024,4096]{1,0:T(8,128)(2,1)S(1)} copy-done((bf16[1024,4096]{1,0:T(8,128)(2,1)S(1)}, bf16[1024,4096]{1,0:T(8,128)(2,1)}, u32[]{:S(2)}) %copy-start) | copy-done | bytes 8388632
  17.8 0.0 copy-start.3
  17.8 1.2 %copy-done.3 = bf16[512,1024]{1,0:T(8,128)(2,1)S(1)} copy-done((bf16[512,1024]{1,0:T(8,128)(2,1)S(1)}, bf16[512,1024]{1,0:T(8,128)(2,1)}, u32[]{:S(2)}) %copy-start.3) | copy-done | bytes 1048600
  19.1 5.0 %shard_map.100 = bf16[16,32,128]{2,1,0:T(8,128)(2,1)} custom-call(bf16[128,512]{1,0:T(8,128)(2,1)S(1)} %get-tuple-element.8.cur_ref, bf16[512,1024]{1,0:T(8,128)(2,1)S(1)} %copy-done.3, f32[8,2048]{1,0:T(8,128)S(1)} %get-tuple-element.12.cos_ref, f32[8,2048]{1,0:T(8,128)S(1)} %get-tuple-element.11.sin_ref, bf16[1024,4096]{1,0:T(8,128)(2,1)S(1)} %copy-done), custom_call_target="tpu_custom_call" | custom-call | flops 1207959552 | bytes 10485760 | tf_op jit(solution)/shard_map/pallas_call | solution.py:20
  24.1 7.5 %all-to-all-start = ((bf16[16,32,128]{2,1,0:T(8,128)(2,1)}), bf16[16,32,128]{2,1,0:T(8,128)(2,1)S(1)}, u32[]{:S(2)}, u32[]{:S(2)}) async-start(bf16[16,32,128]{2,1,0:T(8,128)(2,1)} %shard_map.100), calls=%async_computation | async-start | bytes 262144 | tf_op jit(solution)/shard_map/all_to_all | solution.py:227
  31.6 0.9 %shard_map.101.operator_ref = bf16[20,128,256]{2,1,0:T(8,128)(2,1)S(1)} custom-call(s32[128,20]{1,0:T(8,128)S(1)} %copy.16.kind_ref, bf16[384,256]{1,0:T(8,128)(2,1)S(1)} %fusion.2.table_ref), custom_call_target="tpu_custom_call" | custom-call | flops 503316480 | bytes 4194304 | tf_op jit(solution)/shard_map/pallas_call | solution.py:20
  32.5 0.0 copy-start.4
  32.5 4.3 %all-to-all-done.upper_ref = bf16[16,32,128]{2,1,0:T(8,128)(2,1)S(1)} async-done(((bf16[16,32,128]{2,1,0:T(8,128)(2,1)}), bf16[16,32,128]{2,1,0:T(8,128)(2,1)S(1)}, u32[]{:S(2)}, u32[]{:S(2)}) %all-to-all-start) | async-done | bytes 131104 | tf_op jit(solution)/shard_map/all_to_all | solution.py:227
  36.9 1.4 %shard_map.102 = bf16[16,16,128]{2,1,0:T(8,128)(2,1)} custom-call(bf16[16,32,128]{2,1,0:T(8,128)(2,1)S(1)} %all-to-all-done.upper_ref, s32[128,20]{1,0:T(8,128)S(1)} %fusion.9.index_ref, bf16[20,128,256]{2,1,0:T(8,128)(2,1)S(1)} %shard_map.101.operator_ref), custom_call_target="tpu_custom_call" | custom-call | flops 335544320 | bytes 2097152 | tf_op jit(solution)/shard_map/pallas_call | solution.py:20
  38.3 4.9 %all-to-all-start.1 = ((bf16[16,16,128]{2,1,0:T(8,128)(2,1)}), bf16[16,16,128]{2,1,0:T(8,128)(2,1)S(1)}, u32[]{:S(2)}, u32[]{:S(2)}) async-start(bf16[16,16,128]{2,1,0:T(8,128)(2,1)} %shard_map.102), calls=%async_computation.1 | async-start | bytes 131072 | tf_op jit(solution)/shard_map/all_to_all | solution.py:255
  43.2 0.0 copy-start.2
  43.2 5.0 %copy-done.2 = bf16[27,512,512]{2,1,0:T(8,128)(2,1)S(1)} copy-done((bf16[27,512,512]{2,1,0:T(8,128)(2,1)S(1)}, bf16[27,512,512]{2,1,0:T(8,128)(2,1)}, u32[]{:S(2)}) %copy-start.2) | copy-done | bytes 14155800
  48.2 7.9 %shard_map.103.near_ref = f32[64,512]{1,0:T(8,128)S(1)} custom-call(bf16[128,512]{1,0:T(8,128)(2,1)S(1)} %get-tuple-element.7.cur_ref, s32[64,27]{1,0:T(8,128)S(1)} %fusion.18.col_ref, bf16[27,512,512]{2,1,0:T(8,128)(2,1)S(1)} %copy-done.2), custom_call_target="tpu_custom_call" | custom-call | flops 1132462080 | bytes 15728640 | tf_op jit(solution)/shard_map/pallas_call | solution.py:20
  56.1 0.0 all-to-all-done.1.inc_ref
  56.1 0.0 copy-done.4
  56.1 0.0 copy-start.1
  56.1 3.4 %copy-done.1 = bf16[1024,4096]{1,0:T(8,128)(2,1)S(1)} copy-done((bf16[1024,4096]{1,0:T(8,128)(2,1)S(1)}, bf16[1024,4096]{1,0:T(8,128)(2,1)}, u32[]{:S(2)}) %copy-start.1) | copy-done | bytes 8388632
  59.5 6.5 %shard_map.104 = f32[64,512]{1,0:T(8,128)} custom-call(bf16[16,16,128]{2,1,0:T(8,128)(2,1)S(1)} %all-to-all-done.1.inc_ref, f32[8,2048]{1,0:T(8,128)S(1)} %get-tuple-element.12.cos_ref, f32[8,2048]{1,0:T(8,128)S(1)} %get-tuple-element.11.sin_ref, bf16[1024,512]{1,0:T(8,128)(2,1)S(1)} %copy-done.4, f32[64,512]{1,0:T(8,128)S(1)} %shard_map.103.near_ref, ...), custom_call_target="tpu_custom_call" | custom-call | flops 805306368 | bytes 10485760 | tf_op jit(solution)/shard_map/pallas_call | solution.py:20
  (3 shorter events, 0.1 us)
Async XLA Ops:
  0.0 13.6 %collective-permute-start = (bf16[64,512]{1,0:T(8,128)(2,1)}, bf16[64,512]{1,0:T(8,128)(2,1)S(1)}, u32[]{:S(2)}, u32[]{:S(2)}) collective-permute-start(bf16[64,512]{1,0:T(8,128)(2,1)} %param.10), channel_id=1, source_target_pairs={{0,1},{1,0},{2,3},{3,2},{4,5},{5,4},{6,7},{7,6},{8,20},{9,21},{10,... | collective-permute-start | bytes 196616 | tf_op jit(solution)/shard_map/ppermute | solution.py:183
  6.3 7.3 %collective-permute-start.1 = (bf16[32,512]{1,0:T(8,128)(2,1)S(1)}, bf16[32,512]{1,0:T(8,128)(2,1)S(1)}, u32[]{:S(2)}, u32[]{:S(2)}) collective-permute-start(bf16[32,512]{1,0:T(8,128)(2,1)S(1)} %get-tuple-element.9), channel_id=1, source_target_pairs={{0,1},{1,0},{2,3},{3,2},{4,5},{5,4},{6,7},{7,6},{8,9},{9,8},{10,11... | collective-permute-start | bytes 98312 | tf_op jit(solution)/shard_map/ppermute | solution.py:188
  7.3 6.3 %collective-permute-start.2 = (bf16[32,512]{1,0:T(8,128)(2,1)S(1)}, bf16[32,512]{1,0:T(8,128)(2,1)S(1)}, u32[]{:S(2)}, u32[]{:S(2)}) collective-permute-start(bf16[32,512]{1,0:T(8,128)(2,1)S(1)} %get-tuple-element.10), channel_id=1, source_target_pairs={{0,0},{1,2},{2,1},{3,4},{4,3},{5,6},{6,5},{7,8},{8,7},{9,10},{10,9... | collective-permute-start | bytes 98312 | tf_op jit(solution)/shard_map/ppermute | solution.py:187
  14.5 3.4 %copy-start = (bf16[1024,4096]{1,0:T(8,128)(2,1)S(1)}, bf16[1024,4096]{1,0:T(8,128)(2,1)}, u32[]{:S(2)}) copy-start(bf16[1024,4096]{1,0:T(8,128)(2,1)} %interp.3) | copy-start | bytes 25165828
  17.8 1.2 %copy-start.3 = (bf16[512,1024]{1,0:T(8,128)(2,1)S(1)}, bf16[512,1024]{1,0:T(8,128)(2,1)}, u32[]{:S(2)}) copy-start(bf16[512,1024]{1,0:T(8,128)(2,1)} %agg_ref.1) | copy-start | bytes 3145732
  24.1 12.8 %all-to-all-start = ((bf16[16,32,128]{2,1,0:T(8,128)(2,1)}), bf16[16,32,128]{2,1,0:T(8,128)(2,1)S(1)}, u32[]{:S(2)}, u32[]{:S(2)}) async-start(bf16[16,32,128]{2,1,0:T(8,128)(2,1)} %shard_map.100), calls=%async_computation | async-start | bytes 262144 | tf_op jit(solution)/shard_map/all_to_all | solution.py:227
  32.5 23.6 %copy-start.4 = (bf16[1024,512]{1,0:T(8,128)(2,1)S(1)}, bf16[1024,512]{1,0:T(8,128)(2,1)}, u32[]{:S(2)}) copy-start(bf16[1024,512]{1,0:T(8,128)(2,1)} %receive_ref.1) | copy-start | bytes 3145732
  38.3 17.8 %all-to-all-start.1 = ((bf16[16,16,128]{2,1,0:T(8,128)(2,1)}), bf16[16,16,128]{2,1,0:T(8,128)(2,1)S(1)}, u32[]{:S(2)}, u32[]{:S(2)}) async-start(bf16[16,16,128]{2,1,0:T(8,128)(2,1)} %shard_map.102), calls=%async_computation.1 | async-start | bytes 131072 | tf_op jit(solution)/shard_map/all_to_all | solution.py:255
  43.2 5.0 %copy-start.2 = (bf16[27,512,512]{2,1,0:T(8,128)(2,1)S(1)}, bf16[27,512,512]{2,1,0:T(8,128)(2,1)}, u32[]{:S(2)}) copy-start(bf16[27,512,512]{2,1,0:T(8,128)(2,1)} %near_hbm.1) | copy-start | bytes 42467332
  56.1 3.4 %copy-start.1 = (bf16[1024,4096]{1,0:T(8,128)(2,1)S(1)}, bf16[1024,4096]{1,0:T(8,128)(2,1)}, u32[]{:S(2)}) copy-start(bf16[1024,4096]{1,0:T(8,128)(2,1)} %interp.3) | copy-start | bytes 25165828

commit v2 on v1

v2 whole, which is shorter than its diff:
```python
import functools

import jax
import jax.numpy as jnp
from jax import lax
from jax.experimental import pallas as pl
from jax.experimental.pallas import tpu as pltpu
from jax.sharding import PartitionSpec as P

BF16, F32, I32 = jnp.bfloat16, jnp.float32, jnp.int32
BOTH = ("box", "dir")
VMEM = pltpu.VMEM


def whole(space=VMEM):
    return pl.BlockSpec(memory_space=space)


def call(body, out, args, specs, scratch, mib, flops, moved):
    return pl.pallas_call(
        body,
        out_shape=out,
        in_specs=specs,
        out_specs=jax.tree.map(lambda _: whole(), out),
        scratch_shapes=scratch,
        compiler_params=pltpu.CompilerParams(vmem_limit_bytes=mib << 20),
        cost_estimate=pl.CostEstimate(flops=flops, bytes_accessed=moved, transcendentals=0),
    )(*args)


def dot(a, b, ca=1, cb=0):
    return lax.dot_general(a, b, (((ca,), (cb,)), ((), ())), preferred_element_type=F32)


def prepare_kernel(
    box_ref,
    far_hbm,
    kind_hbm,
    angle_ref,
    table_ref,
    near_list_ref,
    aggregate,
    interp,
    receive,
    operators,
    index_ref,
    column_ref,
    cosine_ref,
    sine_ref,
    aggregate_out,
    interp_out,
    receive_out,
    far_ref,
    kind_ref,
    table,
    sems,
):
    slots, parents = far_ref.shape
    box, me = box_ref[0], box_ref[1]
    mine = pl.ds(pl.multiple_of(box * parents, parents), parents)
    lists = [
        pltpu.make_async_copy(far_hbm.at[:, mine], far_ref, sems.at[0]),
        pltpu.make_async_copy(kind_hbm.at[:, mine], kind_ref, sems.at[1]),
    ]
    weights = [
        pltpu.make_async_copy(aggregate, aggregate_out, sems.at[2]),
        pltpu.make_async_copy(interp, interp_out, sems.at[3]),
        pltpu.make_async_copy(receive, receive_out, sems.at[4]),
    ]
    for copy in lists + weights:
        copy.start()
    cosine_ref[...] = jnp.cos(angle_ref[...])
    sine_ref[...] = jnp.sin(angle_ref[...])
    kinds = table_ref.shape[0] // 2
    table[...] = jnp.zeros_like(table)
    table[0:kinds, 0:128] = table_ref[pl.ds(0, kinds, stride=2), :].astype(BF16)
    table[0:kinds, 128:256] = table_ref[pl.ds(1, kinds, stride=2), :].astype(BF16)

    leaves = near_list_ref.shape[1]
    rel = near_list_ref[...] - me * leaves
    odd = me & 1
    below = jnp.where(odd == 0, 3 * leaves, leaves * 2)
    above = jnp.where(odd == 0, 0, leaves)
    column = jnp.where(rel < 0, rel + below, jnp.where(rel < leaves, rel, rel + above))
    column_ref[...] = jnp.pad(column, ((0, 32 - column.shape[0]), (0, 0))).T

    lists[0].wait()
    lists[1].wait()
    q = far_ref[...] - box * parents
    half = parents // 2
    g = jnp.where(q < 0, q + half, q - parents)
    own = ((q >> 3) << 4) + (q & 7)
    row = (((g >> 3) & 3) << 4) + 8 + (g & 7)
    low, high = row + ((1 - (g >> 5)) << 6), row + ((3 - (g >> 5)) << 6)
    index = jnp.where(q < 0, low, jnp.where(q < parents, own, high))
    index_ref[...] = jnp.pad(index, ((0, 32 - slots), (0, 0))).T
    kind = jnp.pad(kind_ref[...], ((0, 32 - slots), (0, 0))).T
    lane = lax.broadcasted_iota(I32, (parents, table.shape[0]), 1)
    for j in range(slots):
        hot = jnp.where(lane == kind[:, j : j + 1], 1.0, 0.0).astype(BF16)
        operators[j] = dot(hot, table[...]).astype(BF16)
    for copy in weights:
        copy.wait()


def up_kernel(own_ref, far_ref, agg_ref, cos_ref, sin_ref, interp, out_ref):
    width = 256
    directions = cos_ref.shape[1]
    leaves = own_ref.shape[0]
    rows = 2 * leaves
    parents = rows // 8
    r = lax.broadcasted_iota(I32, (rows, leaves), 0)
    c = lax.broadcasted_iota(I32, (rows, leaves), 1)
    leaf = 8 * (r % parents) + r // parents
    from_own = jnp.where(c == leaf, 1.0, 0.0).astype(BF16)
    from_far = jnp.where(c + leaves == leaf, 1.0, 0.0).astype(BF16)
    cur = (dot(from_own, own_ref[...]) + dot(from_far, far_ref[...])).astype(BF16)
    pattern = dot(cur, agg_ref[...]).astype(BF16)
    for j in range(directions // width):
        re = dot(pattern, interp[:, j * width : (j + 1) * width])
        im = dot(pattern, interp[:, directions + j * width : directions + (j + 1) * width])
        acc_re = jnp.zeros((parents, width), F32)
        acc_im = jnp.zeros((parents, width), F32)
        for k in range(8):
            cosine = cos_ref[pl.ds(k, 1), pl.ds(j * width, width)]
            sine = sin_ref[pl.ds(k, 1), pl.ds(j * width, width)]
            a, b = re[k * parents : (k + 1) * parents], im[k * parents : (k + 1) * parents]
            acc_re += a * cosine - b * sine
            acc_im += a * sine + b * cosine
        for h in range(width // 128):
            s = slice(h * 128, (h + 1) * 128)
            out_ref[j * (width // 128) + h, 0:parents, :] = acc_re[:, s].astype(BF16)
            out_ref[j * (width // 128) + h, parents : 2 * parents, :] = acc_im[:, s].astype(BF16)


def translate_kernel(upper_ref, index_ref, operator_ref, _, out_ref):
    sources = upper_ref.shape[0] * 16
    slots, rows = operator_ref.shape[:2]
    field = jnp.concatenate(
        [
            upper_ref[:, 0:16, :].reshape(sources, 128),
            upper_ref[:, 16:32, :].reshape(sources, 128),
        ],
        axis=1,
    )
    lane = lax.broadcasted_iota(I32, (rows, sources), 1)
    acc_re = jnp.zeros((rows, 128), F32)
    acc_im = jnp.zeros((rows, 128), F32)
    for j in range(slots):
        hot = jnp.where(lane == index_ref[:, j : j + 1], 1.0, 0.0).astype(BF16)
        x = dot(hot, field)
        op = operator_ref[j].astype(F32)
        xr, xi = x[:, :128], x[:, 128:]
        tr, ti = op[:, :128], op[:, 128:]
        acc_re += tr * xr - ti * xi
        acc_im += tr * xi + ti * xr
    blocks = out_ref.shape[0]
    out_ref[:, 0:8, :] = acc_re.reshape(blocks, 8, 128).astype(BF16)
    out_ref[:, 8:16, :] = acc_im.reshape(blocks, 8, 128).astype(BF16)


def down_kernel(inc_ref, cos_ref, sin_ref, receive_ref, near_ref, interp, out_ref, received):
    leaves = received.shape[0]
    half = received.shape[1] // 2
    for s in range(inc_ref.shape[0]):
        lanes = slice(s * 128, (s + 1) * 128)
        block = inc_ref[s].astype(F32)
        re, im = block[0:8][:, None, :], block[8:16][:, None, :]
        cosine, sine = cos_ref[:, lanes][None], sin_ref[:, lanes][None]
        received[:, s * 128 : (s + 1) * 128] = (
            (re * cosine + im * sine).reshape(leaves, 128).astype(BF16)
        )
        received[:, half + s * 128 : half + (s + 1) * 128] = (
            (im * cosine - re * sine).reshape(leaves, 128).astype(BF16)
        )
    back = dot(received[...], interp[...], 1, 1).astype(BF16)
    out_ref[...] = near_ref[...] + dot(back, receive_ref[...])


def near_kernel(own_ref, sibling_ref, cross_ref, col_ref, near_hbm, _, out_ref, buf, hot, sems):
    slots = near_hbm.shape[0]
    copies = []
    for n in range(slots):
        copies.append(pltpu.make_async_copy(near_hbm.at[n], buf.at[n], sems.at[n]))
        copies[n].start()
    rows = out_ref.shape[0]
    lane = lax.broadcasted_iota(I32, (rows, 3 * rows), 1)
    for n in range(slots):
        hot[n * rows : (n + 1) * rows] = jnp.where(
            lane == col_ref[:, n : n + 1], 1.0, 0.0
        ).astype(BF16)
    sources = jnp.concatenate([own_ref[...], sibling_ref[...], cross_ref[...]], axis=0)
    picked = dot(hot[...], sources).astype(BF16)
    total = jnp.zeros(out_ref.shape, F32)
    for n in range(slots):
        copies[n].wait()
        total += dot(picked[n * rows : (n + 1) * rows], buf[n])
    out_ref[...] = total


def halo_partner(i, boxes, dirs):
    b, d = divmod(i, dirs)
    quarter = dirs // 4
    z, r = divmod(d, quarter)
    other = b + 1 if z >= 2 else b - 1
    if other < 0 or other >= boxes:
        return i ^ 1
    return other * dirs + (3 - z) * quarter + r


def on_device(
    boxes,
    dirs,
    currents,
    near_list,
    far_list,
    far_kind,
    aggregate,
    interp,
    receive,
    shift_angle,
    translation,
    near_matrix,
):
    leaves, width = currents.shape
    n = boxes * dirs
    me = lax.axis_index(BOTH)
    box = lax.axis_index("box")
    parents = leaves // 8 * dirs
    slots, near_slots = far_list.shape[1], near_list.shape[1]

    far_half = lax.ppermute(currents, BOTH, [(i, halo_partner(i, boxes, dirs)) for i in range(n)])
    cross = [(i, min(max(i + (1 if i % 2 else -1), 0), n - 1)) for i in range(n)]
    from_cross = lax.ppermute(currents, BOTH, cross)
    from_sibling = lax.ppermute(currents, BOTH, [(i, i ^ 1) for i in range(n)])

    place = jnp.stack([box, me]).astype(I32)
    operators, index, column, cosine, sine, aggregate, interp, receive = call(
        prepare_kernel,
        (
            pltpu.VMEM((slots, parents, 256), BF16),
            pltpu.VMEM((parents, 32), I32),
            pltpu.VMEM((leaves, 32), I32),
            pltpu.VMEM(shift_angle.shape, F32),
            pltpu.VMEM(shift_angle.shape, F32),
            pltpu.VMEM(aggregate.shape, BF16),
            pltpu.VMEM(interp.shape, BF16),
            pltpu.VMEM(receive.shape, BF16),
        ),
        (
            place,
            far_list.T,
            far_kind.T,
            shift_angle,
            translation.reshape(-1, translation.shape[2]),
            near_list.T,
            aggregate,
            interp,
            receive,
        ),
        [whole(pltpu.SMEM)] + [whole(pltpu.HBM)] * 2 + [whole()] * 3 + [whole(pltpu.HBM)] * 3,
        [
            pltpu.VMEM((slots, parents), I32),
            pltpu.VMEM((slots, parents), I32),
            pltpu.VMEM((384, 256), BF16),
            pltpu.SemaphoreType.DMA((5,)),
        ],
        8,
        2 * slots * parents * 384 * 256,
        11 << 20,
    )

    up = call(
        up_kernel,
        jax.ShapeDtypeStruct((dirs, 4 * leaves // 8, 128), BF16),
        (currents, far_half, aggregate, cosine, sine, interp),
        [whole()] * 6,
        [],
        8,
        2 * 128 * 1024 * 4608,
        10 << 20,
    )
    upper = lax.all_to_all(up, "dir", split_axis=0, concat_axis=0, tiled=True)

    near = call(
        near_kernel,
        jax.ShapeDtypeStruct((leaves, width), F32),
        (currents, from_sibling, from_cross, column, near_matrix, up),
        [whole()] * 4 + [whole(pltpu.HBM), whole(pl.ANY)],
        [
            pltpu.VMEM(near_matrix.shape, BF16),
            pltpu.VMEM((near_slots * leaves, 3 * leaves), BF16),
            pltpu.SemaphoreType.DMA((near_slots,)),
        ],
        24,
        2 * leaves * 27 * 512 * 640,
        15 << 20,
    )

    local = call(
        translate_kernel,
        jax.ShapeDtypeStruct((dirs, 2 * leaves // 8, 128), BF16),
        (upper, index, operators, near),
        [whole()] * 3 + [whole(pl.ANY)],
        [],
        8,
        2 * slots * parents * 256 * 256,
        2 << 20,
    )
    incoming = lax.all_to_all(local, "dir", split_axis=0, concat_axis=0, tiled=True)

    return call(
        down_kernel,
        jax.ShapeDtypeStruct((leaves, width), F32),
        (incoming, cosine, sine, receive, near, interp),
        [whole()] * 6,
        [pltpu.VMEM((leaves, interp.shape[1]), BF16)],
        8,
        2 * 64 * 4096 * 1536,
        10 << 20,
    )


def solution(mesh):
    placed = (
        P(BOTH, None),
        P(BOTH, None),
        P(),
        P(),
        P(),
        P(),
        P(),
        P(),
        P(None, None, "dir"),
        P(),
    )
    body = functools.partial(on_device, mesh.shape["box"], mesh.shape["dir"])
    return jax.shard_map(
        body, mesh=mesh, in_specs=placed, out_specs=P(BOTH, None), check_vma=False
    )
```

time: 66.7 us -> 63.2 us (0.948)
  the two profiles are of different devices: /device:TPU:27 before, /device:TPU:21 now
where the time goes in v2:
time: 63.2 us; the launch traced here: 62.6 us
  local copies, waits for them, and re-layouts  21.8 us (34%)
  starting transfers between devices  14.8 us (23%)
  Pallas kernels  14.5 us (23%)
  blocking collectives  11.3 us (18%)
    unnamed x24, local copies, waits for them, and re-layouts  21.8 us
    pallas_call x5, Pallas kernels, call(): pl.pallas_call(body, out_shape=out, in_specs=specs, out_specs=jax.tree.ma...  14.5 us
    all_to_all x1, blocking collectives, on_device(): lax.all_to_all(local, 'dir', split_axis=0, concat_axis=0, tiled=True)  11.3 us
    all_to_all x1, starting transfers between devices, on_device(): upper = lax.all_to_all(up, 'dir', split_axis=0, concat_axis=0, tiled=True)  6.51 us
    ppermute x1, starting transfers between devices, on_device(): lax.ppermute(currents, BOTH, [(i, halo_partner(i, boxes, dirs)) for i in...  3.7 us
    ppermute x1, starting transfers between devices, on_device(): from_cross = lax.ppermute(currents, BOTH, cross)  3.6 us
  transfers between devices with their start and end apart: 4, of which 0 were waited for; matrix products, arithmetic and copies ran while one was open for 0% of the time, Pallas kernels for 16%

profile of v2, /device:TPU:21, one launch (start us, length us, event | category | flops | bytes accessed | tf_op | source)
XLA Modules:
  0.0 62.6 jit_solution(13955918035958603039)
XLA Ops:
  0.0 3.7 %collective-permute-start = (bf16[64,512]{1,0:T(8,128)(2,1)}, bf16[64,512]{1,0:T(8,128)(2,1)S(1)}, u32[]{:S(2)}, u32[]{:S(2)}) collective-permute-start(bf16[64,512]{1,0:T(8,128)(2,1)} %own_ref.3), channel_id=1, source_target_pairs={{0,1},{1,0},{2,3},{3,2},{4,5},{5,4},{6,7},{7,6},{8,20},{9,21},{10,... | collective-permute-start | bytes 196616 | tf_op jit(solution)/shard_map/ppermute | solution.py:232
  3.7 1.0 %collective-permute-start.1 = (bf16[64,512]{1,0:T(8,128)(2,1)}, bf16[64,512]{1,0:T(8,128)(2,1)S(1)}, u32[]{:S(2)}, u32[]{:S(2)}) collective-permute-start(bf16[64,512]{1,0:T(8,128)(2,1)} %own_ref.3), channel_id=1, source_target_pairs={{0,1},{1,0},{2,3},{3,2},{4,5},{5,4},{6,7},{7,6},{8,9},{9,8},{10,11... | collective-permute-start | bytes 196616 | tf_op jit(solution)/shard_map/ppermute | solution.py:235
  4.7 3.6 %collective-permute-start.2 = (bf16[64,512]{1,0:T(8,128)(2,1)}, bf16[64,512]{1,0:T(8,128)(2,1)S(1)}, u32[]{:S(2)}, u32[]{:S(2)}) collective-permute-start(bf16[64,512]{1,0:T(8,128)(2,1)} %own_ref.3), channel_id=1, source_target_pairs={{0,0},{1,2},{2,1},{3,4},{4,3},{5,6},{6,5},{7,8},{8,7},{9,10},{10,9... | collective-permute-start | bytes 196616 | tf_op jit(solution)/shard_map/ppermute | solution.py:234
  8.3 0.1 pad_add_fusion.box_ref
  8.4 0.0 copy-start.3
  8.4 3.4 %copy-done.3 = bf16[1024,4096]{1,0:T(8,128)(2,1)S(1)} copy-done((bf16[1024,4096]{1,0:T(8,128)(2,1)S(1)}, bf16[1024,4096]{1,0:T(8,128)(2,1)}, u32[]{:S(2)}) %copy-start.3) | copy-done | bytes 8388632
  11.7 0.0 copy-start.4
  11.7 1.2 %copy-done.4 = bf16[512,1024]{1,0:T(8,128)(2,1)S(1)} copy-done((bf16[512,1024]{1,0:T(8,128)(2,1)S(1)}, bf16[512,1024]{1,0:T(8,128)(2,1)}, u32[]{:S(2)}) %copy-start.4) | copy-done | bytes 1048600
  13.0 0.0 copy-start.5
  13.0 1.2 %copy-done.5 = bf16[1024,512]{1,0:T(8,128)(2,1)S(1)} copy-done((bf16[1024,512]{1,0:T(8,128)(2,1)S(1)}, bf16[1024,512]{1,0:T(8,128)(2,1)}, u32[]{:S(2)}) %copy-start.5) | copy-done | bytes 1048600
  14.2 0.0 copy-start.6
  14.2 1.0 %copy-done.6 = f32[316,2,128]{2,1,0:T(2,128)S(1)} copy-done((f32[316,2,128]{2,1,0:T(2,128)S(1)}, f32[316,2,128]{2,1,0:T(2,128)}, u32[]{:S(2)}) %copy-start.6) | copy-done | bytes 323608
  15.2 0.0 copy-start.8
  15.2 0.9 %copy-done.8 = s32[1024,20]{0,1:T(8,128)S(1)} copy-done((s32[1024,20]{0,1:T(8,128)S(1)}, s32[1024,20]{0,1:T(8,128)}, u32[]{:S(2)}) %copy-start.8) | copy-done | bytes 81944
  16.0 0.0 copy-start.9
  16.1 0.9 %copy-done.9 = s32[1024,20]{0,1:T(8,128)S(1)} copy-done((s32[1024,20]{0,1:T(8,128)S(1)}, s32[1024,20]{0,1:T(8,128)}, u32[]{:S(2)}) %copy-start.9) | copy-done | bytes 81944
  16.9 0.0 copy-start.10
  16.9 0.8 %copy-done.10 = f32[8,2048]{1,0:T(8,128)S(1)} copy-done((f32[8,2048]{1,0:T(8,128)S(1)}, f32[8,2048]{1,0:T(8,128)}, u32[]{:S(2)}) %copy-start.10) | copy-done | bytes 65560
  17.8 0.0 copy-start.11
  17.8 0.7 %copy-done.11 = s32[64,27]{0,1:T(8,128)S(1)} copy-done((s32[64,27]{0,1:T(8,128)S(1)}, s32[64,27]{0,1:T(8,128)}, u32[]{:S(2)}) %copy-start.11) | copy-done | bytes 6936
  18.5 0.0 copy-start.7
  18.5 2.7 %shard_map.100 = (bf16[20,128,256]{2,1,0:T(8,128)(2,1)S(1)}, s32[128,32]{1,0:T(8,128)S(1)}, s32[64,32]{1,0:T(8,128)S(1)}, f32[8,2048]{1,0:T(8,128)S(1)}, f32[8,2...) custom-call(s32[2]{0:T(128)S(1)} %pad_add_fusion.box_ref, ...), custom_call_target="tpu_custom_call" | custom-call | flops 503316480 | bytes 11534336 | tf_op jit(solution)/shard_map/pallas_call | solution.py:20
  21.3 0.0 collective-permute-done.far_ref
  21.3 0.0 copy-done.7
  21.3 2.6 %shard_map.101._ = bf16[16,32,128]{2,1,0:T(8,128)(2,1)} custom-call(bf16[64,512]{1,0:T(8,128)(2,1)S(1)} %copy-done.7, bf16[64,512]{1,0:T(8,128)(2,1)S(1)} %collective-permute-done.far_ref, bf16[512,1024]{1,0:T(8,128)(2,1)S(1)} %get-tuple-element.13.agg_ref, f32[8,2048]{1,0:T(8,128)S(1)} %get-tuple-element.14.cos_ref, ...), custom_call_target="tpu_custom_call" | custom-call | flops 1207959552 | bytes 10485760 | tf_op jit(solution)/shard_map/pallas_call | solution.py:20
  23.9 0.0 copy-start
  23.9 3.2 %copy-done = bf16[1024,4096]{1,0:T(8,128)(2,1)} copy-done((bf16[1024,4096]{1,0:T(8,128)(2,1)}, bf16[1024,4096]{1,0:T(8,128)(2,1)S(1)}, u32[]{:S(2)}) %copy-start) | copy-done | bytes 8388632
  27.1 6.5 %all-to-all-start = ((bf16[16,32,128]{2,1,0:T(8,128)(2,1)}), bf16[16,32,128]{2,1,0:T(8,128)(2,1)S(1)}, u32[]{:S(2)}, u32[]{:S(2)}) async-start(bf16[16,32,128]{2,1,0:T(8,128)(2,1)} %shard_map.101._), calls=%async_computation | async-start | bytes 262144 | tf_op jit(solution)/shard_map/all_to_all | solution.py:283
  33.6 0.0 collective-permute-done.1.sibling_ref
  33.6 0.0 collective-permute-done.2.cross_ref
  33.6 0.0 copy-start.2
  33.6 5.0 %copy-done.2 = bf16[27,512,512]{2,1,0:T(8,128)(2,1)S(1)} copy-done((bf16[27,512,512]{2,1,0:T(8,128)(2,1)S(1)}, bf16[27,512,512]{2,1,0:T(8,128)(2,1)}, u32[]{:S(2)}) %copy-start.2) | copy-done | bytes 14155800
  38.6 4.9 %shard_map.102._.near_ref = f32[64,512]{1,0:T(8,128)S(1)} custom-call(bf16[64,512]{1,0:T(8,128)(2,1)S(1)} %copy-done.7, bf16[64,512]{1,0:T(8,128)(2,1)S(1)} %collective-permute-done.1.sibling_ref, bf16[64,512]{1,0:T(8,128)(2,1)S(1)} %collective-permute-done.2.cross_ref, s32[64,32]{1,0:T(8,128)S(1)} %get-tuple-element.19.col_ref, ...), custom_call_target="tpu_custom_call" | custom-call | flops 1132462080 | bytes 15728640 | tf_op jit(solution)/shard_map/pallas_call | solution.py:20
  43.5 0.0 all-to-all-done.upper_ref
  43.5 0.8 %shard_map.103 = bf16[16,16,128]{2,1,0:T(8,128)(2,1)S(1)} custom-call(bf16[16,32,128]{2,1,0:T(8,128)(2,1)S(1)} %all-to-all-done.upper_ref, s32[128,32]{1,0:T(8,128)S(1)} %get-tuple-element.17.index_ref, bf16[20,128,256]{2,1,0:T(8,128)(2,1)S(1)} %get-tuple-element.18.operator_ref, f32[64,512]{1,0:T(8,128)S(1)} %shard_map.102._.near_ref), custom_call_target="tpu_custom_call" | custom-call | flops 335544320 | bytes 2097152 | tf_op jit(solution)/shard_map/pallas_call | solution.py:20
  44.3 11.3 %all_to_all.10.inc_ref = bf16[16,16,128]{2,1,0:T(8,128)(2,1)S(1)} all-to-all(bf16[16,16,128]{2,1,0:T(8,128)(2,1)S(1)} %shard_map.103), channel_id=1, replica_groups=mesh['box'=8,'dir'=16] {'dir'}, dimensions={0} | all-to-all | bytes 131072 | tf_op jit(solution)/shard_map/all_to_all | solution.py:310
  55.7 0.0 copy-start.1
  55.7 3.4 %copy-done.1 = bf16[1024,4096]{1,0:T(8,128)(2,1)S(1)} copy-done((bf16[1024,4096]{1,0:T(8,128)(2,1)S(1)}, bf16[1024,4096]{1,0:T(8,128)(2,1)}, u32[]{:S(2)}) %copy-start.1) | copy-done | bytes 8388632
  59.1 3.5 %shard_map.104 = f32[64,512]{1,0:T(8,128)} custom-call(bf16[16,16,128]{2,1,0:T(8,128)(2,1)S(1)} %all_to_all.10.inc_ref, f32[8,2048]{1,0:T(8,128)S(1)} %get-tuple-element.14.cos_ref, f32[8,2048]{1,0:T(8,128)S(1)} %get-tuple-element.15.sin_ref, bf16[1024,512]{1,0:T(8,128)(2,1)S(1)} %get-tuple-element.20.receive_ref, f32[64,512]{1,0:T(8,128)S(1)} %shard_map.102._.near_ref, ...), custom_call_target="tpu_custom_call" | custom-call | flops 805306368 | bytes 10485760 | tf_op jit(solution)/shard_map/pallas_call | solution.py:20
Async XLA Ops:
  0.0 21.3 %collective-permute-start = (bf16[64,512]{1,0:T(8,128)(2,1)}, bf16[64,512]{1,0:T(8,128)(2,1)S(1)}, u32[]{:S(2)}, u32[]{:S(2)}) collective-permute-start(bf16[64,512]{1,0:T(8,128)(2,1)} %own_ref.3), channel_id=1, source_target_pairs={{0,1},{1,0},{2,3},{3,2},{4,5},{5,4},{6,7},{7,6},{8,20},{9,21},{10,... | collective-permute-start | bytes 196616 | tf_op jit(solution)/shard_map/ppermute | solution.py:232
  3.7 29.9 %collective-permute-start.1 = (bf16[64,512]{1,0:T(8,128)(2,1)}, bf16[64,512]{1,0:T(8,128)(2,1)S(1)}, u32[]{:S(2)}, u32[]{:S(2)}) collective-permute-start(bf16[64,512]{1,0:T(8,128)(2,1)} %own_ref.3), channel_id=1, source_target_pairs={{0,1},{1,0},{2,3},{3,2},{4,5},{5,4},{6,7},{7,6},{8,9},{9,8},{10,11... | collective-permute-start | bytes 196616 | tf_op jit(solution)/shard_map/ppermute | solution.py:235
  4.7 28.9 %collective-permute-start.2 = (bf16[64,512]{1,0:T(8,128)(2,1)}, bf16[64,512]{1,0:T(8,128)(2,1)S(1)}, u32[]{:S(2)}, u32[]{:S(2)}) collective-permute-start(bf16[64,512]{1,0:T(8,128)(2,1)} %own_ref.3), channel_id=1, source_target_pairs={{0,0},{1,2},{2,1},{3,4},{4,3},{5,6},{6,5},{7,8},{8,7},{9,10},{10,9... | collective-permute-start | bytes 196616 | tf_op jit(solution)/shard_map/ppermute | solution.py:234
  8.4 3.4 %copy-start.3 = (bf16[1024,4096]{1,0:T(8,128)(2,1)S(1)}, bf16[1024,4096]{1,0:T(8,128)(2,1)}, u32[]{:S(2)}) copy-start(bf16[1024,4096]{1,0:T(8,128)(2,1)} %interp.1) | copy-start | bytes 25165828
  11.7 1.2 %copy-start.4 = (bf16[512,1024]{1,0:T(8,128)(2,1)S(1)}, bf16[512,1024]{1,0:T(8,128)(2,1)}, u32[]{:S(2)}) copy-start(bf16[512,1024]{1,0:T(8,128)(2,1)} %aggregate.1) | copy-start | bytes 3145732
  13.0 1.2 %copy-start.5 = (bf16[1024,512]{1,0:T(8,128)(2,1)S(1)}, bf16[1024,512]{1,0:T(8,128)(2,1)}, u32[]{:S(2)}) copy-start(bf16[1024,512]{1,0:T(8,128)(2,1)} %receive.1) | copy-start | bytes 3145732
  14.2 1.0 %copy-start.6 = (f32[316,2,128]{2,1,0:T(2,128)S(1)}, f32[316,2,128]{2,1,0:T(2,128)}, u32[]{:S(2)}) copy-start(f32[316,2,128]{2,1,0:T(2,128)} %param.18) | copy-start | bytes 970756
  15.2 0.9 %copy-start.8 = (s32[1024,20]{0,1:T(8,128)S(1)}, s32[1024,20]{0,1:T(8,128)}, u32[]{:S(2)}) copy-start(s32[1024,20]{0,1:T(8,128)} %param.12) | copy-start | bytes 245764
  16.0 0.9 %copy-start.9 = (s32[1024,20]{0,1:T(8,128)S(1)}, s32[1024,20]{0,1:T(8,128)}, u32[]{:S(2)}) copy-start(s32[1024,20]{0,1:T(8,128)} %param.13) | copy-start | bytes 245764
  16.9 0.8 %copy-start.10 = (f32[8,2048]{1,0:T(8,128)S(1)}, f32[8,2048]{1,0:T(8,128)}, u32[]{:S(2)}) copy-start(f32[8,2048]{1,0:T(8,128)} %angle_ref.1) | copy-start | bytes 196612
  17.8 0.7 %copy-start.11 = (s32[64,27]{0,1:T(8,128)S(1)}, s32[64,27]{0,1:T(8,128)}, u32[]{:S(2)}) copy-start(s32[64,27]{0,1:T(8,128)} %param.11) | copy-start | bytes 20740
  18.5 2.8 %copy-start.7 = (bf16[64,512]{1,0:T(8,128)(2,1)S(1)}, bf16[64,512]{1,0:T(8,128)(2,1)}, u32[]{:S(2)}) copy-start(bf16[64,512]{1,0:T(8,128)(2,1)} %own_ref.3) | copy-start | bytes 196612
  23.9 3.2 %copy-start = (bf16[1024,4096]{1,0:T(8,128)(2,1)}, bf16[1024,4096]{1,0:T(8,128)(2,1)S(1)}, u32[]{:S(2)}) copy-start(bf16[1024,4096]{1,0:T(8,128)(2,1)S(1)} %get-tuple-element.16.interp) | copy-start | bytes 25165828
  27.1 16.4 %all-to-all-start = ((bf16[16,32,128]{2,1,0:T(8,128)(2,1)}), bf16[16,32,128]{2,1,0:T(8,128)(2,1)S(1)}, u32[]{:S(2)}, u32[]{:S(2)}) async-start(bf16[16,32,128]{2,1,0:T(8,128)(2,1)} %shard_map.101._), calls=%async_computation | async-start | bytes 262144 | tf_op jit(solution)/shard_map/all_to_all | solution.py:283
  33.6 5.0 %copy-start.2 = (bf16[27,512,512]{2,1,0:T(8,128)(2,1)S(1)}, bf16[27,512,512]{2,1,0:T(8,128)(2,1)}, u32[]{:S(2)}) copy-start(bf16[27,512,512]{2,1,0:T(8,128)(2,1)} %near_hbm.1) | copy-start | bytes 42467332
  55.7 3.4 %copy-start.1 = (bf16[1024,4096]{1,0:T(8,128)(2,1)S(1)}, bf16[1024,4096]{1,0:T(8,128)(2,1)}, u32[]{:S(2)}) copy-start(bf16[1024,4096]{1,0:T(8,128)(2,1)} %copy-done) | copy-start | bytes 25165828

commit v3 on v2

--- a/solution.py
+++ b/solution.py
@@ -28,6 +28,14 @@
     )(*args)
 
 
+def in_hbm(*arrays):
+    return tuple(pltpu.with_memory_space_constraint(a, pltpu.HBM) for a in arrays)
+
+
+def in_vmem(array):
+    return pltpu.with_memory_space_constraint(array, VMEM)
+
+
 def dot(a, b, ca=1, cb=0):
     return lax.dot_general(a, b, (((ca,), (cb,)), ((), ())), preferred_element_type=F32)
 
@@ -36,9 +44,9 @@
     box_ref,
     far_hbm,
     kind_hbm,
-    angle_ref,
-    table_ref,
-    near_list_ref,
+    angle_hbm,
+    table_hbm,
+    near_list_hbm,
     aggregate,
     interp,
     receive,
@@ -52,6 +60,9 @@
     receive_out,
     far_ref,
     kind_ref,
+    angle_ref,
+    table_ref,
+    near_list_ref,
     table,
     sems,
 ):
@@ -62,17 +73,24 @@
         pltpu.make_async_copy(far_hbm.at[:, mine], far_ref, sems.at[0]),
         pltpu.make_async_copy(kind_hbm.at[:, mine], kind_ref, sems.at[1]),
     ]
+    lists += [
+        pltpu.make_async_copy(near_list_hbm, near_list_ref, sems.at[2]),
+        pltpu.make_async_copy(angle_hbm, angle_ref, sems.at[3]),
+        pltpu.make_async_copy(table_hbm, table_ref, sems.at[4]),
+    ]
     weights = [
-        pltpu.make_async_copy(aggregate, aggregate_out, sems.at[2]),
-        pltpu.make_async_copy(interp, interp_out, sems.at[3]),
-        pltpu.make_async_copy(receive, receive_out, sems.at[4]),
+        pltpu.make_async_copy(aggregate, aggregate_out, sems.at[5]),
+        pltpu.make_async_copy(interp, interp_out, sems.at[6]),
+        pltpu.make_async_copy(receive, receive_out, sems.at[7]),
     ]
     for copy in lists + weights:
         copy.start()
+    table[...] = jnp.zeros_like(table)
+    for copy in lists:
+        copy.wait()
     cosine_ref[...] = jnp.cos(angle_ref[...])
     sine_ref[...] = jnp.sin(angle_ref[...])
     kinds = table_ref.shape[0] // 2
-    table[...] = jnp.zeros_like(table)
     table[0:kinds, 0:128] = table_ref[pl.ds(0, kinds, stride=2), :].astype(BF16)
     table[0:kinds, 128:256] = table_ref[pl.ds(1, kinds, stride=2), :].astype(BF16)
 
@@ -84,8 +102,6 @@
     column = jnp.where(rel < 0, rel + below, jnp.where(rel < leaves, rel, rel + above))
     column_ref[...] = jnp.pad(column, ((0, 32 - column.shape[0]), (0, 0))).T
 
-    lists[0].wait()
-    lists[1].wait()
     q = far_ref[...] - box * parents
     half = parents // 2
     g = jnp.where(q < 0, q + half, q - parents)
@@ -159,7 +175,7 @@
     out_ref[:, 8:16, :] = acc_im.reshape(blocks, 8, 128).astype(BF16)
 
 
-def down_kernel(inc_ref, cos_ref, sin_ref, receive_ref, near_ref, interp, out_ref, received):
+def down_kernel(inc_ref, cos_ref, sin_ref, receive_ref, near_ref, turned, out_ref, received):
     leaves = received.shape[0]
     half = received.shape[1] // 2
     for s in range(inc_ref.shape[0]):
@@ -173,8 +189,19 @@
         received[:, half + s * 128 : half + (s + 1) * 128] = (
             (im * cosine - re * sine).reshape(leaves, 128).astype(BF16)
         )
-    back = dot(received[...], interp[...], 1, 1).astype(BF16)
+    back = dot(received[...], turned[...]).astype(BF16)
     out_ref[...] = near_ref[...] + dot(back, receive_ref[...])
+
+
+def turn_kernel(interp, _, out_ref, buf, sems):
+    chunks, rows = buf.shape[:2]
+    copies = []
+    for j in range(chunks):
+        copies.append(pltpu.make_async_copy(interp.at[pl.ds(j * rows, rows)], buf.at[j], sems.at[j]))
+        copies[j].start()
+    for j in range(chunks):
+        copies[j].wait()
+        out_ref[:, j * rows : (j + 1) * rows] = buf[j].T
 
 
 def near_kernel(own_ref, sibling_ref, cross_ref, col_ref, near_hbm, _, out_ref, buf, hot, sems):
@@ -235,7 +262,7 @@
     from_sibling = lax.ppermute(currents, BOTH, [(i, i ^ 1) for i in range(n)])
 
     place = jnp.stack([box, me]).astype(I32)
-    operators, index, column, cosine, sine, aggregate, interp, receive = call(
+    operators, index, column, cosine, sine, aggregate, held, receive = call(
         prepare_kernel,
         (
             pltpu.VMEM((slots, parents, 256), BF16),
@@ -249,21 +276,26 @@
         ),
         (
             place,
-            far_list.T,
-            far_kind.T,
-            shift_angle,
-            translation.reshape(-1, translation.shape[2]),
-            near_list.T,
-            aggregate,
-            interp,
-            receive,
+            *in_hbm(
+                far_list.T,
+                far_kind.T,
+                shift_angle,
+                translation.reshape(-1, translation.shape[2]),
+                near_list.T,
+                aggregate,
+                interp,
+                receive,
+            ),
         ),
-        [whole(pltpu.SMEM)] + [whole(pltpu.HBM)] * 2 + [whole()] * 3 + [whole(pltpu.HBM)] * 3,
+        [whole(pltpu.SMEM)] + [whole(pltpu.HBM)] * 8,
         [
             pltpu.VMEM((slots, parents), I32),
             pltpu.VMEM((slots, parents), I32),
+            pltpu.VMEM(shift_angle.shape, F32),
+            pltpu.VMEM((2 * translation.shape[0], translation.shape[2]), F32),
+            pltpu.VMEM((near_slots, leaves), I32),
             pltpu.VMEM((384, 256), BF16),
-            pltpu.SemaphoreType.DMA((5,)),
+            pltpu.SemaphoreType.DMA((8,)),
         ],
         8,
         2 * slots * parents * 384 * 256,
@@ -273,7 +305,7 @@
     up = call(
         up_kernel,
         jax.ShapeDtypeStruct((dirs, 4 * leaves // 8, 128), BF16),
-        (currents, far_half, aggregate, cosine, sine, interp),
+        (currents, far_half, aggregate, cosine, sine, in_vmem(held)),
         [whole()] * 6,
         [],
         8,
@@ -285,7 +317,7 @@
     near = call(
         near_kernel,
         jax.ShapeDtypeStruct((leaves, width), F32),
-        (currents, from_sibling, from_cross, column, near_matrix, up),
+        (currents, from_sibling, from_cross, column, *in_hbm(near_matrix), up),
         [whole()] * 4 + [whole(pltpu.HBM), whole(pl.ANY)],
         [
             pltpu.VMEM(near_matrix.shape, BF16),
@@ -309,10 +341,24 @@
     )
     incoming = lax.all_to_all(local, "dir", split_axis=0, concat_axis=0, tiled=True)
 
+    turned = call(
+        turn_kernel,
+        pltpu.VMEM(interp.shape[::-1], BF16),
+        (*in_hbm(interp), local),
+        [whole(pltpu.HBM), whole(pl.ANY)],
+        [
+            pltpu.VMEM((8, interp.shape[0] // 8, interp.shape[1]), BF16),
+            pltpu.SemaphoreType.DMA((8,)),
+        ],
+        20,
+        2 * 64 * 4096 * 1024,
+        12 << 20,
+    )
+
     return call(
         down_kernel,
         jax.ShapeDtypeStruct((leaves, width), F32),
-        (incoming, cosine, sine, receive, near, interp),
+        (incoming, cosine, sine, receive, near, in_vmem(turned)),
         [whole()] * 6,
         [pltpu.VMEM((leaves, interp.shape[1]), BF16)],
         8,

time: 63.2 us -> 49.5 us (0.78)
  the two profiles are of different devices: /device:TPU:21 before, /device:TPU:23 now
where the time goes in v3:
time: 49.5 us; the launch traced here: 49.2 us
  Pallas kernels  21.4 us (43%)
  starting transfers between devices  20.9 us (42%)
  local copies, waits for them, and re-layouts  6.6 us (13%)
    pallas_call x6, Pallas kernels, call(): pl.pallas_call(body, out_shape=out, in_specs=specs, out_specs=jax.tree.ma...  21.4 us
    all_to_all x1, starting transfers between devices, on_device(): upper = lax.all_to_all(up, 'dir', split_axis=0, concat_axis=0, tiled=True)  7.75 us
    unnamed x6, local copies, waits for them, and re-layouts  6.6 us
    all_to_all x1, starting transfers between devices, on_device(): lax.all_to_all(local, 'dir', split_axis=0, concat_axis=0, tiled=True)  5.72 us
    ppermute x1, starting transfers between devices, on_device(): lax.ppermute(currents, BOTH, [(i, halo_partner(i, boxes, dirs)) for i in...  4.6 us
    ppermute x1, starting transfers between devices, on_device(): from_cross = lax.ppermute(currents, BOTH, cross)  1.91 us
  transfers between devices with their start and end apart: 5, of which 0 were waited for; matrix products, arithmetic and copies ran while one was open for 0% of the time, Pallas kernels for 36%

profile of v3, /device:TPU:23, one launch (start us, length us, event | category | flops | bytes accessed | tf_op | source)
XLA Modules:
  0.0 49.2 jit_solution(1109570993393355492)
XLA Ops:
  0.0 0.0 copy-start.2
  0.0 4.6 %collective-permute-start = (bf16[64,512]{1,0:T(8,128)(2,1)}, bf16[64,512]{1,0:T(8,128)(2,1)S(1)}, u32[]{:S(2)}, u32[]{:S(2)}) collective-permute-start(bf16[64,512]{1,0:T(8,128)(2,1)} %own_ref.3), channel_id=1, source_target_pairs={{0,1},{1,0},{2,3},{3,2},{4,5},{5,4},{6,7},{7,6},{8,20},{9,21},{10,... | collective-permute-start | bytes 196616 | tf_op jit(solution)/shard_map/ppermute | solution.py:259
  4.6 1.0 %collective-permute-start.1 = (bf16[64,512]{1,0:T(8,128)(2,1)}, bf16[64,512]{1,0:T(8,128)(2,1)S(1)}, u32[]{:S(2)}, u32[]{:S(2)}) collective-permute-start(bf16[64,512]{1,0:T(8,128)(2,1)} %own_ref.3), channel_id=1, source_target_pairs={{0,1},{1,0},{2,3},{3,2},{4,5},{5,4},{6,7},{7,6},{8,9},{9,8},{10,11... | collective-permute-start | bytes 196616 | tf_op jit(solution)/shard_map/ppermute | solution.py:262
  5.6 1.9 %collective-permute-start.2 = (bf16[64,512]{1,0:T(8,128)(2,1)}, bf16[64,512]{1,0:T(8,128)(2,1)S(1)}, u32[]{:S(2)}, u32[]{:S(2)}) collective-permute-start(bf16[64,512]{1,0:T(8,128)(2,1)} %own_ref.3), channel_id=1, source_target_pairs={{0,0},{1,2},{2,1},{3,4},{4,3},{5,6},{6,5},{7,8},{8,7},{9,10},{10,9... | collective-permute-start | bytes 196616 | tf_op jit(solution)/shard_map/ppermute | solution.py:261
  7.5 0.1 pad_add_fusion.box_ref
  7.6 4.8 %shard_map.100 = (bf16[20,128,256]{2,1,0:T(8,128)(2,1)S(1)}, s32[128,32]{1,0:T(8,128)S(1)}, s32[64,32]{1,0:T(8,128)S(1)}, f32[8,2048]{1,0:T(8,128)S(1)}, f32[8,2...) custom-call(s32[2]{0:T(128)S(1)} %pad_add_fusion.box_ref, ...), custom_call_target="tpu_custom_call" | custom-call | flops 503316480 | bytes 11534336 | tf_op jit(solution)/shard_map/pallas_call | solution.py:20
  12.4 0.0 collective-permute-done.far_ref
  12.4 0.0 copy-done.2
  12.4 2.6 %shard_map.101._ = bf16[16,32,128]{2,1,0:T(8,128)(2,1)} custom-call(bf16[64,512]{1,0:T(8,128)(2,1)S(1)} %copy-done.2, bf16[64,512]{1,0:T(8,128)(2,1)S(1)} %collective-permute-done.far_ref, bf16[512,1024]{1,0:T(8,128)(2,1)S(1)} %get-tuple-element.13.agg_ref, f32[8,2048]{1,0:T(8,128)S(1)} %get-tuple-element.14.cos_ref, ...), custom_call_target="tpu_custom_call" | custom-call | flops 1207959552 | bytes 10485760 | tf_op jit(solution)/shard_map/pallas_call | solution.py:20
  15.0 7.8 %all-to-all-start = ((bf16[16,32,128]{2,1,0:T(8,128)(2,1)}), bf16[16,32,128]{2,1,0:T(8,128)(2,1)S(1)}, u32[]{:S(2)}, u32[]{:S(2)}) async-start(bf16[16,32,128]{2,1,0:T(8,128)(2,1)} %shard_map.101._), calls=%async_computation | async-start | bytes 262144 | tf_op jit(solution)/shard_map/all_to_all | solution.py:315
  22.7 0.0 collective-permute-done.1.sibling_ref
  22.7 0.0 collective-permute-done.2.cross_ref
  22.7 5.9 %shard_map.102._.near_ref = f32[64,512]{1,0:T(8,128)S(1)} custom-call(bf16[64,512]{1,0:T(8,128)(2,1)S(1)} %copy-done.2, bf16[64,512]{1,0:T(8,128)(2,1)S(1)} %collective-permute-done.1.sibling_ref, bf16[64,512]{1,0:T(8,128)(2,1)S(1)} %collective-permute-done.2.cross_ref, s32[64,32]{1,0:T(8,128)S(1)} %get-tuple-element.19.col_ref, ...), custom_call_target="tpu_custom_call" | custom-call | flops 1132462080 | bytes 15728640 | tf_op jit(solution)/shard_map/pallas_call | solution.py:20
  28.6 0.0 all-to-all-done.upper_ref
  28.6 1.4 %shard_map.103._ = bf16[16,16,128]{2,1,0:T(8,128)(2,1)} custom-call(bf16[16,32,128]{2,1,0:T(8,128)(2,1)S(1)} %all-to-all-done.upper_ref, s32[128,32]{1,0:T(8,128)S(1)} %get-tuple-element.17.index_ref, bf16[20,128,256]{2,1,0:T(8,128)(2,1)S(1)} %get-tuple-element.18.operator_ref, f32[64,512]{1,0:T(8,128)S(1)} %shard_map.102._.near_ref), custom_call_target="tpu_custom_call" | custom-call | flops 335544320 | bytes 2097152 | tf_op jit(solution)/shard_map/pallas_call | solution.py:20
  30.1 5.7 %all-to-all-start.1 = ((bf16[16,16,128]{2,1,0:T(8,128)(2,1)}), bf16[16,16,128]{2,1,0:T(8,128)(2,1)S(1)}, u32[]{:S(2)}, u32[]{:S(2)}) async-start(bf16[16,16,128]{2,1,0:T(8,128)(2,1)} %shard_map.103._), calls=%async_computation.1 | async-start | bytes 131072 | tf_op jit(solution)/shard_map/all_to_all | solution.py:342
  35.8 4.3 %shard_map.104.turned = bf16[4096,1024]{1,0:T(8,128)(2,1)S(1)} custom-call(bf16[1024,4096]{1,0:T(8,128)(2,1)} %interp.3, bf16[16,16,128]{2,1,0:T(8,128)(2,1)} %shard_map.103._), custom_call_target="tpu_custom_call" | custom-call | flops 536870912 | bytes 12582912 | tf_op jit(solution)/shard_map/pallas_call | solution.py:20
  40.1 0.0 copy-start
  40.1 3.2 %copy-done = bf16[4096,1024]{1,0:T(8,128)(2,1)} copy-done((bf16[4096,1024]{1,0:T(8,128)(2,1)}, bf16[4096,1024]{1,0:T(8,128)(2,1)S(1)}, u32[]{:S(2)}) %copy-start) | copy-done | bytes 8388632
  43.3 0.0 all-to-all-done.1.inc_ref
  43.3 0.0 copy-start.1
  43.3 3.4 %copy-done.1 = bf16[4096,1024]{1,0:T(8,128)(2,1)S(1)} copy-done((bf16[4096,1024]{1,0:T(8,128)(2,1)S(1)}, bf16[4096,1024]{1,0:T(8,128)(2,1)}, u32[]{:S(2)}) %copy-start.1) | copy-done | bytes 8388632
  46.7 2.5 %shard_map.105 = f32[64,512]{1,0:T(8,128)} custom-call(bf16[16,16,128]{2,1,0:T(8,128)(2,1)S(1)} %all-to-all-done.1.inc_ref, f32[8,2048]{1,0:T(8,128)S(1)} %get-tuple-element.14.cos_ref, f32[8,2048]{1,0:T(8,128)S(1)} %get-tuple-element.15.sin_ref, bf16[1024,512]{1,0:T(8,128)(2,1)S(1)} %get-tuple-element.20.receive_ref, f32[64,512]{1,0:T(8,128)S(1)} %shard_map.102._.near_ref, ...), custom_call_target="tpu_custom_call" | custom-call | flops 805306368 | bytes 10485760 | tf_op jit(solution)/shard_map/pallas_call | solution.py:20
Async XLA Ops:
  0.0 12.4 %copy-start.2 = (bf16[64,512]{1,0:T(8,128)(2,1)S(1)}, bf16[64,512]{1,0:T(8,128)(2,1)}, u32[]{:S(2)}) copy-start(bf16[64,512]{1,0:T(8,128)(2,1)} %own_ref.3) | copy-start | bytes 196612
  0.0 12.4 %collective-permute-start = (bf16[64,512]{1,0:T(8,128)(2,1)}, bf16[64,512]{1,0:T(8,128)(2,1)S(1)}, u32[]{:S(2)}, u32[]{:S(2)}) collective-permute-start(bf16[64,512]{1,0:T(8,128)(2,1)} %own_ref.3), channel_id=1, source_target_pairs={{0,1},{1,0},{2,3},{3,2},{4,5},{5,4},{6,7},{7,6},{8,20},{9,21},{10,... | collective-permute-start | bytes 196616 | tf_op jit(solution)/shard_map/ppermute | solution.py:259
  4.6 18.1 %collective-permute-start.1 = (bf16[64,512]{1,0:T(8,128)(2,1)}, bf16[64,512]{1,0:T(8,128)(2,1)S(1)}, u32[]{:S(2)}, u32[]{:S(2)}) collective-permute-start(bf16[64,512]{1,0:T(8,128)(2,1)} %own_ref.3), channel_id=1, source_target_pairs={{0,1},{1,0},{2,3},{3,2},{4,5},{5,4},{6,7},{7,6},{8,9},{9,8},{10,11... | collective-permute-start | bytes 196616 | tf_op jit(solution)/shard_map/ppermute | solution.py:262
  5.6 17.2 %collective-permute-start.2 = (bf16[64,512]{1,0:T(8,128)(2,1)}, bf16[64,512]{1,0:T(8,128)(2,1)S(1)}, u32[]{:S(2)}, u32[]{:S(2)}) collective-permute-start(bf16[64,512]{1,0:T(8,128)(2,1)} %own_ref.3), channel_id=1, source_target_pairs={{0,0},{1,2},{2,1},{3,4},{4,3},{5,6},{6,5},{7,8},{8,7},{9,10},{10,9... | collective-permute-start | bytes 196616 | tf_op jit(solution)/shard_map/ppermute | solution.py:261
  15.0 13.6 %all-to-all-start = ((bf16[16,32,128]{2,1,0:T(8,128)(2,1)}), bf16[16,32,128]{2,1,0:T(8,128)(2,1)S(1)}, u32[]{:S(2)}, u32[]{:S(2)}) async-start(bf16[16,32,128]{2,1,0:T(8,128)(2,1)} %shard_map.101._), calls=%async_computation | async-start | bytes 262144 | tf_op jit(solution)/shard_map/all_to_all | solution.py:315
  30.1 13.2 %all-to-all-start.1 = ((bf16[16,16,128]{2,1,0:T(8,128)(2,1)}), bf16[16,16,128]{2,1,0:T(8,128)(2,1)S(1)}, u32[]{:S(2)}, u32[]{:S(2)}) async-start(bf16[16,16,128]{2,1,0:T(8,128)(2,1)} %shard_map.103._), calls=%async_computation.1 | async-start | bytes 131072 | tf_op jit(solution)/shard_map/all_to_all | solution.py:342
  40.1 3.2 %copy-start = (bf16[4096,1024]{1,0:T(8,128)(2,1)}, bf16[4096,1024]{1,0:T(8,128)(2,1)S(1)}, u32[]{:S(2)}) copy-start(bf16[4096,1024]{1,0:T(8,128)(2,1)S(1)} %shard_map.104.turned) | copy-start | bytes 25165828
  43.3 3.4 %copy-start.1 = (bf16[4096,1024]{1,0:T(8,128)(2,1)S(1)}, bf16[4096,1024]{1,0:T(8,128)(2,1)}, u32[]{:S(2)}) copy-start(bf16[4096,1024]{1,0:T(8,128)(2,1)} %copy-done) | copy-start | bytes 25165828

commit v4 on v2

--- a/solution.py
+++ b/solution.py
@@ -28,51 +28,67 @@
     )(*args)
 
 
+def in_hbm(*arrays):
+    return tuple(pltpu.with_memory_space_constraint(a, pltpu.HBM) for a in arrays)
+
+
+def in_vmem(array):
+    return pltpu.with_memory_space_constraint(array, VMEM)
+
+
 def dot(a, b, ca=1, cb=0):
     return lax.dot_general(a, b, (((ca,), (cb,)), ((), ())), preferred_element_type=F32)
 
 
 def prepare_kernel(
-    box_ref,
+    angle, aggregate, interp, cosine_ref, sine_ref, aggregate_out, interp_out, angle_ref, sems
+):
+    copies = [
+        pltpu.make_async_copy(angle, angle_ref, sems.at[2]),
+        pltpu.make_async_copy(aggregate, aggregate_out, sems.at[0]),
+        pltpu.make_async_copy(interp, interp_out, sems.at[1]),
+    ]
+    for copy in copies:
+        copy.start()
+    copies[0].wait()
+    cosine_ref[...] = jnp.cos(angle_ref[...])
+    sine_ref[...] = jnp.sin(angle_ref[...])
+    for copy in copies[1:]:
+        copy.wait()
+
+
+def tables_kernel(
+    place_ref,
     far_hbm,
     kind_hbm,
-    angle_ref,
-    table_ref,
-    near_list_ref,
-    aggregate,
-    interp,
-    receive,
+    table_hbm,
+    near_list_hbm,
+    _,
     operators,
     index_ref,
     column_ref,
-    cosine_ref,
-    sine_ref,
-    aggregate_out,
-    interp_out,
-    receive_out,
     far_ref,
     kind_ref,
+    table_ref,
+    near_list_ref,
     table,
     sems,
 ):
     slots, parents = far_ref.shape
-    box, me = box_ref[0], box_ref[1]
+    box, me = place_ref[0], place_ref[1]
     mine = pl.ds(pl.multiple_of(box * parents, parents), parents)
-    lists = [
-        pltpu.make_async_copy(far_hbm.at[:, mine], far_ref, sems.at[0]),
-        pltpu.make_async_copy(kind_hbm.at[:, mine], kind_ref, sems.at[1]),
+    copies = [
+        pltpu.make_async_copy(table_hbm, table_ref, sems.at[0]),
+        pltpu.make_async_copy(far_hbm.at[:, mine], far_ref, sems.at[1]),
+        pltpu.make_async_copy(kind_hbm.at[:, mine], kind_ref, sems.at[2]),
+        pltpu.make_async_copy(near_list_hbm, near_list_ref, sems.at[3]),
     ]
-    weights = [
-        pltpu.make_async_copy(aggregate, aggregate_out, sems.at[2]),
-        pltpu.make_async_copy(interp, interp_out, sems.at[3]),
-        pltpu.make_async_copy(receive, receive_out, sems.at[4]),
-    ]
-    for copy in lists + weights:
+    for copy in copies:
         copy.start()
-    cosine_ref[...] = jnp.cos(angle_ref[...])
-    sine_ref[...] = jnp.sin(angle_ref[...])
+    table[...] = jnp.zeros_like(table)
+    for copy in copies:
+        copy.wait()
     kinds = table_ref.shape[0] // 2
-    table[...] = jnp.zeros_like(table)
     table[0:kinds, 0:128] = table_ref[pl.ds(0, kinds, stride=2), :].astype(BF16)
     table[0:kinds, 128:256] = table_ref[pl.ds(1, kinds, stride=2), :].astype(BF16)
 
@@ -84,8 +100,6 @@
     column = jnp.where(rel < 0, rel + below, jnp.where(rel < leaves, rel, rel + above))
     column_ref[...] = jnp.pad(column, ((0, 32 - column.shape[0]), (0, 0))).T
 
-    lists[0].wait()
-    lists[1].wait()
     q = far_ref[...] - box * parents
     half = parents // 2
     g = jnp.where(q < 0, q + half, q - parents)
@@ -99,11 +113,10 @@
     for j in range(slots):
         hot = jnp.where(lane == kind[:, j : j + 1], 1.0, 0.0).astype(BF16)
         operators[j] = dot(hot, table[...]).astype(BF16)
-    for copy in weights:
-        copy.wait()
-
-
-def up_kernel(own_ref, far_ref, agg_ref, cos_ref, sin_ref, interp, out_ref):
+
+
+def up_kernel(own_ref, far_ref, agg_ref, cos_ref, sin_ref, interp, out_ref, relay_ref):
+    relay_ref[...] = own_ref[...]
     width = 256
     directions = cos_ref.shape[1]
     leaves = own_ref.shape[0]
@@ -133,7 +146,7 @@
             out_ref[j * (width // 128) + h, parents : 2 * parents, :] = acc_im[:, s].astype(BF16)
 
 
-def translate_kernel(upper_ref, index_ref, operator_ref, _, out_ref):
+def translate_kernel(upper_ref, index_ref, operator_ref, out_ref):
     sources = upper_ref.shape[0] * 16
     slots, rows = operator_ref.shape[:2]
     field = jnp.concatenate(
@@ -159,7 +172,16 @@
     out_ref[:, 8:16, :] = acc_im.reshape(blocks, 8, 128).astype(BF16)
 
 
-def down_kernel(inc_ref, cos_ref, sin_ref, receive_ref, near_ref, interp, out_ref, received):
+def down_kernel(inc_ref, cos_ref, sin_ref, near_ref, receive, interp, out_ref, buf, received, receive_ref, sems):
+    width = 256
+    chunks = buf.shape[1] // width
+    copies = []
+    for j in range(chunks):
+        lanes = pl.ds(j * width, width)
+        copies.append(pltpu.make_async_copy(interp.at[:, lanes], buf.at[:, lanes], sems.at[j]))
+    copies.append(pltpu.make_async_copy(receive, receive_ref, sems.at[chunks]))
+    for copy in copies:
+        copy.start()
     leaves = received.shape[0]
     half = received.shape[1] // 2
     for s in range(inc_ref.shape[0]):
@@ -173,8 +195,13 @@
         received[:, half + s * 128 : half + (s + 1) * 128] = (
             (im * cosine - re * sine).reshape(leaves, 128).astype(BF16)
         )
-    back = dot(received[...], interp[...], 1, 1).astype(BF16)
-    out_ref[...] = near_ref[...] + dot(back, receive_ref[...])
+    back = jnp.zeros((leaves, buf.shape[0]), F32)
+    for j in range(chunks):
+        lanes = slice(j * width, (j + 1) * width)
+        copies[j].wait()
+        back += dot(received[:, lanes], buf[:, lanes], 1, 1)
+    copies[chunks].wait()
+    out_ref[...] = near_ref[...] + dot(back.astype(BF16), receive_ref[...])
 
 
 def near_kernel(own_ref, sibling_ref, cross_ref, col_ref, near_hbm, _, out_ref, buf, hot, sems):
@@ -230,50 +257,31 @@
     slots, near_slots = far_list.shape[1], near_list.shape[1]
 
     far_half = lax.ppermute(currents, BOTH, [(i, halo_partner(i, boxes, dirs)) for i in range(n)])
-    cross = [(i, min(max(i + (1 if i % 2 else -1), 0), n - 1)) for i in range(n)]
-    from_cross = lax.ppermute(currents, BOTH, cross)
     from_sibling = lax.ppermute(currents, BOTH, [(i, i ^ 1) for i in range(n)])
 
-    place = jnp.stack([box, me]).astype(I32)
-    operators, index, column, cosine, sine, aggregate, interp, receive = call(
+    cosine, sine, held_aggregate, held = call(
         prepare_kernel,
         (
-            pltpu.VMEM((slots, parents, 256), BF16),
-            pltpu.VMEM((parents, 32), I32),
-            pltpu.VMEM((leaves, 32), I32),
             pltpu.VMEM(shift_angle.shape, F32),
             pltpu.VMEM(shift_angle.shape, F32),
             pltpu.VMEM(aggregate.shape, BF16),
             pltpu.VMEM(interp.shape, BF16),
-            pltpu.VMEM(receive.shape, BF16),
         ),
+        in_hbm(shift_angle, aggregate, interp),
+        [whole(pltpu.HBM)] * 3,
+        [pltpu.VMEM(shift_angle.shape, F32), pltpu.SemaphoreType.DMA((3,))],
+        8,
+        1 << 28,
+        9 << 20,
+    )
+
+    up, relay = call(
+        up_kernel,
         (
-            place,
-            far_list.T,
-            far_kind.T,
-            shift_angle,
-            translation.reshape(-1, translation.shape[2]),
-            near_list.T,
-            aggregate,
-            interp,
-            receive,
+            jax.ShapeDtypeStruct((dirs, 4 * leaves // 8, 128), BF16),
+            jax.ShapeDtypeStruct(currents.shape, BF16),
         ),
-        [whole(pltpu.SMEM)] + [whole(pltpu.HBM)] * 2 + [whole()] * 3 + [whole(pltpu.HBM)] * 3,
-        [
-            pltpu.VMEM((slots, parents), I32),
-            pltpu.VMEM((slots, parents), I32),
-            pltpu.VMEM((384, 256), BF16),
-            pltpu.SemaphoreType.DMA((5,)),
-        ],
-        8,
-        2 * slots * parents * 384 * 256,
-        11 << 20,
-    )
-
-    up = call(
-        up_kernel,
-        jax.ShapeDtypeStruct((dirs, 4 * leaves // 8, 128), BF16),
-        (currents, far_half, aggregate, cosine, sine, interp),
+        (currents, far_half, held_aggregate, cosine, sine, in_vmem(held)),
         [whole()] * 6,
         [],
         8,
@@ -282,10 +290,56 @@
     )
     upper = lax.all_to_all(up, "dir", split_axis=0, concat_axis=0, tiled=True)
 
+    cross = [(i, min(max(i + (1 if i % 2 else -1), 0), n - 1)) for i in range(n)]
+    from_cross = lax.ppermute(relay, BOTH, cross)
+    place = jnp.stack([box, me]).astype(I32)
+    operators, index, column = call(
+        tables_kernel,
+        (
+            pltpu.VMEM((slots, parents, 256), BF16),
+            pltpu.VMEM((parents, 32), I32),
+            pltpu.VMEM((leaves, 32), I32),
+        ),
+        (
+            place,
+            *in_hbm(
+                far_list.T,
+                far_kind.T,
+                translation.reshape(-1, translation.shape[2]),
+                near_list.T,
+            ),
+            relay,
+        ),
+        [whole(pltpu.SMEM)] + [whole(pltpu.HBM)] * 4 + [whole(pl.ANY)],
+        [
+            pltpu.VMEM((slots, parents), I32),
+            pltpu.VMEM((slots, parents), I32),
+            pltpu.VMEM((2 * translation.shape[0], translation.shape[2]), F32),
+            pltpu.VMEM((near_slots, leaves), I32),
+            pltpu.VMEM((384, 256), BF16),
+            pltpu.SemaphoreType.DMA((4,)),
+        ],
+        8,
+        2 * slots * parents * 384 * 256,
+        2 << 20,
+    )
+
+    local = call(
+        translate_kernel,
+        jax.ShapeDtypeStruct((dirs, 2 * leaves // 8, 128), BF16),
+        (upper, index, operators),
+        [whole()] * 3,
+        [],
+        8,
+        2 * slots * parents * 256 * 256,
+        2 << 20,
+    )
+    incoming = lax.all_to_all(local, "dir", split_axis=0, concat_axis=0, tiled=True)
+
     near = call(
         near_kernel,
         jax.ShapeDtypeStruct((leaves, width), F32),
-        (currents, from_sibling, from_cross, column, near_matrix, up),
+        (currents, from_sibling, from_cross, column, *in_hbm(near_matrix), local),
         [whole()] * 4 + [whole(pltpu.HBM), whole(pl.ANY)],
         [
             pltpu.VMEM(near_matrix.shape, BF16),
@@ -297,25 +351,18 @@
         15 << 20,
     )
 
-    local = call(
-        translate_kernel,
-        jax.ShapeDtypeStruct((dirs, 2 * leaves // 8, 128), BF16),
-        (upper, index, operators, near),
-        [whole()] * 3 + [whole(pl.ANY)],
-        [],
-        8,
-        2 * slots * parents * 256 * 256,
-        2 << 20,
-    )
-    incoming = lax.all_to_all(local, "dir", split_axis=0, concat_axis=0, tiled=True)
-
     return call(
         down_kernel,
         jax.ShapeDtypeStruct((leaves, width), F32),
-        (incoming, cosine, sine, receive, near, interp),
-        [whole()] * 6,
-        [pltpu.VMEM((leaves, interp.shape[1]), BF16)],
-        8,
+        (incoming, cosine, sine, near, *in_hbm(receive, interp)),
+        [whole()] * 4 + [whole(pltpu.HBM)] * 2,
+        [
+            pltpu.VMEM(interp.shape, BF16),
+            pltpu.VMEM((leaves, interp.shape[1]), BF16),
+            pltpu.VMEM(receive.shape, BF16),
+            pltpu.SemaphoreType.DMA((interp.shape[1] // 256 + 1,)),
+        ],
+        16,
         2 * 64 * 4096 * 1536,
         10 << 20,
     )

time: 63.2 us -> 44.7 us (0.71)
  the two profiles are of different devices: /device:TPU:21 before, /device:TPU:27 now
where the time goes in v4:
time: 44.7 us; the launch traced here: 44.4 us
  starting transfers between devices  22.8 us (51%)
  Pallas kernels  21.4 us (48%)
    pallas_call x6, Pallas kernels, call(): pl.pallas_call(body, out_shape=out, in_specs=specs, out_specs=jax.tree.ma...  21.4 us
    all_to_all x1, starting transfers between devices, on_device(): lax.all_to_all(local, 'dir', split_axis=0, concat_axis=0, tiled=True)  8.09 us
    ppermute x1, starting transfers between devices, on_device(): lax.ppermute(currents, BOTH, [(i, halo_partner(i, boxes, dirs)) for i in...  5.5 us
    all_to_all x1, starting transfers between devices, on_device(): upper = lax.all_to_all(up, 'dir', split_axis=0, concat_axis=0, tiled=True)  4.96 us
    ppermute x1, starting transfers between devices, on_device(): from_cross = lax.ppermute(relay, BOTH, cross)  3.33 us
    ppermute x1, starting transfers between devices, on_device(): from_sibling = lax.ppermute(currents, BOTH, [(i, i ^ 1) for i in range(n)])  0.96 us
  transfers between devices with their start and end apart: 5, of which 0 were waited for; matrix products, arithmetic and copies ran while one was open for 0% of the time, Pallas kernels for 36%

profile of v4, /device:TPU:27, one launch (start us, length us, event | category | flops | bytes accessed | tf_op | source)
XLA Modules:
  0.0 44.4 jit_solution(16110871888118460421)
XLA Ops:
  0.0 0.0 copy-start
  0.0 5.5 %collective-permute-start = (bf16[64,512]{1,0:T(8,128)(2,1)}, bf16[64,512]{1,0:T(8,128)(2,1)S(1)}, u32[]{:S(2)}, u32[]{:S(2)}) collective-permute-start(bf16[64,512]{1,0:T(8,128)(2,1)} %own_ref.3), channel_id=1, source_target_pairs={{0,1},{1,0},{2,3},{3,2},{4,5},{5,4},{6,7},{7,6},{8,20},{9,21},{10,... | collective-permute-start | bytes 196616 | tf_op jit(solution)/shard_map/ppermute | solution.py:259
  5.5 1.0 %collective-permute-start.1 = (bf16[64,512]{1,0:T(8,128)(2,1)}, bf16[64,512]{1,0:T(8,128)(2,1)S(1)}, u32[]{:S(2)}, u32[]{:S(2)}) collective-permute-start(bf16[64,512]{1,0:T(8,128)(2,1)} %own_ref.3), channel_id=1, source_target_pairs={{0,1},{1,0},{2,3},{3,2},{4,5},{5,4},{6,7},{7,6},{8,9},{9,8},{10,11... | collective-permute-start | bytes 196616 | tf_op jit(solution)/shard_map/ppermute | solution.py:260
  6.5 3.8 %shard_map.100 = (f32[8,2048]{1,0:T(8,128)S(1)}, f32[8,2048]{1,0:T(8,128)S(1)}, bf16[512,1024]{1,0:T(8,128)(2,1)S(1)}, bf16[1024,4096]{1,0:T(8,128)(2,1)S(1)}) custom-call(f32[8,2048]{1,0:T(8,128)} %angle.1, bf16[512,1024]{1,0:T(8,128)(2,1)} %aggregate.1, bf16[1024,4096]{1,0:T(8,128)(2,1)} %interp.3), custom_call_target="tpu_custom_call" | custom-call | flops 268435456 | bytes 9437184 | tf_op jit(solution)/shard_map/pallas_call | solution.py:20
  10.2 0.0 collective-permute-done.far_ref
  10.2 0.0 copy-done
  10.3 2.6 %shard_map.101 = (bf16[16,32,128]{2,1,0:T(8,128)(2,1)}, bf16[64,512]{1,0:T(8,128)(2,1)S(1)}) custom-call(bf16[64,512]{1,0:T(8,128)(2,1)S(1)} %copy-done, bf16[64,512]{1,0:T(8,128)(2,1)S(1)} %collective-permute-done.far_ref, bf16[512,1024]{1,0:T(8,128)(2,1)S(1)} %get-tuple-element.14.agg_ref, f32[8,2048]{1,0:T(8,128)S(1)} %get-tuple-element.15.cos_ref, ...), custom_call_target="tpu_custom_call" | custom-call | flops 1207959552 | bytes 10485760 | tf_op jit(solution)/shard_map/pallas_call | solution.py:20
  12.8 5.0 %all-to-all-start = ((bf16[16,32,128]{2,1,0:T(8,128)(2,1)}), bf16[16,32,128]{2,1,0:T(8,128)(2,1)S(1)}, u32[]{:S(2)}, u32[]{:S(2)}) async-start(bf16[16,32,128]{2,1,0:T(8,128)(2,1)} %get-tuple-element.18), calls=%async_computation | async-start | bytes 262144 | tf_op jit(solution)/shard_map/all_to_all | solution.py:291
  17.8 0.1 pad_add_fusion.place_ref
  17.9 3.3 %collective-permute-start.2 = (bf16[64,512]{1,0:T(8,128)(2,1)S(1)}, bf16[64,512]{1,0:T(8,128)(2,1)S(1)}, u32[]{:S(2)}, u32[]{:S(2)}) collective-permute-start(bf16[64,512]{1,0:T(8,128)(2,1)S(1)} %get-tuple-element.19._), channel_id=1, source_target_pairs={{0,0},{1,2},{2,1},{3,4},{4,3},{5,6},{6,5},{7,8},{8,7},{9,10},{10,9... | collective-permute-start | bytes 196616 | tf_op jit(solution)/shard_map/ppermute | solution.py:294
  21.2 2.6 %shard_map.102 = (bf16[20,128,256]{2,1,0:T(8,128)(2,1)S(1)}, s32[128,32]{1,0:T(8,128)S(1)}, s32[64,32]{1,0:T(8,128)S(1)}) custom-call(s32[2]{0:T(128)S(1)} %pad_add_fusion.place_ref, s32[20,1024]{1,0:T(8,128)} %bitcast.7, s32[20,1024]{1,0:T(8,128)} %bitcast.8, f32[632,128]{1,0:T(8,128)} %bitcast.6, s32[27,64]{1,0:T(8,128)} %bitcast.9, ...), custom_call_target="tpu_custom_call" | custom-call | flops 503316480 | bytes 2097152 | tf_op jit(solution)/shard_map/pallas_call | solution.py:20
  23.8 0.0 all-to-all-done.upper_ref
  23.8 1.4 %shard_map.103._ = bf16[16,16,128]{2,1,0:T(8,128)(2,1)} custom-call(bf16[16,32,128]{2,1,0:T(8,128)(2,1)S(1)} %all-to-all-done.upper_ref, s32[128,32]{1,0:T(8,128)S(1)} %get-tuple-element.20.index_ref, bf16[20,128,256]{2,1,0:T(8,128)(2,1)S(1)} %get-tuple-element.21.operator_ref), custom_call_target="tpu_custom_call" | custom-call | flops 335544320 | bytes 2097152 | tf_op jit(solution)/shard_map/pallas_call | solution.py:20
  25.2 8.1 %all-to-all-start.1 = ((bf16[16,16,128]{2,1,0:T(8,128)(2,1)}), bf16[16,16,128]{2,1,0:T(8,128)(2,1)S(1)}, u32[]{:S(2)}, u32[]{:S(2)}) async-start(bf16[16,16,128]{2,1,0:T(8,128)(2,1)} %shard_map.103._), calls=%async_computation.1 | async-start | bytes 131072 | tf_op jit(solution)/shard_map/all_to_all | solution.py:337
  33.3 0.0 collective-permute-done.1.sibling_ref
  33.3 0.0 collective-permute-done.2.cross_ref
  33.3 5.8 %shard_map.104.near_ref = f32[64,512]{1,0:T(8,128)S(1)} custom-call(bf16[64,512]{1,0:T(8,128)(2,1)S(1)} %copy-done, bf16[64,512]{1,0:T(8,128)(2,1)S(1)} %collective-permute-done.1.sibling_ref, bf16[64,512]{1,0:T(8,128)(2,1)S(1)} %collective-permute-done.2.cross_ref, s32[64,32]{1,0:T(8,128)S(1)} %get-tuple-element.22.col_ref, bf16[27,512,512]{2,1,0:T(8,128)(2,1)} %near_hbm.1, ...), custom_call_target="tpu_custom_call" | custom-call | flops 1132462080 | bytes 15728640 | tf_op jit(solution)/shard_map/pallas_call | solution.py:20
  39.2 0.0 all-to-all-done.1.inc_ref
  39.2 5.2 %shard_map.105 = f32[64,512]{1,0:T(8,128)} custom-call(bf16[16,16,128]{2,1,0:T(8,128)(2,1)S(1)} %all-to-all-done.1.inc_ref, f32[8,2048]{1,0:T(8,128)S(1)} %get-tuple-element.15.cos_ref, f32[8,2048]{1,0:T(8,128)S(1)} %get-tuple-element.16.sin_ref, f32[64,512]{1,0:T(8,128)S(1)} %shard_map.104.near_ref, bf16[1024,512]{1,0:T(8,128)(2,1)} %receive.1, ...), custom_call_target="tpu_custom_call" | custom-call | flops 805306368 | bytes 10485760 | tf_op jit(solution)/shard_map/pallas_call | solution.py:20
Async XLA Ops:
  0.0 10.2 %copy-start = (bf16[64,512]{1,0:T(8,128)(2,1)S(1)}, bf16[64,512]{1,0:T(8,128)(2,1)}, u32[]{:S(2)}) copy-start(bf16[64,512]{1,0:T(8,128)(2,1)} %own_ref.3) | copy-start | bytes 196612
  0.0 10.2 %collective-permute-start = (bf16[64,512]{1,0:T(8,128)(2,1)}, bf16[64,512]{1,0:T(8,128)(2,1)S(1)}, u32[]{:S(2)}, u32[]{:S(2)}) collective-permute-start(bf16[64,512]{1,0:T(8,128)(2,1)} %own_ref.3), channel_id=1, source_target_pairs={{0,1},{1,0},{2,3},{3,2},{4,5},{5,4},{6,7},{7,6},{8,20},{9,21},{10,... | collective-permute-start | bytes 196616 | tf_op jit(solution)/shard_map/ppermute | solution.py:259
  5.5 27.8 %collective-permute-start.1 = (bf16[64,512]{1,0:T(8,128)(2,1)}, bf16[64,512]{1,0:T(8,128)(2,1)S(1)}, u32[]{:S(2)}, u32[]{:S(2)}) collective-permute-start(bf16[64,512]{1,0:T(8,128)(2,1)} %own_ref.3), channel_id=1, source_target_pairs={{0,1},{1,0},{2,3},{3,2},{4,5},{5,4},{6,7},{7,6},{8,9},{9,8},{10,11... | collective-permute-start | bytes 196616 | tf_op jit(solution)/shard_map/ppermute | solution.py:260
  12.8 10.9 %all-to-all-start = ((bf16[16,32,128]{2,1,0:T(8,128)(2,1)}), bf16[16,32,128]{2,1,0:T(8,128)(2,1)S(1)}, u32[]{:S(2)}, u32[]{:S(2)}) async-start(bf16[16,32,128]{2,1,0:T(8,128)(2,1)} %get-tuple-element.18), calls=%async_computation | async-start | bytes 262144 | tf_op jit(solution)/shard_map/all_to_all | solution.py:291
  17.9 15.5 %collective-permute-start.2 = (bf16[64,512]{1,0:T(8,128)(2,1)S(1)}, bf16[64,512]{1,0:T(8,128)(2,1)S(1)}, u32[]{:S(2)}, u32[]{:S(2)}) collective-permute-start(bf16[64,512]{1,0:T(8,128)(2,1)S(1)} %get-tuple-element.19._), channel_id=1, source_target_pairs={{0,0},{1,2},{2,1},{3,4},{4,3},{5,6},{6,5},{7,8},{8,7},{9,10},{10,9... | collective-permute-start | bytes 196616 | tf_op jit(solution)/shard_map/ppermute | solution.py:294
  25.2 14.0 %all-to-all-start.1 = ((bf16[16,16,128]{2,1,0:T(8,128)(2,1)}), bf16[16,16,128]{2,1,0:T(8,128)(2,1)S(1)}, u32[]{:S(2)}, u32[]{:S(2)}) async-start(bf16[16,16,128]{2,1,0:T(8,128)(2,1)} %shard_map.103._), calls=%async_computation.1 | async-start | bytes 131072 | tf_op jit(solution)/shard_map/all_to_all | solution.py:337

commit v5 on v4

--- a/solution.py
+++ b/solution.py
@@ -41,34 +41,24 @@
 
 
 def prepare_kernel(
-    angle, aggregate, interp, cosine_ref, sine_ref, aggregate_out, interp_out, angle_ref, sems
-):
-    copies = [
-        pltpu.make_async_copy(angle, angle_ref, sems.at[2]),
-        pltpu.make_async_copy(aggregate, aggregate_out, sems.at[0]),
-        pltpu.make_async_copy(interp, interp_out, sems.at[1]),
-    ]
-    for copy in copies:
-        copy.start()
-    copies[0].wait()
-    cosine_ref[...] = jnp.cos(angle_ref[...])
-    sine_ref[...] = jnp.sin(angle_ref[...])
-    for copy in copies[1:]:
-        copy.wait()
-
-
-def tables_kernel(
     place_ref,
     far_hbm,
     kind_hbm,
+    angle_hbm,
     table_hbm,
     near_list_hbm,
-    _,
+    aggregate,
+    interp,
     operators,
     index_ref,
     column_ref,
+    cosine_ref,
+    sine_ref,
+    aggregate_out,
+    interp_out,
     far_ref,
     kind_ref,
+    angle_ref,
     table_ref,
     near_list_ref,
     table,
@@ -82,12 +72,19 @@
         pltpu.make_async_copy(far_hbm.at[:, mine], far_ref, sems.at[1]),
         pltpu.make_async_copy(kind_hbm.at[:, mine], kind_ref, sems.at[2]),
         pltpu.make_async_copy(near_list_hbm, near_list_ref, sems.at[3]),
+        pltpu.make_async_copy(angle_hbm, angle_ref, sems.at[4]),
     ]
-    for copy in copies:
+    weights = [
+        pltpu.make_async_copy(aggregate, aggregate_out, sems.at[5]),
+        pltpu.make_async_copy(interp, interp_out, sems.at[6]),
+    ]
+    for copy in copies + weights:
         copy.start()
     table[...] = jnp.zeros_like(table)
     for copy in copies:
         copy.wait()
+    cosine_ref[...] = jnp.cos(angle_ref[...])
+    sine_ref[...] = jnp.sin(angle_ref[...])
     kinds = table_ref.shape[0] // 2
     table[0:kinds, 0:128] = table_ref[pl.ds(0, kinds, stride=2), :].astype(BF16)
     table[0:kinds, 128:256] = table_ref[pl.ds(1, kinds, stride=2), :].astype(BF16)
@@ -104,8 +101,8 @@
     half = parents // 2
     g = jnp.where(q < 0, q + half, q - parents)
     own = ((q >> 3) << 4) + (q & 7)
-    row = (((g >> 3) & 3) << 4) + 8 + (g & 7)
-    low, high = row + ((1 - (g >> 5)) << 6), row + ((3 - (g >> 5)) << 6)
+    row = ((((g >> 3) & 3) ^ 2) << 4) + 8 + (g & 7)
+    low, high = row + ((2 + (g >> 5)) << 6), row + ((g >> 5) << 6)
     index = jnp.where(q < 0, low, jnp.where(q < parents, own, high))
     index_ref[...] = jnp.pad(index, ((0, 32 - slots), (0, 0))).T
     kind = jnp.pad(kind_ref[...], ((0, 32 - slots), (0, 0))).T
@@ -113,6 +110,8 @@
     for j in range(slots):
         hot = jnp.where(lane == kind[:, j : j + 1], 1.0, 0.0).astype(BF16)
         operators[j] = dot(hot, table[...]).astype(BF16)
+    for copy in weights:
+        copy.wait()
 
 
 def up_kernel(own_ref, far_ref, agg_ref, cos_ref, sin_ref, interp, out_ref, relay_ref):
@@ -225,14 +224,13 @@
     out_ref[...] = total
 
 
-def halo_partner(i, boxes, dirs):
+def halo_target(i, boxes, dirs):
     b, d = divmod(i, dirs)
-    quarter = dirs // 4
-    z, r = divmod(d, quarter)
+    z, r = divmod(d, dirs // 4)
     other = b + 1 if z >= 2 else b - 1
     if other < 0 or other >= boxes:
-        return i ^ 1
-    return other * dirs + (3 - z) * quarter + r
+        return b * dirs + (3 - z) * (dirs // 4) + r
+    return other * dirs + z * (dirs // 4) + (r ^ 2)
 
 
 def on_device(
@@ -256,23 +254,46 @@
     parents = leaves // 8 * dirs
     slots, near_slots = far_list.shape[1], near_list.shape[1]
 
-    far_half = lax.ppermute(currents, BOTH, [(i, halo_partner(i, boxes, dirs)) for i in range(n)])
+    far_half = lax.ppermute(currents, BOTH, [(i, halo_target(i, boxes, dirs)) for i in range(n)])
     from_sibling = lax.ppermute(currents, BOTH, [(i, i ^ 1) for i in range(n)])
 
-    cosine, sine, held_aggregate, held = call(
+    place = jnp.stack([box, me]).astype(I32)
+    operators, index, column, cosine, sine, held_aggregate, held = call(
         prepare_kernel,
         (
+            pltpu.VMEM((slots, parents, 256), BF16),
+            pltpu.VMEM((parents, 32), I32),
+            pltpu.VMEM((leaves, 32), I32),
             pltpu.VMEM(shift_angle.shape, F32),
             pltpu.VMEM(shift_angle.shape, F32),
             pltpu.VMEM(aggregate.shape, BF16),
             pltpu.VMEM(interp.shape, BF16),
         ),
-        in_hbm(shift_angle, aggregate, interp),
-        [whole(pltpu.HBM)] * 3,
-        [pltpu.VMEM(shift_angle.shape, F32), pltpu.SemaphoreType.DMA((3,))],
+        (
+            place,
+            *in_hbm(
+                far_list.T,
+                far_kind.T,
+                shift_angle,
+                translation.reshape(-1, translation.shape[2]),
+                near_list.T,
+                aggregate,
+                interp,
+            ),
+        ),
+        [whole(pltpu.SMEM)] + [whole(pltpu.HBM)] * 7,
+        [
+            pltpu.VMEM((slots, parents), I32),
+            pltpu.VMEM((slots, parents), I32),
+            pltpu.VMEM(shift_angle.shape, F32),
+            pltpu.VMEM((2 * translation.shape[0], translation.shape[2]), F32),
+            pltpu.VMEM((near_slots, leaves), I32),
+            pltpu.VMEM((384, 256), BF16),
+            pltpu.SemaphoreType.DMA((7,)),
+        ],
         8,
-        1 << 28,
-        9 << 20,
+        2 * slots * parents * 384 * 256,
+        11 << 20,
     )
 
     up, relay = call(
@@ -292,38 +313,6 @@
 
     cross = [(i, min(max(i + (1 if i % 2 else -1), 0), n - 1)) for i in range(n)]
     from_cross = lax.ppermute(relay, BOTH, cross)
-    place = jnp.stack([box, me]).astype(I32)
-    operators, index, column = call(
-        tables_kernel,
-        (
-            pltpu.VMEM((slots, parents, 256), BF16),
-            pltpu.VMEM((parents, 32), I32),
-            pltpu.VMEM((leaves, 32), I32),
-        ),
-        (
-            place,
-            *in_hbm(
-                far_list.T,
-                far_kind.T,
-                translation.reshape(-1, translation.shape[2]),
-                near_list.T,
-            ),
-            relay,
-        ),
-        [whole(pltpu.SMEM)] + [whole(pltpu.HBM)] * 4 + [whole(pl.ANY)],
-        [
-            pltpu.VMEM((slots, parents), I32),
-            pltpu.VMEM((slots, parents), I32),
-            pltpu.VMEM((2 * translation.shape[0], translation.shape[2]), F32),
-            pltpu.VMEM((near_slots, leaves), I32),
-            pltpu.VMEM((384, 256), BF16),
-            pltpu.SemaphoreType.DMA((4,)),
-        ],
-        8,
-        2 * slots * parents * 384 * 256,
-        2 << 20,
-    )
-
     local = call(
         translate_kernel,
         jax.ShapeDtypeStruct((dirs, 2 * leaves // 8, 128), BF16),

time: 44.7 us -> 39.7 us (0.89)
  starting transfers between devices: 22.8 us -> 17.5 us
  Pallas kernels: 21.4 us -> 19.6 us
  waiting for transfers between devices: 0.01 us -> 1.77 us
    ppermute x1, starting transfers between devices: 5.5 us -> 1.39 us  [on_device(): lax.ppermute(currents, BOTH, [(i, halo_target(i, boxes, dirs)) for i in r...]
    all_to_all x1, starting transfers between devices: 8.09 us -> 5.06 us  [on_device(): lax.all_to_all(local, 'dir', split_axis=0, concat_axis=0, tiled=True)]
    all_to_all x1, starting transfers between devices: 4.96 us -> 7.54 us  [on_device(): upper = lax.all_to_all(up, 'dir', split_axis=0, concat_axis=0, tiled=True)]
    pallas_call x6 -> x5, Pallas kernels: 21.4 us -> 19.6 us  [call(): pl.pallas_call(body, out_shape=out, in_specs=specs, out_specs=jax.tree.ma...]
    all_to_all x1, waiting for transfers between devices: 0.01 us -> 1.76 us  [on_device(): upper = lax.all_to_all(up, 'dir', split_axis=0, concat_axis=0, tiled=True)]
    ppermute x1, starting transfers between devices: 0.96 us -> 0.36 us  [on_device(): from_sibling = lax.ppermute(currents, BOTH, [(i, i ^ 1) for i in range(n)])]
  transfers between devices with their start and end apart: 5 -> 5, of which waited for: 0 -> 1; matrix products, arithmetic and copies ran while one was open for 0% -> 0% of each run, Pallas kernels for 36% -> 30%
where the time goes in v5:
time: 39.7 us; the launch traced here: 39 us
  Pallas kernels  19.6 us (49%)
  starting transfers between devices  17.5 us (44%)
  waiting for transfers between devices  1.77 us (4%)
    pallas_call x5, Pallas kernels, call(): pl.pallas_call(body, out_shape=out, in_specs=specs, out_specs=jax.tree.ma...  19.6 us
    all_to_all x1, starting transfers between devices, on_device(): upper = lax.all_to_all(up, 'dir', split_axis=0, concat_axis=0, tiled=True)  7.54 us
    all_to_all x1, starting transfers between devices, on_device(): lax.all_to_all(local, 'dir', split_axis=0, concat_axis=0, tiled=True)  5.06 us
    ppermute x1, starting transfers between devices, on_device(): from_cross = lax.ppermute(relay, BOTH, cross)  3.11 us
    all_to_all x1, waiting for transfers between devices, on_device(): upper = lax.all_to_all(up, 'dir', split_axis=0, concat_axis=0, tiled=True)  1.76 us
    ppermute x1, starting transfers between devices, on_device(): lax.ppermute(currents, BOTH, [(i, halo_target(i, boxes, dirs)) for i in r...  1.39 us
  transfers between devices with their start and end apart: 5, of which 1 were waited for; matrix products, arithmetic and copies ran while one was open for 0% of the time, Pallas kernels for 30%

profile of v5, /device:TPU:27, one launch (start us, length us, event | category | flops | bytes accessed | tf_op | source)
XLA Modules:
  0.0 39.0 jit_solution(1511704629185230083)
XLA Ops:
  0.0 0.0 copy-start
  0.0 1.4 %collective-permute-start = (bf16[64,512]{1,0:T(8,128)(2,1)}, bf16[64,512]{1,0:T(8,128)(2,1)S(1)}, u32[]{:S(2)}, u32[]{:S(2)}) collective-permute-start(bf16[64,512]{1,0:T(8,128)(2,1)} %own_ref.3), channel_id=1, source_target_pairs={{0,12},{1,13},{2,14},{3,15},{4,8},{5,9},{6,10},{7,11},{8,26},{9,27... | collective-permute-start | bytes 196616 | tf_op jit(solution)/shard_map/ppermute | solution.py:257
  1.4 0.1 pad_add_fusion.place_ref
  1.5 4.5 %shard_map.100 = (bf16[20,128,256]{2,1,0:T(8,128)(2,1)S(1)}, s32[128,32]{1,0:T(8,128)S(1)}, s32[64,32]{1,0:T(8,128)S(1)}, f32[8,2048]{1,0:T(8,128)S(1)}, f32[8,2...) custom-call(s32[2]{0:T(128)S(1)} %pad_add_fusion.place_ref, s32[20,1024]{1,0:T(8,128)} %bitcast.7, ...), custom_call_target="tpu_custom_call" | custom-call | flops 503316480 | bytes 11534336 | tf_op jit(solution)/shard_map/pallas_call | solution.py:20
  6.0 0.0 collective-permute-done.far_ref
  6.0 0.0 copy-done
  6.0 2.6 %shard_map.101 = (bf16[16,32,128]{2,1,0:T(8,128)(2,1)}, bf16[64,512]{1,0:T(8,128)(2,1)S(1)}) custom-call(bf16[64,512]{1,0:T(8,128)(2,1)S(1)} %copy-done, bf16[64,512]{1,0:T(8,128)(2,1)S(1)} %collective-permute-done.far_ref, bf16[512,1024]{1,0:T(8,128)(2,1)S(1)} %get-tuple-element.14.agg_ref, f32[8,2048]{1,0:T(8,128)S(1)} %get-tuple-element.15.cos_ref, ...), custom_call_target="tpu_custom_call" | custom-call | flops 1207959552 | bytes 10485760 | tf_op jit(solution)/shard_map/pallas_call | solution.py:20
  8.6 7.5 %all-to-all-start = ((bf16[16,32,128]{2,1,0:T(8,128)(2,1)}), bf16[16,32,128]{2,1,0:T(8,128)(2,1)S(1)}, u32[]{:S(2)}, u32[]{:S(2)}) async-start(bf16[16,32,128]{2,1,0:T(8,128)(2,1)} %get-tuple-element.18), calls=%async_computation | async-start | bytes 262144 | tf_op jit(solution)/shard_map/all_to_all | solution.py:312
  16.1 0.4 collective-permute-start.1
  16.5 3.1 %collective-permute-start.2 = (bf16[64,512]{1,0:T(8,128)(2,1)S(1)}, bf16[64,512]{1,0:T(8,128)(2,1)S(1)}, u32[]{:S(2)}, u32[]{:S(2)}) collective-permute-start(bf16[64,512]{1,0:T(8,128)(2,1)S(1)} %get-tuple-element.21), channel_id=1, source_target_pairs={{0,0},{1,2},{2,1},{3,4},{4,3},{5,6},{6,5},{7,8},{8,7},{9,10},{10,9... | collective-permute-start | bytes 196616 | tf_op jit(solution)/shard_map/ppermute | solution.py:315
  19.6 1.8 %all-to-all-done.upper_ref = bf16[16,32,128]{2,1,0:T(8,128)(2,1)S(1)} async-done(((bf16[16,32,128]{2,1,0:T(8,128)(2,1)}), bf16[16,32,128]{2,1,0:T(8,128)(2,1)S(1)}, u32[]{:S(2)}, u32[]{:S(2)}) %all-to-all-start) | async-done | bytes 131104 | tf_op jit(solution)/shard_map/all_to_all | solution.py:312
  21.4 1.4 %shard_map.102._ = bf16[16,16,128]{2,1,0:T(8,128)(2,1)} custom-call(bf16[16,32,128]{2,1,0:T(8,128)(2,1)S(1)} %all-to-all-done.upper_ref, s32[128,32]{1,0:T(8,128)S(1)} %get-tuple-element.19.index_ref, bf16[20,128,256]{2,1,0:T(8,128)(2,1)S(1)} %get-tuple-element.20.operator_ref), custom_call_target="tpu_custom_call" | custom-call | flops 335544320 | bytes 2097152 | tf_op jit(solution)/shard_map/pallas_call | solution.py:20
  22.8 5.1 %all-to-all-start.1 = ((bf16[16,16,128]{2,1,0:T(8,128)(2,1)}), bf16[16,16,128]{2,1,0:T(8,128)(2,1)S(1)}, u32[]{:S(2)}, u32[]{:S(2)}) async-start(bf16[16,16,128]{2,1,0:T(8,128)(2,1)} %shard_map.102._), calls=%async_computation.1 | async-start | bytes 131072 | tf_op jit(solution)/shard_map/all_to_all | solution.py:326
  27.9 0.0 collective-permute-done.1.sibling_ref
  27.9 0.0 collective-permute-done.2.cross_ref
  27.9 5.8 %shard_map.103.near_ref = f32[64,512]{1,0:T(8,128)S(1)} custom-call(bf16[64,512]{1,0:T(8,128)(2,1)S(1)} %copy-done, bf16[64,512]{1,0:T(8,128)(2,1)S(1)} %collective-permute-done.1.sibling_ref, bf16[64,512]{1,0:T(8,128)(2,1)S(1)} %collective-permute-done.2.cross_ref, s32[64,32]{1,0:T(8,128)S(1)} %get-tuple-element.22.col_ref, bf16[27,512,512]{2,1,0:T(8,128)(2,1)} %near_hbm.1, ...), custom_call_target="tpu_custom_call" | custom-call | flops 1132462080 | bytes 15728640 | tf_op jit(solution)/shard_map/pallas_call | solution.py:20
  33.8 0.0 all-to-all-done.1.inc_ref
  33.8 5.2 %shard_map.104 = f32[64,512]{1,0:T(8,128)} custom-call(bf16[16,16,128]{2,1,0:T(8,128)(2,1)S(1)} %all-to-all-done.1.inc_ref, f32[8,2048]{1,0:T(8,128)S(1)} %get-tuple-element.15.cos_ref, f32[8,2048]{1,0:T(8,128)S(1)} %get-tuple-element.16.sin_ref, f32[64,512]{1,0:T(8,128)S(1)} %shard_map.103.near_ref, bf16[1024,512]{1,0:T(8,128)(2,1)} %receive.1, ...), custom_call_target="tpu_custom_call" | custom-call | flops 805306368 | bytes 10485760 | tf_op jit(solution)/shard_map/pallas_call | solution.py:20
Async XLA Ops:
  0.0 6.0 %copy-start = (bf16[64,512]{1,0:T(8,128)(2,1)S(1)}, bf16[64,512]{1,0:T(8,128)(2,1)}, u32[]{:S(2)}) copy-start(bf16[64,512]{1,0:T(8,128)(2,1)} %own_ref.3) | copy-start | bytes 196612
  0.0 6.0 %collective-permute-start = (bf16[64,512]{1,0:T(8,128)(2,1)}, bf16[64,512]{1,0:T(8,128)(2,1)S(1)}, u32[]{:S(2)}, u32[]{:S(2)}) collective-permute-start(bf16[64,512]{1,0:T(8,128)(2,1)} %own_ref.3), channel_id=1, source_target_pairs={{0,12},{1,13},{2,14},{3,15},{4,8},{5,9},{6,10},{7,11},{8,26},{9,27... | collective-permute-start | bytes 196616 | tf_op jit(solution)/shard_map/ppermute | solution.py:257
  8.6 12.8 %all-to-all-start = ((bf16[16,32,128]{2,1,0:T(8,128)(2,1)}), bf16[16,32,128]{2,1,0:T(8,128)(2,1)S(1)}, u32[]{:S(2)}, u32[]{:S(2)}) async-start(bf16[16,32,128]{2,1,0:T(8,128)(2,1)} %get-tuple-element.18), calls=%async_computation | async-start | bytes 262144 | tf_op jit(solution)/shard_map/all_to_all | solution.py:312
  16.1 11.8 %collective-permute-start.1 = (bf16[64,512]{1,0:T(8,128)(2,1)S(1)}, bf16[64,512]{1,0:T(8,128)(2,1)S(1)}, u32[]{:S(2)}, u32[]{:S(2)}) collective-permute-start(bf16[64,512]{1,0:T(8,128)(2,1)S(1)} %copy-done), channel_id=1, source_target_pairs={{0,1},{1,0},{2,3},{3,2},{4,5},{5,4},{6,7},{7,6},{8,9},{9,8},{10,11... | collective-permute-start | bytes 196616 | tf_op jit(solution)/shard_map/ppermute | solution.py:258
  16.5 11.4 %collective-permute-start.2 = (bf16[64,512]{1,0:T(8,128)(2,1)S(1)}, bf16[64,512]{1,0:T(8,128)(2,1)S(1)}, u32[]{:S(2)}, u32[]{:S(2)}) collective-permute-start(bf16[64,512]{1,0:T(8,128)(2,1)S(1)} %get-tuple-element.21), channel_id=1, source_target_pairs={{0,0},{1,2},{2,1},{3,4},{4,3},{5,6},{6,5},{7,8},{8,7},{9,10},{10,9... | collective-permute-start | bytes 196616 | tf_op jit(solution)/shard_map/ppermute | solution.py:315
  22.8 10.9 %all-to-all-start.1 = ((bf16[16,16,128]{2,1,0:T(8,128)(2,1)}), bf16[16,16,128]{2,1,0:T(8,128)(2,1)S(1)}, u32[]{:S(2)}, u32[]{:S(2)}) async-start(bf16[16,16,128]{2,1,0:T(8,128)(2,1)} %shard_map.102._), calls=%async_computation.1 | async-start | bytes 131072 | tf_op jit(solution)/shard_map/all_to_all | solution.py:326

commit v6 on v5

--- a/solution.py
+++ b/solution.py
@@ -10,6 +10,9 @@
 BF16, F32, I32 = jnp.bfloat16, jnp.float32, jnp.int32
 BOTH = ("box", "dir")
 VMEM = pltpu.VMEM
+WIDTH = 256
+EARLY = 5
+KEPT = 3
 
 
 def whole(space=VMEM):
@@ -38,6 +41,18 @@
 
 def dot(a, b, ca=1, cb=0):
     return lax.dot_general(a, b, (((ca,), (cb,)), ((), ())), preferred_element_type=F32)
+
+
+def early_copies(interp, held, sems, at):
+    span, half = EARLY * WIDTH, interp.shape[1] // 2
+    return [
+        pltpu.make_async_copy(
+            interp.at[:, pl.ds(part * half, span)],
+            held.at[:, pl.ds(part * span, span)],
+            sems.at[at + part],
+        )
+        for part in range(2)
+    ]
 
 
 def prepare_kernel(
@@ -76,7 +91,7 @@
     ]
     weights = [
         pltpu.make_async_copy(aggregate, aggregate_out, sems.at[5]),
-        pltpu.make_async_copy(interp, interp_out, sems.at[6]),
+        *early_copies(interp, interp_out, sems, 6),
     ]
     for copy in copies + weights:
         copy.start()
@@ -114,9 +129,26 @@
         copy.wait()
 
 
-def up_kernel(own_ref, far_ref, agg_ref, cos_ref, sin_ref, interp, out_ref, relay_ref):
+def up_kernel(
+    own_ref, far_ref, agg_ref, cos_ref, sin_ref, held, interp, out_ref, relay_ref, late, sems
+):
+    rest = late.shape[1] // 2
+    copies = []
+    for j in range(rest // WIDTH):
+        for part in range(2):
+            copies.append(
+                pltpu.make_async_copy(
+                    interp.at[
+                        :, pl.ds(part * cos_ref.shape[1] + (EARLY + j) * WIDTH, WIDTH)
+                    ],
+                    late.at[:, pl.ds(part * rest + j * WIDTH, WIDTH)],
+                    sems.at[2 * j + part],
+                )
+            )
+    for copy in copies:
+        copy.start()
     relay_ref[...] = own_ref[...]
-    width = 256
+    width = WIDTH
     directions = cos_ref.shape[1]
     leaves = own_ref.shape[0]
     rows = 2 * leaves
@@ -129,8 +161,13 @@
     cur = (dot(from_own, own_ref[...]) + dot(from_far, far_ref[...])).astype(BF16)
     pattern = dot(cur, agg_ref[...]).astype(BF16)
     for j in range(directions // width):
-        re = dot(pattern, interp[:, j * width : (j + 1) * width])
-        im = dot(pattern, interp[:, directions + j * width : directions + (j + 1) * width])
+        source, at, step = held, j * width, EARLY * WIDTH
+        if j >= EARLY:
+            source, at, step = late, (j - EARLY) * width, rest
+            copies[2 * (j - EARLY)].wait()
+            copies[2 * (j - EARLY) + 1].wait()
+        re = dot(pattern, source[:, at : at + width])
+        im = dot(pattern, source[:, step + at : step + at + width])
         acc_re = jnp.zeros((parents, width), F32)
         acc_im = jnp.zeros((parents, width), F32)
         for k in range(8):
@@ -145,7 +182,11 @@
             out_ref[j * (width // 128) + h, parents : 2 * parents, :] = acc_im[:, s].astype(BF16)
 
 
-def translate_kernel(upper_ref, index_ref, operator_ref, out_ref):
+def translate_kernel(
+    upper_ref, index_ref, operator_ref, interp, out_ref, kept, sem
+):
+    copy = pltpu.make_async_copy(interp.at[:, pl.ds(0, KEPT * WIDTH)], kept, sem)
+    copy.start()
     sources = upper_ref.shape[0] * 16
     slots, rows = operator_ref.shape[:2]
     field = jnp.concatenate(
@@ -169,15 +210,34 @@
     blocks = out_ref.shape[0]
     out_ref[:, 0:8, :] = acc_re.reshape(blocks, 8, 128).astype(BF16)
     out_ref[:, 8:16, :] = acc_im.reshape(blocks, 8, 128).astype(BF16)
-
-
-def down_kernel(inc_ref, cos_ref, sin_ref, near_ref, receive, interp, out_ref, buf, received, receive_ref, sems):
-    width = 256
+    copy.wait()
+
+
+def down_kernel(
+    inc_ref,
+    cos_ref,
+    sin_ref,
+    near_ref,
+    kept,
+    receive,
+    interp,
+    out_ref,
+    buf,
+    received,
+    receive_ref,
+    sems,
+):
+    width = WIDTH
     chunks = buf.shape[1] // width
     copies = []
     for j in range(chunks):
-        lanes = pl.ds(j * width, width)
-        copies.append(pltpu.make_async_copy(interp.at[:, lanes], buf.at[:, lanes], sems.at[j]))
+        copies.append(
+            pltpu.make_async_copy(
+                interp.at[:, pl.ds((KEPT + j) * width, width)],
+                buf.at[:, pl.ds(j * width, width)],
+                sems.at[j],
+            )
+        )
     copies.append(pltpu.make_async_copy(receive, receive_ref, sems.at[chunks]))
     for copy in copies:
         copy.start()
@@ -194,11 +254,11 @@
         received[:, half + s * 128 : half + (s + 1) * 128] = (
             (im * cosine - re * sine).reshape(leaves, 128).astype(BF16)
         )
-    back = jnp.zeros((leaves, buf.shape[0]), F32)
+    back = dot(received[:, : KEPT * width], kept[...], 1, 1)
     for j in range(chunks):
-        lanes = slice(j * width, (j + 1) * width)
         copies[j].wait()
-        back += dot(received[:, lanes], buf[:, lanes], 1, 1)
+        at = (KEPT + j) * width
+        back += dot(received[:, at : at + width], buf[:, j * width : (j + 1) * width], 1, 1)
     copies[chunks].wait()
     out_ref[...] = near_ref[...] + dot(back.astype(BF16), receive_ref[...])
 
@@ -267,7 +327,7 @@
             pltpu.VMEM(shift_angle.shape, F32),
             pltpu.VMEM(shift_angle.shape, F32),
             pltpu.VMEM(aggregate.shape, BF16),
-            pltpu.VMEM(interp.shape, BF16),
+            pltpu.VMEM((interp.shape[0], 2 * EARLY * WIDTH), BF16),
         ),
         (
             place,
@@ -289,7 +349,7 @@
             pltpu.VMEM((2 * translation.shape[0], translation.shape[2]), F32),
             pltpu.VMEM((near_slots, leaves), I32),
             pltpu.VMEM((384, 256), BF16),
-            pltpu.SemaphoreType.DMA((7,)),
+            pltpu.SemaphoreType.DMA((8,)),
         ],
         8,
         2 * slots * parents * 384 * 256,
@@ -299,13 +359,16 @@
     up, relay = call(
         up_kernel,
         (
-            jax.ShapeDtypeStruct((dirs, 4 * leaves // 8, 128), BF16),
+            pltpu.VMEM((dirs, 4 * leaves // 8, 128), BF16),
             jax.ShapeDtypeStruct(currents.shape, BF16),
         ),
-        (currents, far_half, held_aggregate, cosine, sine, in_vmem(held)),
-        [whole()] * 6,
-        [],
-        8,
+        (currents, far_half, held_aggregate, cosine, sine, in_vmem(held), *in_hbm(interp)),
+        [whole()] * 6 + [whole(pltpu.HBM)],
+        [
+            pltpu.VMEM((interp.shape[0], interp.shape[1] - 2 * EARLY * WIDTH), BF16),
+            pltpu.SemaphoreType.DMA((16 - 2 * EARLY,)),
+        ],
+        12,
         2 * 128 * 1024 * 4608,
         10 << 20,
     )
@@ -313,12 +376,15 @@
 
     cross = [(i, min(max(i + (1 if i % 2 else -1), 0), n - 1)) for i in range(n)]
     from_cross = lax.ppermute(relay, BOTH, cross)
-    local = call(
+    local, kept = call(
         translate_kernel,
-        jax.ShapeDtypeStruct((dirs, 2 * leaves // 8, 128), BF16),
-        (upper, index, operators),
-        [whole()] * 3,
-        [],
+        (
+            pltpu.VMEM((dirs, 2 * leaves // 8, 128), BF16),
+            pltpu.VMEM((interp.shape[0], KEPT * WIDTH), BF16),
+        ),
+        (upper, index, operators, *in_hbm(interp)),
+        [whole()] * 3 + [whole(pltpu.HBM)],
+        [pltpu.SemaphoreType.DMA],
         8,
         2 * slots * parents * 256 * 256,
         2 << 20,
@@ -343,13 +409,13 @@
     return call(
         down_kernel,
         jax.ShapeDtypeStruct((leaves, width), F32),
-        (incoming, cosine, sine, near, *in_hbm(receive, interp)),
-        [whole()] * 4 + [whole(pltpu.HBM)] * 2,
+        (incoming, cosine, sine, near, in_vmem(kept), *in_hbm(receive, interp)),
+        [whole()] * 5 + [whole(pltpu.HBM)] * 2,
         [
-            pltpu.VMEM(interp.shape, BF16),
+            pltpu.VMEM((interp.shape[0], interp.shape[1] - KEPT * WIDTH), BF16),
             pltpu.VMEM((leaves, interp.shape[1]), BF16),
             pltpu.VMEM(receive.shape, BF16),
-            pltpu.SemaphoreType.DMA((interp.shape[1] // 256 + 1,)),
+            pltpu.SemaphoreType.DMA((interp.shape[1] // WIDTH - KEPT + 1,)),
         ],
         16,
         2 * 64 * 4096 * 1536,

time: 39.7 us -> 40.8 us (1.028)
  Pallas kernels: 19.6 us -> 20.3 us
  starting transfers between devices: 17.5 us -> 18.2 us
    pallas_call x5, Pallas kernels: 19.6 us -> 20.3 us  [call(): pl.pallas_call(body, out_shape=out, in_specs=specs, out_specs=jax.tree.ma...]
    all_to_all x1, starting transfers between devices: 5.06 us -> 5.71 us  [on_device(): lax.all_to_all(local, 'dir', split_axis=0, concat_axis=0, tiled=True)]
  transfers between devices with their start and end apart: 5 -> 5, of which waited for: 1 -> 1; matrix products, arithmetic and copies ran while one was open for 0% -> 0% of each run, Pallas kernels for 30% -> 29%
where the time goes in v6:
time: 40.8 us; the launch traced here: 40.4 us
  Pallas kernels  20.3 us (50%)
  starting transfers between devices  18.2 us (45%)
  waiting for transfers between devices  1.77 us (4%)
    pallas_call x5, Pallas kernels, call(): pl.pallas_call(body, out_shape=out, in_specs=specs, out_specs=jax.tree.ma...  20.3 us
    all_to_all x1, starting transfers between devices, on_device(): upper = lax.all_to_all(up, 'dir', split_axis=0, concat_axis=0, tiled=True)  7.58 us
    all_to_all x1, starting transfers between devices, on_device(): lax.all_to_all(local, 'dir', split_axis=0, concat_axis=0, tiled=True)  5.71 us
    ppermute x1, starting transfers between devices, on_device(): from_cross = lax.ppermute(relay, BOTH, cross)  3.11 us
    all_to_all x1, waiting for transfers between devices, on_device(): upper = lax.all_to_all(up, 'dir', split_axis=0, concat_axis=0, tiled=True)  1.76 us
    ppermute x1, starting transfers between devices, on_device(): lax.ppermute(currents, BOTH, [(i, halo_target(i, boxes, dirs)) for i in r...  1.39 us
  transfers between devices with their start and end apart: 5, of which 1 were waited for; matrix products, arithmetic and copies ran while one was open for 0% of the time, Pallas kernels for 29%

profile of v6, /device:TPU:27, one launch (start us, length us, event | category | flops | bytes accessed | tf_op | source)
XLA Modules:
  0.0 40.4 jit_solution(8933375814200997284)
XLA Ops:
  0.0 0.0 copy-start
  0.0 1.4 %collective-permute-start = (bf16[64,512]{1,0:T(8,128)(2,1)}, bf16[64,512]{1,0:T(8,128)(2,1)S(1)}, u32[]{:S(2)}, u32[]{:S(2)}) collective-permute-start(bf16[64,512]{1,0:T(8,128)(2,1)} %own_ref.3), channel_id=1, source_target_pairs={{0,12},{1,13},{2,14},{3,15},{4,8},{5,9},{6,10},{7,11},{8,26},{9,27... | collective-permute-start | bytes 196616 | tf_op jit(solution)/shard_map/ppermute | solution.py:317
  1.4 0.1 pad_add_fusion.place_ref
  1.5 3.7 %shard_map.100 = (bf16[20,128,256]{2,1,0:T(8,128)(2,1)S(1)}, s32[128,32]{1,0:T(8,128)S(1)}, s32[64,32]{1,0:T(8,128)S(1)}, f32[8,2048]{1,0:T(8,128)S(1)}, f32[8,2...) custom-call(s32[2]{0:T(128)S(1)} %pad_add_fusion.place_ref, s32[20,1024]{1,0:T(8,128)} %bitcast.7, ...), custom_call_target="tpu_custom_call" | custom-call | flops 503316480 | bytes 11534336 | tf_op jit(solution)/shard_map/pallas_call | solution.py:23
  5.2 0.0 collective-permute-done.far_ref
  5.2 0.0 copy-done
  5.2 3.8 %shard_map.101 = (bf16[16,32,128]{2,1,0:T(8,128)(2,1)}, bf16[64,512]{1,0:T(8,128)(2,1)S(1)}) custom-call(bf16[64,512]{1,0:T(8,128)(2,1)S(1)} %copy-done, bf16[64,512]{1,0:T(8,128)(2,1)S(1)} %collective-permute-done.far_ref, bf16[512,1024]{1,0:T(8,128)(2,1)S(1)} %get-tuple-element.16.agg_ref, f32[8,2048]{1,0:T(8,128)S(1)} %get-tuple-element.17.cos_ref, ...), custom_call_target="tpu_custom_call" | custom-call | flops 1207959552 | bytes 10485760 | tf_op jit(solution)/shard_map/pallas_call | solution.py:23
  9.0 7.6 %all-to-all-start = ((bf16[16,32,128]{2,1,0:T(8,128)(2,1)}), bf16[16,32,128]{2,1,0:T(8,128)(2,1)S(1)}, u32[]{:S(2)}, u32[]{:S(2)}) async-start(bf16[16,32,128]{2,1,0:T(8,128)(2,1)} %get-tuple-element.20), calls=%async_computation | async-start | bytes 262144 | tf_op jit(solution)/shard_map/all_to_all | solution.py:375
  16.6 0.4 collective-permute-start.1
  16.9 3.1 %collective-permute-start.2 = (bf16[64,512]{1,0:T(8,128)(2,1)S(1)}, bf16[64,512]{1,0:T(8,128)(2,1)S(1)}, u32[]{:S(2)}, u32[]{:S(2)}) collective-permute-start(bf16[64,512]{1,0:T(8,128)(2,1)S(1)} %get-tuple-element.24), channel_id=1, source_target_pairs={{0,0},{1,2},{2,1},{3,4},{4,3},{5,6},{6,5},{7,8},{8,7},{9,10},{10,9... | collective-permute-start | bytes 196616 | tf_op jit(solution)/shard_map/ppermute | solution.py:378
  20.1 1.8 %all-to-all-done.upper_ref = bf16[16,32,128]{2,1,0:T(8,128)(2,1)S(1)} async-done(((bf16[16,32,128]{2,1,0:T(8,128)(2,1)}), bf16[16,32,128]{2,1,0:T(8,128)(2,1)S(1)}, u32[]{:S(2)}, u32[]{:S(2)}) %all-to-all-start) | async-done | bytes 131104 | tf_op jit(solution)/shard_map/all_to_all | solution.py:375
  21.8 2.1 %shard_map.102 = (bf16[16,16,128]{2,1,0:T(8,128)(2,1)}, bf16[1024,768]{1,0:T(8,128)(2,1)S(1)}) custom-call(bf16[16,32,128]{2,1,0:T(8,128)(2,1)S(1)} %all-to-all-done.upper_ref, s32[128,32]{1,0:T(8,128)S(1)} %get-tuple-element.21.index_ref, bf16[20,128,256]{2,1,0:T(8,128)(2,1)S(1)} %get-tuple-element.22.operator_ref, bf16[1024,4096]{1,0:T(8,128)(2,1)} %interp.7), custom_call_target="tpu_custom_call" | custom-call | flops 335544320 | bytes 2097152 | tf_op jit(solution)/shard_map/pallas_call | solution.py:23
  23.9 5.7 %all-to-all-start.1 = ((bf16[16,16,128]{2,1,0:T(8,128)(2,1)}), bf16[16,16,128]{2,1,0:T(8,128)(2,1)S(1)}, u32[]{:S(2)}, u32[]{:S(2)}) async-start(bf16[16,16,128]{2,1,0:T(8,128)(2,1)} %get-tuple-element.23._), calls=%async_computation.1 | async-start | bytes 131072 | tf_op jit(solution)/shard_map/all_to_all | solution.py:392
  29.6 0.0 collective-permute-done.1.sibling_ref
  29.6 0.0 collective-permute-done.2.cross_ref
  29.6 5.9 %shard_map.103.near_ref = f32[64,512]{1,0:T(8,128)S(1)} custom-call(bf16[64,512]{1,0:T(8,128)(2,1)S(1)} %copy-done, bf16[64,512]{1,0:T(8,128)(2,1)S(1)} %collective-permute-done.1.sibling_ref, bf16[64,512]{1,0:T(8,128)(2,1)S(1)} %collective-permute-done.2.cross_ref, s32[64,32]{1,0:T(8,128)S(1)} %get-tuple-element.25.col_ref, bf16[27,512,512]{2,1,0:T(8,128)(2,1)} %near_hbm.1, ...), custom_call_target="tpu_custom_call" | custom-call | flops 1132462080 | bytes 15728640 | tf_op jit(solution)/shard_map/pallas_call | solution.py:23
  35.5 0.0 all-to-all-done.1.inc_ref
  35.5 4.9 %shard_map.104 = f32[64,512]{1,0:T(8,128)} custom-call(bf16[16,16,128]{2,1,0:T(8,128)(2,1)S(1)} %all-to-all-done.1.inc_ref, f32[8,2048]{1,0:T(8,128)S(1)} %get-tuple-element.17.cos_ref, f32[8,2048]{1,0:T(8,128)S(1)} %get-tuple-element.18.sin_ref, f32[64,512]{1,0:T(8,128)S(1)} %shard_map.103.near_ref, bf16[1024,768]{1,0:T(8,128)(2,1)S(1)} %get-tuple-element.26.kept, ...), custom_call_target="tpu_custom_call" | custom-call | flops 805306368 | bytes 10485760 | tf_op jit(solution)/shard_map/pallas_call | solution.py:23
Async XLA Ops:
  0.0 5.2 %copy-start = (bf16[64,512]{1,0:T(8,128)(2,1)S(1)}, bf16[64,512]{1,0:T(8,128)(2,1)}, u32[]{:S(2)}) copy-start(bf16[64,512]{1,0:T(8,128)(2,1)} %own_ref.3) | copy-start | bytes 196612
  0.0 5.2 %collective-permute-start = (bf16[64,512]{1,0:T(8,128)(2,1)}, bf16[64,512]{1,0:T(8,128)(2,1)S(1)}, u32[]{:S(2)}, u32[]{:S(2)}) collective-permute-start(bf16[64,512]{1,0:T(8,128)(2,1)} %own_ref.3), channel_id=1, source_target_pairs={{0,12},{1,13},{2,14},{3,15},{4,8},{5,9},{6,10},{7,11},{8,26},{9,27... | collective-permute-start | bytes 196616 | tf_op jit(solution)/shard_map/ppermute | solution.py:317
  9.0 12.8 %all-to-all-start = ((bf16[16,32,128]{2,1,0:T(8,128)(2,1)}), bf16[16,32,128]{2,1,0:T(8,128)(2,1)S(1)}, u32[]{:S(2)}, u32[]{:S(2)}) async-start(bf16[16,32,128]{2,1,0:T(8,128)(2,1)} %get-tuple-element.20), calls=%async_computation | async-start | bytes 262144 | tf_op jit(solution)/shard_map/all_to_all | solution.py:375
  16.6 13.0 %collective-permute-start.1 = (bf16[64,512]{1,0:T(8,128)(2,1)S(1)}, bf16[64,512]{1,0:T(8,128)(2,1)S(1)}, u32[]{:S(2)}, u32[]{:S(2)}) collective-permute-start(bf16[64,512]{1,0:T(8,128)(2,1)S(1)} %copy-done), channel_id=1, source_target_pairs={{0,1},{1,0},{2,3},{3,2},{4,5},{5,4},{6,7},{7,6},{8,9},{9,8},{10,11... | collective-permute-start | bytes 196616 | tf_op jit(solution)/shard_map/ppermute | solution.py:318
  16.9 12.7 %collective-permute-start.2 = (bf16[64,512]{1,0:T(8,128)(2,1)S(1)}, bf16[64,512]{1,0:T(8,128)(2,1)S(1)}, u32[]{:S(2)}, u32[]{:S(2)}) collective-permute-start(bf16[64,512]{1,0:T(8,128)(2,1)S(1)} %get-tuple-element.24), channel_id=1, source_target_pairs={{0,0},{1,2},{2,1},{3,4},{4,3},{5,6},{6,5},{7,8},{8,7},{9,10},{10,9... | collective-permute-start | bytes 196616 | tf_op jit(solution)/shard_map/ppermute | solution.py:378
  23.9 11.6 %all-to-all-start.1 = ((bf16[16,16,128]{2,1,0:T(8,128)(2,1)}), bf16[16,16,128]{2,1,0:T(8,128)(2,1)S(1)}, u32[]{:S(2)}, u32[]{:S(2)}) async-start(bf16[16,16,128]{2,1,0:T(8,128)(2,1)} %get-tuple-element.23._), calls=%async_computation.1 | async-start | bytes 131072 | tf_op jit(solution)/shard_map/all_to_all | solution.py:392

commit v7 on v5

--- a/solution.py
+++ b/solution.py
@@ -10,6 +10,7 @@
 BF16, F32, I32 = jnp.bfloat16, jnp.float32, jnp.int32
 BOTH = ("box", "dir")
 VMEM = pltpu.VMEM
+KEPT = 3
 
 
 def whole(space=VMEM):
@@ -171,14 +172,14 @@
     out_ref[:, 8:16, :] = acc_im.reshape(blocks, 8, 128).astype(BF16)
 
 
-def down_kernel(inc_ref, cos_ref, sin_ref, near_ref, receive, interp, out_ref, buf, received, receive_ref, sems):
+def down_kernel(inc_ref, cos_ref, sin_ref, near_ref, receive_ref, kept, interp, out_ref, buf, received, sems):
     width = 256
     chunks = buf.shape[1] // width
     copies = []
     for j in range(chunks):
-        lanes = pl.ds(j * width, width)
-        copies.append(pltpu.make_async_copy(interp.at[:, lanes], buf.at[:, lanes], sems.at[j]))
-    copies.append(pltpu.make_async_copy(receive, receive_ref, sems.at[chunks]))
+        source = interp.at[:, pl.ds((KEPT + j) * width, width)]
+        target = buf.at[:, pl.ds(j * width, width)]
+        copies.append(pltpu.make_async_copy(source, target, sems.at[j]))
     for copy in copies:
         copy.start()
     leaves = received.shape[0]
@@ -194,12 +195,11 @@
         received[:, half + s * 128 : half + (s + 1) * 128] = (
             (im * cosine - re * sine).reshape(leaves, 128).astype(BF16)
         )
-    back = jnp.zeros((leaves, buf.shape[0]), F32)
+    back = dot(received[:, : KEPT * width], kept[...], 1, 1)
     for j in range(chunks):
-        lanes = slice(j * width, (j + 1) * width)
+        at = (KEPT + j) * width
         copies[j].wait()
-        back += dot(received[:, lanes], buf[:, lanes], 1, 1)
-    copies[chunks].wait()
+        back += dot(received[:, at : at + width], buf[:, j * width : (j + 1) * width], 1, 1)
     out_ref[...] = near_ref[...] + dot(back.astype(BF16), receive_ref[...])
 
 
@@ -343,13 +343,12 @@
     return call(
         down_kernel,
         jax.ShapeDtypeStruct((leaves, width), F32),
-        (incoming, cosine, sine, near, *in_hbm(receive, interp)),
-        [whole()] * 4 + [whole(pltpu.HBM)] * 2,
+        (incoming, cosine, sine, near, in_vmem(receive), in_vmem(interp[:, : KEPT * 256]), *in_hbm(interp)),
+        [whole()] * 6 + [whole(pltpu.HBM)],
         [
-            pltpu.VMEM(interp.shape, BF16),
+            pltpu.VMEM((interp.shape[0], interp.shape[1] - KEPT * 256), BF16),
             pltpu.VMEM((leaves, interp.shape[1]), BF16),
-            pltpu.VMEM(receive.shape, BF16),
-            pltpu.SemaphoreType.DMA((interp.shape[1] // 256 + 1,)),
+            pltpu.SemaphoreType.DMA((interp.shape[1] // 256,)),
         ],
         16,
         2 * 64 * 4096 * 1536,

time: 39.7 us -> 40.6 us (1.023)
  starting transfers between devices: 17.5 us -> 19.1 us
  local copies, waits for them, and re-layouts: 0.01 us -> 1.52 us
  waiting for transfers between devices: 1.77 us -> 0.26 us
    all_to_all x1, starting transfers between devices: 5.06 us -> 6.71 us  [on_device(): lax.all_to_all(local, 'dir', split_axis=0, concat_axis=0, tiled=True)]
    all_to_all x1, waiting for transfers between devices: 1.76 us -> 0.25 us  [on_device(): upper = lax.all_to_all(up, 'dir', split_axis=0, concat_axis=0, tiled=True)]
    slice x0 -> x1, local copies, waits for them, and re-layouts: none -> 1.51 us  [on_device(): interp[:, :KEPT * 256]]
  transfers between devices with their start and end apart: 5 -> 5, of which waited for: 1 -> 1; matrix products, arithmetic and copies ran while one was open for 0% -> 4% of each run, Pallas kernels for 30% -> 29%
where the time goes in v7:
time: 40.6 us; the launch traced here: 40.3 us
  Pallas kernels  19.2 us (47%)
  starting transfers between devices  19.1 us (47%)
  local copies, waits for them, and re-layouts  1.52 us (4%)
    pallas_call x5, Pallas kernels, call(): pl.pallas_call(body, out_shape=out, in_specs=specs, out_specs=jax.tree.ma...  19.2 us
    all_to_all x1, starting transfers between devices, on_device(): upper = lax.all_to_all(up, 'dir', split_axis=0, concat_axis=0, tiled=True)  7.54 us
    all_to_all x1, starting transfers between devices, on_device(): lax.all_to_all(local, 'dir', split_axis=0, concat_axis=0, tiled=True)  6.71 us
    ppermute x1, starting transfers between devices, on_device(): from_cross = lax.ppermute(relay, BOTH, cross)  3.11 us
    slice x1, local copies, waits for them, and re-layouts, on_device(): interp[:, :KEPT * 256]  1.51 us
    ppermute x1, starting transfers between devices, on_device(): lax.ppermute(currents, BOTH, [(i, halo_target(i, boxes, dirs)) for i in r...  1.39 us
  transfers between devices with their start and end apart: 5, of which 1 were waited for; matrix products, arithmetic and copies ran while one was open for 4% of the time, Pallas kernels for 29%

profile of v7, /device:TPU:27, one launch (start us, length us, event | category | flops | bytes accessed | tf_op | source)
XLA Modules:
  0.0 40.3 jit_solution(16314966324237494751)
XLA Ops:
  0.0 0.0 copy-start.1
  0.0 1.4 %collective-permute-start = (bf16[64,512]{1,0:T(8,128)(2,1)}, bf16[64,512]{1,0:T(8,128)(2,1)S(1)}, u32[]{:S(2)}, u32[]{:S(2)}) collective-permute-start(bf16[64,512]{1,0:T(8,128)(2,1)} %own_ref.3), channel_id=1, source_target_pairs={{0,12},{1,13},{2,14},{3,15},{4,8},{5,9},{6,10},{7,11},{8,26},{9,27... | collective-permute-start | bytes 196616 | tf_op jit(solution)/shard_map/ppermute | solution.py:257
  1.4 0.1 pad_add_fusion.place_ref
  1.5 4.5 %shard_map.100 = (bf16[20,128,256]{2,1,0:T(8,128)(2,1)S(1)}, s32[128,32]{1,0:T(8,128)S(1)}, s32[64,32]{1,0:T(8,128)S(1)}, f32[8,2048]{1,0:T(8,128)S(1)}, f32[8,2...) custom-call(s32[2]{0:T(128)S(1)} %pad_add_fusion.place_ref, s32[20,1024]{1,0:T(8,128)} %bitcast.7, ...), custom_call_target="tpu_custom_call" | custom-call | flops 503316480 | bytes 11534336 | tf_op jit(solution)/shard_map/pallas_call | solution.py:21
  6.0 0.0 collective-permute-done.far_ref
  6.0 0.0 copy-done.1
  6.0 2.6 %shard_map.101 = (bf16[16,32,128]{2,1,0:T(8,128)(2,1)}, bf16[64,512]{1,0:T(8,128)(2,1)S(1)}) custom-call(bf16[64,512]{1,0:T(8,128)(2,1)S(1)} %copy-done.1, bf16[64,512]{1,0:T(8,128)(2,1)S(1)} %collective-permute-done.far_ref, bf16[512,1024]{1,0:T(8,128)(2,1)S(1)} %get-tuple-element.14.agg_ref, f32[8,2048]{1,0:T(8,128)S(1)} %get-tuple-element.15.cos_ref, ...), custom_call_target="tpu_custom_call" | custom-call | flops 1207959552 | bytes 10485760 | tf_op jit(solution)/shard_map/pallas_call | solution.py:21
  8.6 7.5 %all-to-all-start = ((bf16[16,32,128]{2,1,0:T(8,128)(2,1)}), bf16[16,32,128]{2,1,0:T(8,128)(2,1)S(1)}, u32[]{:S(2)}, u32[]{:S(2)}) async-start(bf16[16,32,128]{2,1,0:T(8,128)(2,1)} %get-tuple-element.18), calls=%async_computation | async-start | bytes 262144 | tf_op jit(solution)/shard_map/all_to_all | solution.py:312
  16.1 0.4 collective-permute-start.1
  16.5 3.1 %collective-permute-start.2 = (bf16[64,512]{1,0:T(8,128)(2,1)S(1)}, bf16[64,512]{1,0:T(8,128)(2,1)S(1)}, u32[]{:S(2)}, u32[]{:S(2)}) collective-permute-start(bf16[64,512]{1,0:T(8,128)(2,1)S(1)} %get-tuple-element.21), channel_id=1, source_target_pairs={{0,0},{1,2},{2,1},{3,4},{4,3},{5,6},{6,5},{7,8},{8,7},{9,10},{10,9... | collective-permute-start | bytes 196616 | tf_op jit(solution)/shard_map/ppermute | solution.py:315
  19.6 1.5 %slice.3.kept = bf16[1024,768]{1,0:T(8,128)(2,1)S(1)} slice(bf16[1024,4096]{1,0:T(8,128)(2,1)} %interp.3), slice={[0:1024], [0:768]} | slice | bytes 3145728 | tf_op jit(solution)/shard_map/slice | solution.py:346
  21.1 0.2 all-to-all-done.upper_ref
  21.4 1.4 %shard_map.102._ = bf16[16,16,128]{2,1,0:T(8,128)(2,1)} custom-call(bf16[16,32,128]{2,1,0:T(8,128)(2,1)S(1)} %all-to-all-done.upper_ref, s32[128,32]{1,0:T(8,128)S(1)} %get-tuple-element.19.index_ref, bf16[20,128,256]{2,1,0:T(8,128)(2,1)S(1)} %get-tuple-element.20.operator_ref), custom_call_target="tpu_custom_call" | custom-call | flops 335544320 | bytes 2097152 | tf_op jit(solution)/shard_map/pallas_call | solution.py:21
  22.8 0.0 copy-start
  22.8 6.7 %all-to-all-start.1 = ((bf16[16,16,128]{2,1,0:T(8,128)(2,1)}), bf16[16,16,128]{2,1,0:T(8,128)(2,1)S(1)}, u32[]{:S(2)}, u32[]{:S(2)}) async-start(bf16[16,16,128]{2,1,0:T(8,128)(2,1)} %shard_map.102._), calls=%async_computation.1 | async-start | bytes 131072 | tf_op jit(solution)/shard_map/all_to_all | solution.py:326
  29.6 0.0 collective-permute-done.1.sibling_ref
  29.6 0.0 collective-permute-done.2.cross_ref
  29.6 5.8 %shard_map.103.near_ref = f32[64,512]{1,0:T(8,128)S(1)} custom-call(bf16[64,512]{1,0:T(8,128)(2,1)S(1)} %copy-done.1, bf16[64,512]{1,0:T(8,128)(2,1)S(1)} %collective-permute-done.1.sibling_ref, bf16[64,512]{1,0:T(8,128)(2,1)S(1)} %collective-permute-done.2.cross_ref, s32[64,32]{1,0:T(8,128)S(1)} %get-tuple-element.22.col_ref, ...), custom_call_target="tpu_custom_call" | custom-call | flops 1132462080 | bytes 15728640 | tf_op jit(solution)/shard_map/pallas_call | solution.py:21
  35.4 0.0 all-to-all-done.1.inc_ref
  35.4 0.0 copy-done
  35.4 4.8 %shard_map.104 = f32[64,512]{1,0:T(8,128)} custom-call(bf16[16,16,128]{2,1,0:T(8,128)(2,1)S(1)} %all-to-all-done.1.inc_ref, f32[8,2048]{1,0:T(8,128)S(1)} %get-tuple-element.15.cos_ref, f32[8,2048]{1,0:T(8,128)S(1)} %get-tuple-element.16.sin_ref, f32[64,512]{1,0:T(8,128)S(1)} %shard_map.103.near_ref, bf16[1024,512]{1,0:T(8,128)(2,1)S(1)} %copy-done, ...), custom_call_target="tpu_custom_call" | custom-call | flops 805306368 | bytes 10485760 | tf_op jit(solution)/shard_map/pallas_call | solution.py:21
Async XLA Ops:
  0.0 6.0 %copy-start.1 = (bf16[64,512]{1,0:T(8,128)(2,1)S(1)}, bf16[64,512]{1,0:T(8,128)(2,1)}, u32[]{:S(2)}) copy-start(bf16[64,512]{1,0:T(8,128)(2,1)} %own_ref.3) | copy-start | bytes 196612
  0.0 6.0 %collective-permute-start = (bf16[64,512]{1,0:T(8,128)(2,1)}, bf16[64,512]{1,0:T(8,128)(2,1)S(1)}, u32[]{:S(2)}, u32[]{:S(2)}) collective-permute-start(bf16[64,512]{1,0:T(8,128)(2,1)} %own_ref.3), channel_id=1, source_target_pairs={{0,12},{1,13},{2,14},{3,15},{4,8},{5,9},{6,10},{7,11},{8,26},{9,27... | collective-permute-start | bytes 196616 | tf_op jit(solution)/shard_map/ppermute | solution.py:257
  8.6 12.8 %all-to-all-start = ((bf16[16,32,128]{2,1,0:T(8,128)(2,1)}), bf16[16,32,128]{2,1,0:T(8,128)(2,1)S(1)}, u32[]{:S(2)}, u32[]{:S(2)}) async-start(bf16[16,32,128]{2,1,0:T(8,128)(2,1)} %get-tuple-element.18), calls=%async_computation | async-start | bytes 262144 | tf_op jit(solution)/shard_map/all_to_all | solution.py:312
  16.1 13.4 %collective-permute-start.1 = (bf16[64,512]{1,0:T(8,128)(2,1)S(1)}, bf16[64,512]{1,0:T(8,128)(2,1)S(1)}, u32[]{:S(2)}, u32[]{:S(2)}) collective-permute-start(bf16[64,512]{1,0:T(8,128)(2,1)S(1)} %copy-done.1), channel_id=1, source_target_pairs={{0,1},{1,0},{2,3},{3,2},{4,5},{5,4},{6,7},{7,6},{8,9},{9,8},{10,11... | collective-permute-start | bytes 196616 | tf_op jit(solution)/shard_map/ppermute | solution.py:258
  16.5 13.1 %collective-permute-start.2 = (bf16[64,512]{1,0:T(8,128)(2,1)S(1)}, bf16[64,512]{1,0:T(8,128)(2,1)S(1)}, u32[]{:S(2)}, u32[]{:S(2)}) collective-permute-start(bf16[64,512]{1,0:T(8,128)(2,1)S(1)} %get-tuple-element.21), channel_id=1, source_target_pairs={{0,0},{1,2},{2,1},{3,4},{4,3},{5,6},{6,5},{7,8},{8,7},{9,10},{10,9... | collective-permute-start | bytes 196616 | tf_op jit(solution)/shard_map/ppermute | solution.py:315
  22.8 12.6 %copy-start = (bf16[1024,512]{1,0:T(8,128)(2,1)S(1)}, bf16[1024,512]{1,0:T(8,128)(2,1)}, u32[]{:S(2)}) copy-start(bf16[1024,512]{1,0:T(8,128)(2,1)} %receive_ref.1) | copy-start | bytes 3145732
  22.8 12.6 %all-to-all-start.1 = ((bf16[16,16,128]{2,1,0:T(8,128)(2,1)}), bf16[16,16,128]{2,1,0:T(8,128)(2,1)S(1)}, u32[]{:S(2)}, u32[]{:S(2)}) async-start(bf16[16,16,128]{2,1,0:T(8,128)(2,1)} %shard_map.102._), calls=%async_computation.1 | async-start | bytes 131072 | tf_op jit(solution)/shard_map/all_to_all | solution.py:326

commit v8 on v5

--- a/solution.py
+++ b/solution.py
@@ -10,6 +10,7 @@
 BF16, F32, I32 = jnp.bfloat16, jnp.float32, jnp.int32
 BOTH = ("box", "dir")
 VMEM = pltpu.VMEM
+AHEAD = 5 * 10**9
 
 
 def whole(space=VMEM):
@@ -47,15 +48,11 @@
     angle_hbm,
     table_hbm,
     near_list_hbm,
-    aggregate,
-    interp,
     operators,
     index_ref,
     column_ref,
     cosine_ref,
     sine_ref,
-    aggregate_out,
-    interp_out,
     far_ref,
     kind_ref,
     angle_ref,
@@ -74,11 +71,7 @@
         pltpu.make_async_copy(near_list_hbm, near_list_ref, sems.at[3]),
         pltpu.make_async_copy(angle_hbm, angle_ref, sems.at[4]),
     ]
-    weights = [
-        pltpu.make_async_copy(aggregate, aggregate_out, sems.at[5]),
-        pltpu.make_async_copy(interp, interp_out, sems.at[6]),
-    ]
-    for copy in copies + weights:
+    for copy in copies:
         copy.start()
     table[...] = jnp.zeros_like(table)
     for copy in copies:
@@ -110,8 +103,6 @@
     for j in range(slots):
         hot = jnp.where(lane == kind[:, j : j + 1], 1.0, 0.0).astype(BF16)
         operators[j] = dot(hot, table[...]).astype(BF16)
-    for copy in weights:
-        copy.wait()
 
 
 def up_kernel(own_ref, far_ref, agg_ref, cos_ref, sin_ref, interp, out_ref, relay_ref):
@@ -171,14 +162,13 @@
     out_ref[:, 8:16, :] = acc_im.reshape(blocks, 8, 128).astype(BF16)
 
 
-def down_kernel(inc_ref, cos_ref, sin_ref, near_ref, receive, interp, out_ref, buf, received, receive_ref, sems):
+def down_kernel(inc_ref, cos_ref, sin_ref, near_ref, receive_ref, interp, out_ref, buf, received, sems):
     width = 256
     chunks = buf.shape[1] // width
     copies = []
     for j in range(chunks):
         lanes = pl.ds(j * width, width)
         copies.append(pltpu.make_async_copy(interp.at[:, lanes], buf.at[:, lanes], sems.at[j]))
-    copies.append(pltpu.make_async_copy(receive, receive_ref, sems.at[chunks]))
     for copy in copies:
         copy.start()
     leaves = received.shape[0]
@@ -199,7 +189,6 @@
         lanes = slice(j * width, (j + 1) * width)
         copies[j].wait()
         back += dot(received[:, lanes], buf[:, lanes], 1, 1)
-    copies[chunks].wait()
     out_ref[...] = near_ref[...] + dot(back.astype(BF16), receive_ref[...])
 
 
@@ -258,7 +247,7 @@
     from_sibling = lax.ppermute(currents, BOTH, [(i, i ^ 1) for i in range(n)])
 
     place = jnp.stack([box, me]).astype(I32)
-    operators, index, column, cosine, sine, held_aggregate, held = call(
+    operators, index, column, cosine, sine = call(
         prepare_kernel,
         (
             pltpu.VMEM((slots, parents, 256), BF16),
@@ -266,8 +255,6 @@
             pltpu.VMEM((leaves, 32), I32),
             pltpu.VMEM(shift_angle.shape, F32),
             pltpu.VMEM(shift_angle.shape, F32),
-            pltpu.VMEM(aggregate.shape, BF16),
-            pltpu.VMEM(interp.shape, BF16),
         ),
         (
             place,
@@ -277,11 +264,9 @@
                 shift_angle,
                 translation.reshape(-1, translation.shape[2]),
                 near_list.T,
-                aggregate,
-                interp,
             ),
         ),
-        [whole(pltpu.SMEM)] + [whole(pltpu.HBM)] * 7,
+        [whole(pltpu.SMEM)] + [whole(pltpu.HBM)] * 5,
         [
             pltpu.VMEM((slots, parents), I32),
             pltpu.VMEM((slots, parents), I32),
@@ -289,10 +274,10 @@
             pltpu.VMEM((2 * translation.shape[0], translation.shape[2]), F32),
             pltpu.VMEM((near_slots, leaves), I32),
             pltpu.VMEM((384, 256), BF16),
-            pltpu.SemaphoreType.DMA((7,)),
+            pltpu.SemaphoreType.DMA((5,)),
         ],
         8,
-        2 * slots * parents * 384 * 256,
+        AHEAD,
         11 << 20,
     )
 
@@ -302,7 +287,7 @@
             jax.ShapeDtypeStruct((dirs, 4 * leaves // 8, 128), BF16),
             jax.ShapeDtypeStruct(currents.shape, BF16),
         ),
-        (currents, far_half, held_aggregate, cosine, sine, in_vmem(held)),
+        (currents, far_half, in_vmem(aggregate), cosine, sine, in_vmem(interp)),
         [whole()] * 6,
         [],
         8,
@@ -343,13 +328,12 @@
     return call(
         down_kernel,
         jax.ShapeDtypeStruct((leaves, width), F32),
-        (incoming, cosine, sine, near, *in_hbm(receive, interp)),
-        [whole()] * 4 + [whole(pltpu.HBM)] * 2,
+        (incoming, cosine, sine, near, in_vmem(receive), *in_hbm(interp)),
+        [whole()] * 5 + [whole(pltpu.HBM)],
         [
             pltpu.VMEM(interp.shape, BF16),
             pltpu.VMEM((leaves, interp.shape[1]), BF16),
-            pltpu.VMEM(receive.shape, BF16),
-            pltpu.SemaphoreType.DMA((interp.shape[1] // 256 + 1,)),
+            pltpu.SemaphoreType.DMA((interp.shape[1] // 256,)),
         ],
         16,
         2 * 64 * 4096 * 1536,

time: 39.7 us -> 39.1 us (0.985); the launches traced: 39 us -> 38.8 us
  Pallas kernels: 19.6 us -> 18.2 us
  starting transfers between devices: 17.5 us -> 18.2 us
  local copies, waits for them, and re-layouts: 0.01 us -> 0.57 us
    pallas_call x5, Pallas kernels: 19.6 us -> 18.2 us  [call(): pl.pallas_call(body, out_shape=out, in_specs=specs, out_specs=jax.tree.ma...]
    all_to_all x1, starting transfers between devices: 5.06 us -> 5.65 us  [on_device(): lax.all_to_all(local, 'dir', split_axis=0, concat_axis=0, tiled=True)]
    unnamed x2 -> x8, local copies, waits for them, and re-layouts: 0.01 us -> 0.57 us
  transfers between devices with their start and end apart: 5 -> 5, of which waited for: 1 -> 1; matrix products, arithmetic and copies ran while one was open for 0% -> 0% of each run, Pallas kernels for 30% -> 27%
where the time goes in v8:
time: 39.1 us; the launch traced here: 38.8 us
  starting transfers between devices  18.2 us (47%)
  Pallas kernels  18.2 us (47%)
  waiting for transfers between devices  1.77 us (5%)
  local copies, waits for them, and re-layouts  0.57 us (1%)
    pallas_call x5, Pallas kernels, call(): pl.pallas_call(body, out_shape=out, in_specs=specs, out_specs=jax.tree.ma...  18.2 us
    all_to_all x1, starting transfers between devices, on_device(): upper = lax.all_to_all(up, 'dir', split_axis=0, concat_axis=0, tiled=True)  7.69 us
    all_to_all x1, starting transfers between devices, on_device(): lax.all_to_all(local, 'dir', split_axis=0, concat_axis=0, tiled=True)  5.65 us
    ppermute x1, starting transfers between devices, on_device(): from_cross = lax.ppermute(relay, BOTH, cross)  3.11 us
    all_to_all x1, waiting for transfers between devices, on_device(): upper = lax.all_to_all(up, 'dir', split_axis=0, concat_axis=0, tiled=True)  1.76 us
    ppermute x1, starting transfers between devices, on_device(): lax.ppermute(currents, BOTH, [(i, halo_target(i, boxes, dirs)) for i in r...  1.39 us
  transfers between devices with their start and end apart: 5, of which 1 were waited for; matrix products, arithmetic and copies ran while one was open for 0% of the time, Pallas kernels for 27%

profile of v8, /device:TPU:27, one launch (start us, length us, event | category | flops | bytes accessed | tf_op | source)
XLA Modules:
  0.0 38.8 jit_solution(15347239419424388252)
XLA Ops:
  0.0 1.4 %collective-permute-start = (bf16[64,512]{1,0:T(8,128)(2,1)}, bf16[64,512]{1,0:T(8,128)(2,1)S(1)}, u32[]{:S(2)}, u32[]{:S(2)}) collective-permute-start(bf16[64,512]{1,0:T(8,128)(2,1)} %own_ref.3), channel_id=1, source_target_pairs={{0,12},{1,13},{2,14},{3,15},{4,8},{5,9},{6,10},{7,11},{8,26},{9,27... | collective-permute-start | bytes 196616 | tf_op jit(solution)/shard_map/ppermute | solution.py:246
  1.4 0.1 pad_add_fusion.place_ref
  1.5 0.0 copy-start
  1.5 0.0 copy-start.1
  1.5 0.0 copy-start.3
  1.5 3.2 %shard_map.100 = (bf16[20,128,256]{2,1,0:T(8,128)(2,1)S(1)}, s32[128,32]{1,0:T(8,128)S(1)}, s32[64,32]{1,0:T(8,128)S(1)}, f32[8,2048]{1,0:T(8,128)S(1)}, f32[8,2048]{1,0:T(8,128)S(1)}) custom-call(s32[2]{0:T(128)S(1)} %pad_add_fusion.place_ref, s32[20,1024]{1,0:T(8,128)} %bitcast.7, s32[20,1024]{1,0:T(8,128)} %bitcast.8, f32[8,2048]{1,0:T(8,128)} %angle_hbm.1, ...), custom_call_target="tpu_custom_call" | custom-call | flops 5000000000 | bytes 11534336 | tf_op jit(solution)/shard_map/pallas_call | solution.py:21
  4.7 0.0 collective-permute-done.far_ref
  4.7 0.3 copy-done
  5.0 0.2 copy-done.1
  5.3 0.0 copy-done.3
  5.3 2.6 %shard_map.101 = (bf16[16,32,128]{2,1,0:T(8,128)(2,1)}, bf16[64,512]{1,0:T(8,128)(2,1)S(1)}) custom-call(bf16[64,512]{1,0:T(8,128)(2,1)S(1)} %copy-done.3, bf16[64,512]{1,0:T(8,128)(2,1)S(1)} %collective-permute-done.far_ref, bf16[512,1024]{1,0:T(8,128)(2,1)S(1)} %copy-done.1, f32[8,2048]{1,0:T(8,128)S(1)} %get-tuple-element.12.cos_ref, ...), custom_call_target="tpu_custom_call" | custom-call | flops 1207959552 | bytes 10485760 | tf_op jit(solution)/shard_map/pallas_call | solution.py:21
  7.8 0.0 copy-start.2
  7.8 7.7 %all-to-all-start = ((bf16[16,32,128]{2,1,0:T(8,128)(2,1)}), bf16[16,32,128]{2,1,0:T(8,128)(2,1)S(1)}, u32[]{:S(2)}, u32[]{:S(2)}) async-start(bf16[16,32,128]{2,1,0:T(8,128)(2,1)} %get-tuple-element.14), calls=%async_computation | async-start | bytes 262144 | tf_op jit(solution)/shard_map/all_to_all | solution.py:297
  15.5 0.4 collective-permute-start.1
  15.9 3.1 %collective-permute-start.2 = (bf16[64,512]{1,0:T(8,128)(2,1)S(1)}, bf16[64,512]{1,0:T(8,128)(2,1)S(1)}, u32[]{:S(2)}, u32[]{:S(2)}) collective-permute-start(bf16[64,512]{1,0:T(8,128)(2,1)S(1)} %get-tuple-element.17), channel_id=1, source_target_pairs={{0,0},{1,2},{2,1},{3,4},{4,3},{5,6},{6,5},{7,8},{8,7},{9,10},{10,9... | collective-permute-start | bytes 196616 | tf_op jit(solution)/shard_map/ppermute | solution.py:300
  19.0 1.8 %all-to-all-done.upper_ref = bf16[16,32,128]{2,1,0:T(8,128)(2,1)S(1)} async-done(((bf16[16,32,128]{2,1,0:T(8,128)(2,1)}), bf16[16,32,128]{2,1,0:T(8,128)(2,1)S(1)}, u32[]{:S(2)}, u32[]{:S(2)}) %all-to-all-start) | async-done | bytes 131104 | tf_op jit(solution)/shard_map/all_to_all | solution.py:297
  20.8 1.4 %shard_map.102._ = bf16[16,16,128]{2,1,0:T(8,128)(2,1)} custom-call(bf16[16,32,128]{2,1,0:T(8,128)(2,1)S(1)} %all-to-all-done.upper_ref, s32[128,32]{1,0:T(8,128)S(1)} %get-tuple-element.15.index_ref, bf16[20,128,256]{2,1,0:T(8,128)(2,1)S(1)} %get-tuple-element.16.operator_ref), custom_call_target="tpu_custom_call" | custom-call | flops 335544320 | bytes 2097152 | tf_op jit(solution)/shard_map/pallas_call | solution.py:21
  22.2 5.7 %all-to-all-start.1 = ((bf16[16,16,128]{2,1,0:T(8,128)(2,1)}), bf16[16,16,128]{2,1,0:T(8,128)(2,1)S(1)}, u32[]{:S(2)}, u32[]{:S(2)}) async-start(bf16[16,16,128]{2,1,0:T(8,128)(2,1)} %shard_map.102._), calls=%async_computation.1 | async-start | bytes 131072 | tf_op jit(solution)/shard_map/all_to_all | solution.py:311
  27.9 0.0 collective-permute-done.1.sibling_ref
  27.9 0.0 collective-permute-done.2.cross_ref
  27.9 5.8 %shard_map.103.near_ref = f32[64,512]{1,0:T(8,128)S(1)} custom-call(bf16[64,512]{1,0:T(8,128)(2,1)S(1)} %copy-done.3, bf16[64,512]{1,0:T(8,128)(2,1)S(1)} %collective-permute-done.1.sibling_ref, bf16[64,512]{1,0:T(8,128)(2,1)S(1)} %collective-permute-done.2.cross_ref, s32[64,32]{1,0:T(8,128)S(1)} %get-tuple-element.18.col_ref, ...), custom_call_target="tpu_custom_call" | custom-call | flops 1132462080 | bytes 15728640 | tf_op jit(solution)/shard_map/pallas_call | solution.py:21
  33.8 0.0 all-to-all-done.1.inc_ref
  33.8 0.0 copy-done.2
  33.8 5.1 %shard_map.104 = f32[64,512]{1,0:T(8,128)} custom-call(bf16[16,16,128]{2,1,0:T(8,128)(2,1)S(1)} %all-to-all-done.1.inc_ref, f32[8,2048]{1,0:T(8,128)S(1)} %get-tuple-element.12.cos_ref, f32[8,2048]{1,0:T(8,128)S(1)} %get-tuple-element.13.sin_ref, f32[64,512]{1,0:T(8,128)S(1)} %shard_map.103.near_ref, bf16[1024,512]{1,0:T(8,128)(2,1)S(1)} %copy-done.2, ...), custom_call_target="tpu_custom_call" | custom-call | flops 805306368 | bytes 10485760 | tf_op jit(solution)/shard_map/pallas_call | solution.py:21
Async XLA Ops:
  0.0 4.7 %collective-permute-start = (bf16[64,512]{1,0:T(8,128)(2,1)}, bf16[64,512]{1,0:T(8,128)(2,1)S(1)}, u32[]{:S(2)}, u32[]{:S(2)}) collective-permute-start(bf16[64,512]{1,0:T(8,128)(2,1)} %own_ref.3), channel_id=1, source_target_pairs={{0,12},{1,13},{2,14},{3,15},{4,8},{5,9},{6,10},{7,11},{8,26},{9,27... | collective-permute-start | bytes 196616 | tf_op jit(solution)/shard_map/ppermute | solution.py:246
  1.5 3.6 %copy-start = (bf16[1024,4096]{1,0:T(8,128)(2,1)S(1)}, bf16[1024,4096]{1,0:T(8,128)(2,1)}, u32[]{:S(2)}) copy-start(bf16[1024,4096]{1,0:T(8,128)(2,1)} %interp.3) | copy-start | bytes 25165828
  1.5 3.8 %copy-start.1 = (bf16[512,1024]{1,0:T(8,128)(2,1)S(1)}, bf16[512,1024]{1,0:T(8,128)(2,1)}, u32[]{:S(2)}) copy-start(bf16[512,1024]{1,0:T(8,128)(2,1)} %agg_ref.1) | copy-start | bytes 3145732
  1.5 3.8 %copy-start.3 = (bf16[64,512]{1,0:T(8,128)(2,1)S(1)}, bf16[64,512]{1,0:T(8,128)(2,1)}, u32[]{:S(2)}) copy-start(bf16[64,512]{1,0:T(8,128)(2,1)} %own_ref.3) | copy-start | bytes 196612
  7.8 25.9 %copy-start.2 = (bf16[1024,512]{1,0:T(8,128)(2,1)S(1)}, bf16[1024,512]{1,0:T(8,128)(2,1)}, u32[]{:S(2)}) copy-start(bf16[1024,512]{1,0:T(8,128)(2,1)} %receive_ref.1) | copy-start | bytes 3145732
  7.8 12.9 %all-to-all-start = ((bf16[16,32,128]{2,1,0:T(8,128)(2,1)}), bf16[16,32,128]{2,1,0:T(8,128)(2,1)S(1)}, u32[]{:S(2)}, u32[]{:S(2)}) async-start(bf16[16,32,128]{2,1,0:T(8,128)(2,1)} %get-tuple-element.14), calls=%async_computation | async-start | bytes 262144 | tf_op jit(solution)/shard_map/all_to_all | solution.py:297
  15.5 12.3 %collective-permute-start.1 = (bf16[64,512]{1,0:T(8,128)(2,1)S(1)}, bf16[64,512]{1,0:T(8,128)(2,1)S(1)}, u32[]{:S(2)}, u32[]{:S(2)}) collective-permute-start(bf16[64,512]{1,0:T(8,128)(2,1)S(1)} %copy-done.3), channel_id=1, source_target_pairs={{0,1},{1,0},{2,3},{3,2},{4,5},{5,4},{6,7},{7,6},{8,9},{9,8},{10,11... | collective-permute-start | bytes 196616 | tf_op jit(solution)/shard_map/ppermute | solution.py:247
  15.9 12.0 %collective-permute-start.2 = (bf16[64,512]{1,0:T(8,128)(2,1)S(1)}, bf16[64,512]{1,0:T(8,128)(2,1)S(1)}, u32[]{:S(2)}, u32[]{:S(2)}) collective-permute-start(bf16[64,512]{1,0:T(8,128)(2,1)S(1)} %get-tuple-element.17), channel_id=1, source_target_pairs={{0,0},{1,2},{2,1},{3,4},{4,3},{5,6},{6,5},{7,8},{8,7},{9,10},{10,9... | collective-permute-start | bytes 196616 | tf_op jit(solution)/shard_map/ppermute | solution.py:300
  22.2 11.5 %all-to-all-start.1 = ((bf16[16,16,128]{2,1,0:T(8,128)(2,1)}), bf16[16,16,128]{2,1,0:T(8,128)(2,1)S(1)}, u32[]{:S(2)}, u32[]{:S(2)}) async-start(bf16[16,16,128]{2,1,0:T(8,128)(2,1)} %shard_map.102._), calls=%async_computation.1 | async-start | bytes 131072 | tf_op jit(solution)/shard_map/all_to_all | solution.py:311

commit v9 on v8

--- a/solution.py
+++ b/solution.py
@@ -10,6 +10,7 @@
 BF16, F32, I32 = jnp.bfloat16, jnp.float32, jnp.int32
 BOTH = ("box", "dir")
 VMEM = pltpu.VMEM
+KEPT = 3
 AHEAD = 5 * 10**9
 
 
@@ -105,7 +106,11 @@
         operators[j] = dot(hot, table[...]).astype(BF16)
 
 
-def up_kernel(own_ref, far_ref, agg_ref, cos_ref, sin_ref, interp, out_ref, relay_ref):
+def up_kernel(
+    own_ref, far_ref, agg_ref, cos_ref, sin_ref, interp, out_ref, relay_ref, kept, sem
+):
+    copy = pltpu.make_async_copy(interp.at[:, pl.ds(0, KEPT * 256)], kept, sem)
+    copy.start()
     relay_ref[...] = own_ref[...]
     width = 256
     directions = cos_ref.shape[1]
@@ -134,6 +139,7 @@
             s = slice(h * 128, (h + 1) * 128)
             out_ref[j * (width // 128) + h, 0:parents, :] = acc_re[:, s].astype(BF16)
             out_ref[j * (width // 128) + h, parents : 2 * parents, :] = acc_im[:, s].astype(BF16)
+    copy.wait()
 
 
 def translate_kernel(upper_ref, index_ref, operator_ref, out_ref):
@@ -162,13 +168,14 @@
     out_ref[:, 8:16, :] = acc_im.reshape(blocks, 8, 128).astype(BF16)
 
 
-def down_kernel(inc_ref, cos_ref, sin_ref, near_ref, receive_ref, interp, out_ref, buf, received, sems):
+def down_kernel(inc_ref, cos_ref, sin_ref, near_ref, receive_ref, kept, interp, out_ref, buf, received, sems):
     width = 256
     chunks = buf.shape[1] // width
     copies = []
     for j in range(chunks):
-        lanes = pl.ds(j * width, width)
-        copies.append(pltpu.make_async_copy(interp.at[:, lanes], buf.at[:, lanes], sems.at[j]))
+        source = interp.at[:, pl.ds((KEPT + j) * width, width)]
+        target = buf.at[:, pl.ds(j * width, width)]
+        copies.append(pltpu.make_async_copy(source, target, sems.at[j]))
     for copy in copies:
         copy.start()
     leaves = received.shape[0]
@@ -184,11 +191,11 @@
         received[:, half + s * 128 : half + (s + 1) * 128] = (
             (im * cosine - re * sine).reshape(leaves, 128).astype(BF16)
         )
-    back = jnp.zeros((leaves, buf.shape[0]), F32)
+    back = dot(received[:, : KEPT * width], kept[...], 1, 1)
     for j in range(chunks):
-        lanes = slice(j * width, (j + 1) * width)
+        at = (KEPT + j) * width
         copies[j].wait()
-        back += dot(received[:, lanes], buf[:, lanes], 1, 1)
+        back += dot(received[:, at : at + width], buf[:, j * width : (j + 1) * width], 1, 1)
     out_ref[...] = near_ref[...] + dot(back.astype(BF16), receive_ref[...])
 
 
@@ -281,15 +288,16 @@
         11 << 20,
     )
 
-    up, relay = call(
+    up, relay, kept = call(
         up_kernel,
         (
             jax.ShapeDtypeStruct((dirs, 4 * leaves // 8, 128), BF16),
             jax.ShapeDtypeStruct(currents.shape, BF16),
+            pltpu.VMEM((interp.shape[0], KEPT * 256), BF16),
         ),
         (currents, far_half, in_vmem(aggregate), cosine, sine, in_vmem(interp)),
         [whole()] * 6,
-        [],
+        [pltpu.SemaphoreType.DMA],
         8,
         2 * 128 * 1024 * 4608,
         10 << 20,
@@ -328,10 +336,10 @@
     return call(
         down_kernel,
         jax.ShapeDtypeStruct((leaves, width), F32),
-        (incoming, cosine, sine, near, in_vmem(receive), *in_hbm(interp)),
-        [whole()] * 5 + [whole(pltpu.HBM)],
+        (incoming, cosine, sine, near, in_vmem(receive), in_vmem(kept), *in_hbm(interp)),
+        [whole()] * 6 + [whole(pltpu.HBM)],
         [
-            pltpu.VMEM(interp.shape, BF16),
+            pltpu.VMEM((interp.shape[0], interp.shape[1] - KEPT * 256), BF16),
             pltpu.VMEM((leaves, interp.shape[1]), BF16),
             pltpu.SemaphoreType.DMA((interp.shape[1] // 256,)),
         ],

time: 39.1 us -> 39.1 us (level)
  no operation moved by 1% of the time
where the time goes in v9:
time: 39.1 us; the launch traced here: 38.8 us
  starting transfers between devices  18.2 us (47%)
  Pallas kernels  18.2 us (47%)
  waiting for transfers between devices  1.77 us (5%)
  local copies, waits for them, and re-layouts  0.57 us (1%)
    pallas_call x5, Pallas kernels, call(): pl.pallas_call(body, out_shape=out, in_specs=specs, out_specs=jax.tree.ma...  18.2 us
    all_to_all x1, starting transfers between devices, on_device(): upper = lax.all_to_all(up, 'dir', split_axis=0, concat_axis=0, tiled=True)  7.55 us
    all_to_all x1, starting transfers between devices, on_device(): lax.all_to_all(local, 'dir', split_axis=0, concat_axis=0, tiled=True)  5.79 us
    ppermute x1, starting transfers between devices, on_device(): from_cross = lax.ppermute(relay, BOTH, cross)  3.11 us
    all_to_all x1, waiting for transfers between devices, on_device(): upper = lax.all_to_all(up, 'dir', split_axis=0, concat_axis=0, tiled=True)  1.76 us
    ppermute x1, starting transfers between devices, on_device(): lax.ppermute(currents, BOTH, [(i, halo_target(i, boxes, dirs)) for i in r...  1.39 us
  transfers between devices with their start and end apart: 5, of which 1 were waited for; matrix products, arithmetic and copies ran while one was open for 0% of the time, Pallas kernels for 27%

profile of v9, /device:TPU:27, one launch (start us, length us, event | category | flops | bytes accessed | tf_op | source)
XLA Modules:
  0.0 38.8 jit_solution(248433304705740010)
XLA Ops:
  0.0 1.4 %collective-permute-start = (bf16[64,512]{1,0:T(8,128)(2,1)}, bf16[64,512]{1,0:T(8,128)(2,1)S(1)}, u32[]{:S(2)}, u32[]{:S(2)}) collective-permute-start(bf16[64,512]{1,0:T(8,128)(2,1)} %own_ref.3), channel_id=1, source_target_pairs={{0,12},{1,13},{2,14},{3,15},{4,8},{5,9},{6,10},{7,11},{8,26},{9,27... | collective-permute-start | bytes 196616 | tf_op jit(solution)/shard_map/ppermute | solution.py:253
  1.4 0.1 pad_add_fusion.place_ref
  1.5 0.0 copy-start
  1.5 0.0 copy-start.1
  1.5 0.0 copy-start.3
  1.5 3.2 %shard_map.100 = (bf16[20,128,256]{2,1,0:T(8,128)(2,1)S(1)}, s32[128,32]{1,0:T(8,128)S(1)}, s32[64,32]{1,0:T(8,128)S(1)}, f32[8,2048]{1,0:T(8,128)S(1)}, f32[8,2048]{1,0:T(8,128)S(1)}) custom-call(s32[2]{0:T(128)S(1)} %pad_add_fusion.place_ref, s32[20,1024]{1,0:T(8,128)} %bitcast.7, s32[20,1024]{1,0:T(8,128)} %bitcast.8, f32[8,2048]{1,0:T(8,128)} %angle_hbm.1, ...), custom_call_target="tpu_custom_call" | custom-call | flops 5000000000 | bytes 11534336 | tf_op jit(solution)/shard_map/pallas_call | solution.py:22
  4.7 0.0 collective-permute-done.far_ref
  4.7 0.3 copy-done
  5.0 0.2 copy-done.1
  5.3 0.0 copy-done.3
  5.3 2.8 %shard_map.101 = (bf16[16,32,128]{2,1,0:T(8,128)(2,1)}, bf16[64,512]{1,0:T(8,128)(2,1)S(1)}, bf16[1024,768]{1,0:T(8,128)(2,1)S(1)}) custom-call(bf16[64,512]{1,0:T(8,128)(2,1)S(1)} %copy-done.3, bf16[64,512]{1,0:T(8,128)(2,1)S(1)} %collective-permute-done.far_ref, bf16[512,1024]{1,0:T(8,128)(2,1)S(1)} %copy-done.1, f32[8,2048]{1,0:T(8,128)S(1)} %get-tuple-element.13.cos_ref, ...), custom_call_target="tpu_custom_call" | custom-call | flops 1207959552 | bytes 10485760 | tf_op jit(solution)/shard_map/pallas_call | solution.py:22
  8.1 7.5 %all-to-all-start = ((bf16[16,32,128]{2,1,0:T(8,128)(2,1)}), bf16[16,32,128]{2,1,0:T(8,128)(2,1)S(1)}, u32[]{:S(2)}, u32[]{:S(2)}) async-start(bf16[16,32,128]{2,1,0:T(8,128)(2,1)} %get-tuple-element.15), calls=%async_computation | async-start | bytes 262144 | tf_op jit(solution)/shard_map/all_to_all | solution.py:305
  15.6 0.4 collective-permute-start.1
  16.0 3.1 %collective-permute-start.2 = (bf16[64,512]{1,0:T(8,128)(2,1)S(1)}, bf16[64,512]{1,0:T(8,128)(2,1)S(1)}, u32[]{:S(2)}, u32[]{:S(2)}) collective-permute-start(bf16[64,512]{1,0:T(8,128)(2,1)S(1)} %get-tuple-element.18), channel_id=1, source_target_pairs={{0,0},{1,2},{2,1},{3,4},{4,3},{5,6},{6,5},{7,8},{8,7},{9,10},{10,9... | collective-permute-start | bytes 196616 | tf_op jit(solution)/shard_map/ppermute | solution.py:308
  19.1 1.8 %all-to-all-done.upper_ref = bf16[16,32,128]{2,1,0:T(8,128)(2,1)S(1)} async-done(((bf16[16,32,128]{2,1,0:T(8,128)(2,1)}), bf16[16,32,128]{2,1,0:T(8,128)(2,1)S(1)}, u32[]{:S(2)}, u32[]{:S(2)}) %all-to-all-start) | async-done | bytes 131104 | tf_op jit(solution)/shard_map/all_to_all | solution.py:305
  20.9 1.4 %shard_map.102._ = bf16[16,16,128]{2,1,0:T(8,128)(2,1)} custom-call(bf16[16,32,128]{2,1,0:T(8,128)(2,1)S(1)} %all-to-all-done.upper_ref, s32[128,32]{1,0:T(8,128)S(1)} %get-tuple-element.16.index_ref, bf16[20,128,256]{2,1,0:T(8,128)(2,1)S(1)} %get-tuple-element.17.operator_ref), custom_call_target="tpu_custom_call" | custom-call | flops 335544320 | bytes 2097152 | tf_op jit(solution)/shard_map/pallas_call | solution.py:22
  22.3 0.0 copy-start.2
  22.3 5.8 %all-to-all-start.1 = ((bf16[16,16,128]{2,1,0:T(8,128)(2,1)}), bf16[16,16,128]{2,1,0:T(8,128)(2,1)S(1)}, u32[]{:S(2)}, u32[]{:S(2)}) async-start(bf16[16,16,128]{2,1,0:T(8,128)(2,1)} %shard_map.102._), calls=%async_computation.1 | async-start | bytes 131072 | tf_op jit(solution)/shard_map/all_to_all | solution.py:319
  28.1 0.0 collective-permute-done.1.sibling_ref
  28.1 0.0 collective-permute-done.2.cross_ref
  28.1 5.8 %shard_map.103.near_ref = f32[64,512]{1,0:T(8,128)S(1)} custom-call(bf16[64,512]{1,0:T(8,128)(2,1)S(1)} %copy-done.3, bf16[64,512]{1,0:T(8,128)(2,1)S(1)} %collective-permute-done.1.sibling_ref, bf16[64,512]{1,0:T(8,128)(2,1)S(1)} %collective-permute-done.2.cross_ref, s32[64,32]{1,0:T(8,128)S(1)} %get-tuple-element.19.col_ref, ...), custom_call_target="tpu_custom_call" | custom-call | flops 1132462080 | bytes 15728640 | tf_op jit(solution)/shard_map/pallas_call | solution.py:22
  34.0 0.0 all-to-all-done.1.inc_ref
  34.0 0.0 copy-done.2
  34.0 4.8 %shard_map.104 = f32[64,512]{1,0:T(8,128)} custom-call(bf16[16,16,128]{2,1,0:T(8,128)(2,1)S(1)} %all-to-all-done.1.inc_ref, f32[8,2048]{1,0:T(8,128)S(1)} %get-tuple-element.13.cos_ref, f32[8,2048]{1,0:T(8,128)S(1)} %get-tuple-element.14.sin_ref, f32[64,512]{1,0:T(8,128)S(1)} %shard_map.103.near_ref, bf16[1024,512]{1,0:T(8,128)(2,1)S(1)} %copy-done.2, ...), custom_call_target="tpu_custom_call" | custom-call | flops 805306368 | bytes 10485760 | tf_op jit(solution)/shard_map/pallas_call | solution.py:22
Async XLA Ops:
  0.0 4.7 %collective-permute-start = (bf16[64,512]{1,0:T(8,128)(2,1)}, bf16[64,512]{1,0:T(8,128)(2,1)S(1)}, u32[]{:S(2)}, u32[]{:S(2)}) collective-permute-start(bf16[64,512]{1,0:T(8,128)(2,1)} %own_ref.3), channel_id=1, source_target_pairs={{0,12},{1,13},{2,14},{3,15},{4,8},{5,9},{6,10},{7,11},{8,26},{9,27... | collective-permute-start | bytes 196616 | tf_op jit(solution)/shard_map/ppermute | solution.py:253
  1.5 3.6 %copy-start = (bf16[1024,4096]{1,0:T(8,128)(2,1)S(1)}, bf16[1024,4096]{1,0:T(8,128)(2,1)}, u32[]{:S(2)}) copy-start(bf16[1024,4096]{1,0:T(8,128)(2,1)} %interp.3) | copy-start | bytes 25165828
  1.5 3.8 %copy-start.1 = (bf16[512,1024]{1,0:T(8,128)(2,1)S(1)}, bf16[512,1024]{1,0:T(8,128)(2,1)}, u32[]{:S(2)}) copy-start(bf16[512,1024]{1,0:T(8,128)(2,1)} %agg_ref.1) | copy-start | bytes 3145732
  1.5 3.8 %copy-start.3 = (bf16[64,512]{1,0:T(8,128)(2,1)S(1)}, bf16[64,512]{1,0:T(8,128)(2,1)}, u32[]{:S(2)}) copy-start(bf16[64,512]{1,0:T(8,128)(2,1)} %own_ref.3) | copy-start | bytes 196612
  8.1 12.8 %all-to-all-start = ((bf16[16,32,128]{2,1,0:T(8,128)(2,1)}), bf16[16,32,128]{2,1,0:T(8,128)(2,1)S(1)}, u32[]{:S(2)}, u32[]{:S(2)}) async-start(bf16[16,32,128]{2,1,0:T(8,128)(2,1)} %get-tuple-element.15), calls=%async_computation | async-start | bytes 262144 | tf_op jit(solution)/shard_map/all_to_all | solution.py:305
  15.6 12.5 %collective-permute-start.1 = (bf16[64,512]{1,0:T(8,128)(2,1)S(1)}, bf16[64,512]{1,0:T(8,128)(2,1)S(1)}, u32[]{:S(2)}, u32[]{:S(2)}) collective-permute-start(bf16[64,512]{1,0:T(8,128)(2,1)S(1)} %copy-done.3), channel_id=1, source_target_pairs={{0,1},{1,0},{2,3},{3,2},{4,5},{5,4},{6,7},{7,6},{8,9},{9,8},{10,11... | collective-permute-start | bytes 196616 | tf_op jit(solution)/shard_map/ppermute | solution.py:254
  16.0 12.1 %collective-permute-start.2 = (bf16[64,512]{1,0:T(8,128)(2,1)S(1)}, bf16[64,512]{1,0:T(8,128)(2,1)S(1)}, u32[]{:S(2)}, u32[]{:S(2)}) collective-permute-start(bf16[64,512]{1,0:T(8,128)(2,1)S(1)} %get-tuple-element.18), channel_id=1, source_target_pairs={{0,0},{1,2},{2,1},{3,4},{4,3},{5,6},{6,5},{7,8},{8,7},{9,10},{10,9... | collective-permute-start | bytes 196616 | tf_op jit(solution)/shard_map/ppermute | solution.py:308
  22.3 11.7 %copy-start.2 = (bf16[1024,512]{1,0:T(8,128)(2,1)S(1)}, bf16[1024,512]{1,0:T(8,128)(2,1)}, u32[]{:S(2)}) copy-start(bf16[1024,512]{1,0:T(8,128)(2,1)} %receive_ref.1) | copy-start | bytes 3145732
  22.3 11.7 %all-to-all-start.1 = ((bf16[16,16,128]{2,1,0:T(8,128)(2,1)}), bf16[16,16,128]{2,1,0:T(8,128)(2,1)S(1)}, u32[]{:S(2)}, u32[]{:S(2)}) async-start(bf16[16,16,128]{2,1,0:T(8,128)(2,1)} %shard_map.102._), calls=%async_computation.1 | async-start | bytes 131072 | tf_op jit(solution)/shard_map/all_to_all | solution.py:319

commit v10 on v9

--- a/solution.py
+++ b/solution.py
@@ -66,7 +66,9 @@
     box, me = place_ref[0], place_ref[1]
     mine = pl.ds(pl.multiple_of(box * parents, parents), parents)
     copies = [
-        pltpu.make_async_copy(table_hbm, table_ref, sems.at[0]),
+        pltpu.make_async_copy(
+            table_hbm, table_ref.at[pl.ds(0, table_hbm.shape[0])], sems.at[0]
+        ),
         pltpu.make_async_copy(far_hbm.at[:, mine], far_ref, sems.at[1]),
         pltpu.make_async_copy(kind_hbm.at[:, mine], kind_ref, sems.at[2]),
         pltpu.make_async_copy(near_list_hbm, near_list_ref, sems.at[3]),
@@ -74,7 +76,8 @@
     ]
     for copy in copies:
         copy.start()
-    table[...] = jnp.zeros_like(table)
+    used = table_hbm.shape[0]
+    table_ref[used:, :] = jnp.zeros((table_ref.shape[0] - used, table_ref.shape[1]), F32)
     for copy in copies:
         copy.wait()
     cosine_ref[...] = jnp.cos(angle_ref[...])
@@ -82,6 +85,7 @@
     kinds = table_ref.shape[0] // 2
     table[0:kinds, 0:128] = table_ref[pl.ds(0, kinds, stride=2), :].astype(BF16)
     table[0:kinds, 128:256] = table_ref[pl.ds(1, kinds, stride=2), :].astype(BF16)
+    table[kinds:, :] = jnp.zeros((table.shape[0] - kinds, table.shape[1]), BF16)
 
     leaves = near_list_ref.shape[1]
     rel = near_list_ref[...] - me * leaves
@@ -206,12 +210,13 @@
         copies.append(pltpu.make_async_copy(near_hbm.at[n], buf.at[n], sems.at[n]))
         copies[n].start()
     rows = out_ref.shape[0]
-    lane = lax.broadcasted_iota(I32, (rows, 3 * rows), 1)
+    lane = lax.broadcasted_iota(I32, (rows, 4 * rows), 1)
     for n in range(slots):
         hot[n * rows : (n + 1) * rows] = jnp.where(
             lane == col_ref[:, n : n + 1], 1.0, 0.0
         ).astype(BF16)
-    sources = jnp.concatenate([own_ref[...], sibling_ref[...], cross_ref[...]], axis=0)
+    blocks = (own_ref, sibling_ref, cross_ref, own_ref)
+    sources = jnp.concatenate([block[...] for block in blocks], axis=0)
     picked = dot(hot[...], sources).astype(BF16)
     total = jnp.zeros(out_ref.shape, F32)
     for n in range(slots):
@@ -278,7 +283,7 @@
             pltpu.VMEM((slots, parents), I32),
             pltpu.VMEM((slots, parents), I32),
             pltpu.VMEM(shift_angle.shape, F32),
-            pltpu.VMEM((2 * translation.shape[0], translation.shape[2]), F32),
+            pltpu.VMEM((640, translation.shape[2]), F32),
             pltpu.VMEM((near_slots, leaves), I32),
             pltpu.VMEM((384, 256), BF16),
             pltpu.SemaphoreType.DMA((5,)),
@@ -325,7 +330,7 @@
         [whole()] * 4 + [whole(pltpu.HBM), whole(pl.ANY)],
         [
             pltpu.VMEM(near_matrix.shape, BF16),
-            pltpu.VMEM((near_slots * leaves, 3 * leaves), BF16),
+            pltpu.VMEM((near_slots * leaves, 4 * leaves), BF16),
             pltpu.SemaphoreType.DMA((near_slots,)),
         ],
         24,

time: 39.1 us -> 39.1 us (level)
  no operation moved by 1% of the time
where the time goes in v10:
time: 39.1 us; the launch traced here: 38.8 us
  starting transfers between devices  18.2 us (47%)
  Pallas kernels  18.2 us (47%)
  waiting for transfers between devices  1.77 us (5%)
  local copies, waits for them, and re-layouts  0.57 us (1%)
    pallas_call x5, Pallas kernels, call(): pl.pallas_call(body, out_shape=out, in_specs=specs, out_specs=jax.tree.ma...  18.2 us
    all_to_all x1, starting transfers between devices, on_device(): upper = lax.all_to_all(up, 'dir', split_axis=0, concat_axis=0, tiled=True)  7.55 us
    all_to_all x1, starting transfers between devices, on_device(): lax.all_to_all(local, 'dir', split_axis=0, concat_axis=0, tiled=True)  5.79 us
    ppermute x1, starting transfers between devices, on_device(): from_cross = lax.ppermute(relay, BOTH, cross)  3.11 us
    all_to_all x1, waiting for transfers between devices, on_device(): upper = lax.all_to_all(up, 'dir', split_axis=0, concat_axis=0, tiled=True)  1.76 us
    ppermute x1, starting transfers between devices, on_device(): lax.ppermute(currents, BOTH, [(i, halo_target(i, boxes, dirs)) for i in r...  1.39 us
  transfers between devices with their start and end apart: 5, of which 1 were waited for; matrix products, arithmetic and copies ran while one was open for 0% of the time, Pallas kernels for 27%

profile of v10, /device:TPU:27, one launch (start us, length us, event | category | flops | bytes accessed | tf_op | source)
XLA Modules:
  0.0 38.8 jit_solution(164881890521705007)
XLA Ops:
  0.0 1.4 %collective-permute-start = (bf16[64,512]{1,0:T(8,128)(2,1)}, bf16[64,512]{1,0:T(8,128)(2,1)S(1)}, u32[]{:S(2)}, u32[]{:S(2)}) collective-permute-start(bf16[64,512]{1,0:T(8,128)(2,1)} %own_ref.3), channel_id=1, source_target_pairs={{0,12},{1,13},{2,14},{3,15},{4,8},{5,9},{6,10},{7,11},{8,26},{9,27... | collective-permute-start | bytes 196616 | tf_op jit(solution)/shard_map/ppermute | solution.py:258
  1.4 0.1 pad_add_fusion.place_ref
  1.5 0.0 copy-start
  1.5 0.0 copy-start.1
  1.5 0.0 copy-start.3
  1.5 3.2 %shard_map.100 = (bf16[20,128,256]{2,1,0:T(8,128)(2,1)S(1)}, s32[128,32]{1,0:T(8,128)S(1)}, s32[64,32]{1,0:T(8,128)S(1)}, f32[8,2048]{1,0:T(8,128)S(1)}, f32[8,2048]{1,0:T(8,128)S(1)}) custom-call(s32[2]{0:T(128)S(1)} %pad_add_fusion.place_ref, s32[20,1024]{1,0:T(8,128)} %bitcast.7, s32[20,1024]{1,0:T(8,128)} %bitcast.8, f32[8,2048]{1,0:T(8,128)} %angle_hbm.1, ...), custom_call_target="tpu_custom_call" | custom-call | flops 5000000000 | bytes 11534336 | tf_op jit(solution)/shard_map/pallas_call | solution.py:22
  4.7 0.0 collective-permute-done.far_ref
  4.7 0.3 copy-done
  5.0 0.2 copy-done.1
  5.3 0.0 copy-done.3
  5.3 2.8 %shard_map.101 = (bf16[16,32,128]{2,1,0:T(8,128)(2,1)}, bf16[64,512]{1,0:T(8,128)(2,1)S(1)}, bf16[1024,768]{1,0:T(8,128)(2,1)S(1)}) custom-call(bf16[64,512]{1,0:T(8,128)(2,1)S(1)} %copy-done.3, bf16[64,512]{1,0:T(8,128)(2,1)S(1)} %collective-permute-done.far_ref, bf16[512,1024]{1,0:T(8,128)(2,1)S(1)} %copy-done.1, f32[8,2048]{1,0:T(8,128)S(1)} %get-tuple-element.13.cos_ref, ...), custom_call_target="tpu_custom_call" | custom-call | flops 1207959552 | bytes 10485760 | tf_op jit(solution)/shard_map/pallas_call | solution.py:22
  8.1 7.5 %all-to-all-start = ((bf16[16,32,128]{2,1,0:T(8,128)(2,1)}), bf16[16,32,128]{2,1,0:T(8,128)(2,1)S(1)}, u32[]{:S(2)}, u32[]{:S(2)}) async-start(bf16[16,32,128]{2,1,0:T(8,128)(2,1)} %get-tuple-element.15), calls=%async_computation | async-start | bytes 262144 | tf_op jit(solution)/shard_map/all_to_all | solution.py:310
  15.6 0.4 collective-permute-start.1
  16.0 3.1 %collective-permute-start.2 = (bf16[64,512]{1,0:T(8,128)(2,1)S(1)}, bf16[64,512]{1,0:T(8,128)(2,1)S(1)}, u32[]{:S(2)}, u32[]{:S(2)}) collective-permute-start(bf16[64,512]{1,0:T(8,128)(2,1)S(1)} %get-tuple-element.18), channel_id=1, source_target_pairs={{0,0},{1,2},{2,1},{3,4},{4,3},{5,6},{6,5},{7,8},{8,7},{9,10},{10,9... | collective-permute-start | bytes 196616 | tf_op jit(solution)/shard_map/ppermute | solution.py:313
  19.1 1.8 %all-to-all-done.upper_ref = bf16[16,32,128]{2,1,0:T(8,128)(2,1)S(1)} async-done(((bf16[16,32,128]{2,1,0:T(8,128)(2,1)}), bf16[16,32,128]{2,1,0:T(8,128)(2,1)S(1)}, u32[]{:S(2)}, u32[]{:S(2)}) %all-to-all-start) | async-done | bytes 131104 | tf_op jit(solution)/shard_map/all_to_all | solution.py:310
  20.9 1.4 %shard_map.102._ = bf16[16,16,128]{2,1,0:T(8,128)(2,1)} custom-call(bf16[16,32,128]{2,1,0:T(8,128)(2,1)S(1)} %all-to-all-done.upper_ref, s32[128,32]{1,0:T(8,128)S(1)} %get-tuple-element.16.index_ref, bf16[20,128,256]{2,1,0:T(8,128)(2,1)S(1)} %get-tuple-element.17.operator_ref), custom_call_target="tpu_custom_call" | custom-call | flops 335544320 | bytes 2097152 | tf_op jit(solution)/shard_map/pallas_call | solution.py:22
  22.3 0.0 copy-start.2
  22.3 5.8 %all-to-all-start.1 = ((bf16[16,16,128]{2,1,0:T(8,128)(2,1)}), bf16[16,16,128]{2,1,0:T(8,128)(2,1)S(1)}, u32[]{:S(2)}, u32[]{:S(2)}) async-start(bf16[16,16,128]{2,1,0:T(8,128)(2,1)} %shard_map.102._), calls=%async_computation.1 | async-start | bytes 131072 | tf_op jit(solution)/shard_map/all_to_all | solution.py:324
  28.1 0.0 collective-permute-done.1.sibling_ref
  28.1 0.0 collective-permute-done.2.cross_ref
  28.1 5.8 %shard_map.103.near_ref = f32[64,512]{1,0:T(8,128)S(1)} custom-call(bf16[64,512]{1,0:T(8,128)(2,1)S(1)} %copy-done.3, bf16[64,512]{1,0:T(8,128)(2,1)S(1)} %collective-permute-done.1.sibling_ref, bf16[64,512]{1,0:T(8,128)(2,1)S(1)} %collective-permute-done.2.cross_ref, s32[64,32]{1,0:T(8,128)S(1)} %get-tuple-element.19.col_ref, ...), custom_call_target="tpu_custom_call" | custom-call | flops 1132462080 | bytes 15728640 | tf_op jit(solution)/shard_map/pallas_call | solution.py:22
  34.0 0.0 all-to-all-done.1.inc_ref
  34.0 0.0 copy-done.2
  34.0 4.8 %shard_map.104 = f32[64,512]{1,0:T(8,128)} custom-call(bf16[16,16,128]{2,1,0:T(8,128)(2,1)S(1)} %all-to-all-done.1.inc_ref, f32[8,2048]{1,0:T(8,128)S(1)} %get-tuple-element.13.cos_ref, f32[8,2048]{1,0:T(8,128)S(1)} %get-tuple-element.14.sin_ref, f32[64,512]{1,0:T(8,128)S(1)} %shard_map.103.near_ref, bf16[1024,512]{1,0:T(8,128)(2,1)S(1)} %copy-done.2, ...), custom_call_target="tpu_custom_call" | custom-call | flops 805306368 | bytes 10485760 | tf_op jit(solution)/shard_map/pallas_call | solution.py:22
Async XLA Ops:
  0.0 4.7 %collective-permute-start = (bf16[64,512]{1,0:T(8,128)(2,1)}, bf16[64,512]{1,0:T(8,128)(2,1)S(1)}, u32[]{:S(2)}, u32[]{:S(2)}) collective-permute-start(bf16[64,512]{1,0:T(8,128)(2,1)} %own_ref.3), channel_id=1, source_target_pairs={{0,12},{1,13},{2,14},{3,15},{4,8},{5,9},{6,10},{7,11},{8,26},{9,27... | collective-permute-start | bytes 196616 | tf_op jit(solution)/shard_map/ppermute | solution.py:258
  1.5 3.6 %copy-start = (bf16[1024,4096]{1,0:T(8,128)(2,1)S(1)}, bf16[1024,4096]{1,0:T(8,128)(2,1)}, u32[]{:S(2)}) copy-start(bf16[1024,4096]{1,0:T(8,128)(2,1)} %interp.3) | copy-start | bytes 25165828
  1.5 3.8 %copy-start.1 = (bf16[512,1024]{1,0:T(8,128)(2,1)S(1)}, bf16[512,1024]{1,0:T(8,128)(2,1)}, u32[]{:S(2)}) copy-start(bf16[512,1024]{1,0:T(8,128)(2,1)} %agg_ref.1) | copy-start | bytes 3145732
  1.5 3.8 %copy-start.3 = (bf16[64,512]{1,0:T(8,128)(2,1)S(1)}, bf16[64,512]{1,0:T(8,128)(2,1)}, u32[]{:S(2)}) copy-start(bf16[64,512]{1,0:T(8,128)(2,1)} %own_ref.3) | copy-start | bytes 196612
  8.1 12.8 %all-to-all-start = ((bf16[16,32,128]{2,1,0:T(8,128)(2,1)}), bf16[16,32,128]{2,1,0:T(8,128)(2,1)S(1)}, u32[]{:S(2)}, u32[]{:S(2)}) async-start(bf16[16,32,128]{2,1,0:T(8,128)(2,1)} %get-tuple-element.15), calls=%async_computation | async-start | bytes 262144 | tf_op jit(solution)/shard_map/all_to_all | solution.py:310
  15.6 12.5 %collective-permute-start.1 = (bf16[64,512]{1,0:T(8,128)(2,1)S(1)}, bf16[64,512]{1,0:T(8,128)(2,1)S(1)}, u32[]{:S(2)}, u32[]{:S(2)}) collective-permute-start(bf16[64,512]{1,0:T(8,128)(2,1)S(1)} %copy-done.3), channel_id=1, source_target_pairs={{0,1},{1,0},{2,3},{3,2},{4,5},{5,4},{6,7},{7,6},{8,9},{9,8},{10,11... | collective-permute-start | bytes 196616 | tf_op jit(solution)/shard_map/ppermute | solution.py:259
  16.0 12.1 %collective-permute-start.2 = (bf16[64,512]{1,0:T(8,128)(2,1)S(1)}, bf16[64,512]{1,0:T(8,128)(2,1)S(1)}, u32[]{:S(2)}, u32[]{:S(2)}) collective-permute-start(bf16[64,512]{1,0:T(8,128)(2,1)S(1)} %get-tuple-element.18), channel_id=1, source_target_pairs={{0,0},{1,2},{2,1},{3,4},{4,3},{5,6},{6,5},{7,8},{8,7},{9,10},{10,9... | collective-permute-start | bytes 196616 | tf_op jit(solution)/shard_map/ppermute | solution.py:313
  22.3 11.7 %copy-start.2 = (bf16[1024,512]{1,0:T(8,128)(2,1)S(1)}, bf16[1024,512]{1,0:T(8,128)(2,1)}, u32[]{:S(2)}) copy-start(bf16[1024,512]{1,0:T(8,128)(2,1)} %receive_ref.1) | copy-start | bytes 3145732
  22.3 11.7 %all-to-all-start.1 = ((bf16[16,16,128]{2,1,0:T(8,128)(2,1)}), bf16[16,16,128]{2,1,0:T(8,128)(2,1)S(1)}, u32[]{:S(2)}, u32[]{:S(2)}) async-start(bf16[16,16,128]{2,1,0:T(8,128)(2,1)} %shard_map.102._), calls=%async_computation.1 | async-start | bytes 131072 | tf_op jit(solution)/shard_map/all_to_all | solution.py:324

commit v11 on v10

--- a/solution.py
+++ b/solution.py
@@ -10,7 +10,7 @@
 BF16, F32, I32 = jnp.bfloat16, jnp.float32, jnp.int32
 BOTH = ("box", "dir")
 VMEM = pltpu.VMEM
-KEPT = 3
+KEPT = 2
 AHEAD = 5 * 10**9
 
 
@@ -156,28 +156,32 @@
         ],
         axis=1,
     )
-    lane = lax.broadcasted_iota(I32, (rows, sources), 1)
+    lane = lax.broadcasted_iota(I32, (rows, sources), 1).astype(BF16)
+    index = index_ref[...].astype(BF16)
+    one, zero = jnp.ones((), BF16), jnp.zeros((), BF16)
     acc_re = jnp.zeros((rows, 128), F32)
     acc_im = jnp.zeros((rows, 128), F32)
-    for j in range(slots):
-        hot = jnp.where(lane == index_ref[:, j : j + 1], 1.0, 0.0).astype(BF16)
-        x = dot(hot, field)
-        op = operator_ref[j].astype(F32)
-        xr, xi = x[:, :128], x[:, 128:]
-        tr, ti = op[:, :128], op[:, 128:]
-        acc_re += tr * xr - ti * xi
-        acc_im += tr * xi + ti * xr
+    for first in range(0, slots, 4):
+        hot = [jnp.where(lane == index[:, j : j + 1], one, zero) for j in range(first, first + 4)]
+        picked = dot(jnp.concatenate(hot, axis=0), field)
+        for k in range(4):
+            x = picked[k * rows : (k + 1) * rows]
+            op = operator_ref[first + k].astype(F32)
+            xr, xi = x[:, :128], x[:, 128:]
+            tr, ti = op[:, :128], op[:, 128:]
+            acc_re += tr * xr - ti * xi
+            acc_im += tr * xi + ti * xr
     blocks = out_ref.shape[0]
     out_ref[:, 0:8, :] = acc_re.reshape(blocks, 8, 128).astype(BF16)
     out_ref[:, 8:16, :] = acc_im.reshape(blocks, 8, 128).astype(BF16)
 
 
-def down_kernel(inc_ref, cos_ref, sin_ref, near_ref, receive_ref, kept, interp, out_ref, buf, received, sems):
+def down_kernel(inc_ref, cos_ref, sin_ref, near_ref, receive_ref, kept, more, interp, out_ref, buf, received, sems):
     width = 256
     chunks = buf.shape[1] // width
     copies = []
     for j in range(chunks):
-        source = interp.at[:, pl.ds((KEPT + j) * width, width)]
+        source = interp.at[:, pl.ds((KEPT + 1 + j) * width, width)]
         target = buf.at[:, pl.ds(j * width, width)]
         copies.append(pltpu.make_async_copy(source, target, sems.at[j]))
     for copy in copies:
@@ -196,19 +200,26 @@
             (im * cosine - re * sine).reshape(leaves, 128).astype(BF16)
         )
     back = dot(received[:, : KEPT * width], kept[...], 1, 1)
+    back += dot(received[:, KEPT * width : (KEPT + 1) * width], more[...], 1, 1)
     for j in range(chunks):
-        at = (KEPT + j) * width
+        at = (KEPT + 1 + j) * width
         copies[j].wait()
         back += dot(received[:, at : at + width], buf[:, j * width : (j + 1) * width], 1, 1)
     out_ref[...] = near_ref[...] + dot(back.astype(BF16), receive_ref[...])
 
 
-def near_kernel(own_ref, sibling_ref, cross_ref, col_ref, near_hbm, _, out_ref, buf, hot, sems):
+def near_kernel(
+    own_ref, sibling_ref, cross_ref, col_ref, near_hbm, interp, _, out_ref, more, buf, hot, sems
+):
     slots = near_hbm.shape[0]
     copies = []
     for n in range(slots):
         copies.append(pltpu.make_async_copy(near_hbm.at[n], buf.at[n], sems.at[n]))
         copies[n].start()
+    extra = pltpu.make_async_copy(
+        interp.at[:, pl.ds(KEPT * 256, more.shape[1])], more, sems.at[slots]
+    )
+    extra.start()
     rows = out_ref.shape[0]
     lane = lax.broadcasted_iota(I32, (rows, 4 * rows), 1)
     for n in range(slots):
@@ -223,6 +234,7 @@
         copies[n].wait()
         total += dot(picked[n * rows : (n + 1) * rows], buf[n])
     out_ref[...] = total
+    extra.wait()
 
 
 def halo_target(i, boxes, dirs):
@@ -323,15 +335,18 @@
     )
     incoming = lax.all_to_all(local, "dir", split_axis=0, concat_axis=0, tiled=True)
 
-    near = call(
+    near, more = call(
         near_kernel,
-        jax.ShapeDtypeStruct((leaves, width), F32),
-        (currents, from_sibling, from_cross, column, *in_hbm(near_matrix), local),
-        [whole()] * 4 + [whole(pltpu.HBM), whole(pl.ANY)],
+        (
+            jax.ShapeDtypeStruct((leaves, width), F32),
+            pltpu.VMEM((interp.shape[0], 256), BF16),
+        ),
+        (currents, from_sibling, from_cross, column, *in_hbm(near_matrix, interp), local),
+        [whole()] * 4 + [whole(pltpu.HBM)] * 2 + [whole(pl.ANY)],
         [
             pltpu.VMEM(near_matrix.shape, BF16),
             pltpu.VMEM((near_slots * leaves, 4 * leaves), BF16),
-            pltpu.SemaphoreType.DMA((near_slots,)),
+            pltpu.SemaphoreType.DMA((near_slots + 1,)),
         ],
         24,
         2 * leaves * 27 * 512 * 640,
@@ -341,10 +356,10 @@
     return call(
         down_kernel,
         jax.ShapeDtypeStruct((leaves, width), F32),
-        (incoming, cosine, sine, near, in_vmem(receive), in_vmem(kept), *in_hbm(interp)),
-        [whole()] * 6 + [whole(pltpu.HBM)],
+        (incoming, cosine, sine, near, in_vmem(receive), in_vmem(kept), in_vmem(more), *in_hbm(interp)),
+        [whole()] * 7 + [whole(pltpu.HBM)],
         [
-            pltpu.VMEM((interp.shape[0], interp.shape[1] - KEPT * 256), BF16),
+            pltpu.VMEM((interp.shape[0], interp.shape[1] - (KEPT + 1) * 256), BF16),
             pltpu.VMEM((leaves, interp.shape[1]), BF16),
             pltpu.SemaphoreType.DMA((interp.shape[1] // 256,)),
         ],

time: 39.1 us -> 38.7 us (0.990)
  no operation moved by 1% of the time
where the time goes in v11:
time: 38.7 us; the launch traced here: 38.4 us
  starting transfers between devices  18.1 us (47%)
  Pallas kernels  17.9 us (46%)
  waiting for transfers between devices  1.77 us (5%)
  local copies, waits for them, and re-layouts  0.57 us (1%)
    pallas_call x5, Pallas kernels, call(): pl.pallas_call(body, out_shape=out, in_specs=specs, out_specs=jax.tree.ma...  17.9 us
    all_to_all x1, starting transfers between devices, on_device(): upper = lax.all_to_all(up, 'dir', split_axis=0, concat_axis=0, tiled=True)  7.53 us
    all_to_all x1, starting transfers between devices, on_device(): lax.all_to_all(local, 'dir', split_axis=0, concat_axis=0, tiled=True)  5.65 us
    ppermute x1, starting transfers between devices, on_device(): from_cross = lax.ppermute(relay, BOTH, cross)  3.11 us
    all_to_all x1, waiting for transfers between devices, on_device(): upper = lax.all_to_all(up, 'dir', split_axis=0, concat_axis=0, tiled=True)  1.76 us
    ppermute x1, starting transfers between devices, on_device(): lax.ppermute(currents, BOTH, [(i, halo_target(i, boxes, dirs)) for i in r...  1.39 us
  transfers between devices with their start and end apart: 5, of which 1 were waited for; matrix products, arithmetic and copies ran while one was open for 0% of the time, Pallas kernels for 27%

profile of v11, /device:TPU:27, one launch (start us, length us, event | category | flops | bytes accessed | tf_op | source)
XLA Modules:
  0.0 38.4 jit_solution(9943309324434390504)
XLA Ops:
  0.0 1.4 %collective-permute-start = (bf16[64,512]{1,0:T(8,128)(2,1)}, bf16[64,512]{1,0:T(8,128)(2,1)S(1)}, u32[]{:S(2)}, u32[]{:S(2)}) collective-permute-start(bf16[64,512]{1,0:T(8,128)(2,1)} %own_ref.3), channel_id=1, source_target_pairs={{0,12},{1,13},{2,14},{3,15},{4,8},{5,9},{6,10},{7,11},{8,26},{9,27... | collective-permute-start | bytes 196616 | tf_op jit(solution)/shard_map/ppermute | solution.py:270
  1.4 0.1 pad_add_fusion.place_ref
  1.5 0.0 copy-start
  1.5 0.0 copy-start.1
  1.5 0.0 copy-start.3
  1.5 3.2 %shard_map.100 = (bf16[20,128,256]{2,1,0:T(8,128)(2,1)S(1)}, s32[128,32]{1,0:T(8,128)S(1)}, s32[64,32]{1,0:T(8,128)S(1)}, f32[8,2048]{1,0:T(8,128)S(1)}, f32[8,2048]{1,0:T(8,128)S(1)}) custom-call(s32[2]{0:T(128)S(1)} %pad_add_fusion.place_ref, s32[20,1024]{1,0:T(8,128)} %bitcast.7, s32[20,1024]{1,0:T(8,128)} %bitcast.8, f32[8,2048]{1,0:T(8,128)} %angle_hbm.1, ...), custom_call_target="tpu_custom_call" | custom-call | flops 5000000000 | bytes 11534336 | tf_op jit(solution)/shard_map/pallas_call | solution.py:22
  4.7 0.0 collective-permute-done.far_ref
  4.7 0.3 copy-done
  5.0 0.2 copy-done.1
  5.3 0.0 copy-done.3
  5.3 2.8 %shard_map.101 = (bf16[16,32,128]{2,1,0:T(8,128)(2,1)}, bf16[64,512]{1,0:T(8,128)(2,1)S(1)}, bf16[1024,512]{1,0:T(8,128)(2,1)S(1)}) custom-call(bf16[64,512]{1,0:T(8,128)(2,1)S(1)} %copy-done.3, bf16[64,512]{1,0:T(8,128)(2,1)S(1)} %collective-permute-done.far_ref, bf16[512,1024]{1,0:T(8,128)(2,1)S(1)} %copy-done.1, f32[8,2048]{1,0:T(8,128)S(1)} %get-tuple-element.15.cos_ref, ...), custom_call_target="tpu_custom_call" | custom-call | flops 1207959552 | bytes 10485760 | tf_op jit(solution)/shard_map/pallas_call | solution.py:22
  8.0 7.5 %all-to-all-start = ((bf16[16,32,128]{2,1,0:T(8,128)(2,1)}), bf16[16,32,128]{2,1,0:T(8,128)(2,1)S(1)}, u32[]{:S(2)}, u32[]{:S(2)}) async-start(bf16[16,32,128]{2,1,0:T(8,128)(2,1)} %get-tuple-element.17), calls=%async_computation | async-start | bytes 262144 | tf_op jit(solution)/shard_map/all_to_all | solution.py:322
  15.6 0.4 collective-permute-start.1
  15.9 3.1 %collective-permute-start.2 = (bf16[64,512]{1,0:T(8,128)(2,1)S(1)}, bf16[64,512]{1,0:T(8,128)(2,1)S(1)}, u32[]{:S(2)}, u32[]{:S(2)}) collective-permute-start(bf16[64,512]{1,0:T(8,128)(2,1)S(1)} %get-tuple-element.20), channel_id=1, source_target_pairs={{0,0},{1,2},{2,1},{3,4},{4,3},{5,6},{6,5},{7,8},{8,7},{9,10},{10,9... | collective-permute-start | bytes 196616 | tf_op jit(solution)/shard_map/ppermute | solution.py:325
  19.1 1.8 %all-to-all-done.upper_ref = bf16[16,32,128]{2,1,0:T(8,128)(2,1)S(1)} async-done(((bf16[16,32,128]{2,1,0:T(8,128)(2,1)}), bf16[16,32,128]{2,1,0:T(8,128)(2,1)S(1)}, u32[]{:S(2)}, u32[]{:S(2)}) %all-to-all-start) | async-done | bytes 131104 | tf_op jit(solution)/shard_map/all_to_all | solution.py:322
  20.8 1.4 %shard_map.102._ = bf16[16,16,128]{2,1,0:T(8,128)(2,1)} custom-call(bf16[16,32,128]{2,1,0:T(8,128)(2,1)S(1)} %all-to-all-done.upper_ref, s32[128,32]{1,0:T(8,128)S(1)} %get-tuple-element.18.index_ref, bf16[20,128,256]{2,1,0:T(8,128)(2,1)S(1)} %get-tuple-element.19.operator_ref), custom_call_target="tpu_custom_call" | custom-call | flops 335544320 | bytes 2097152 | tf_op jit(solution)/shard_map/pallas_call | solution.py:22
  22.2 5.7 %all-to-all-start.1 = ((bf16[16,16,128]{2,1,0:T(8,128)(2,1)}), bf16[16,16,128]{2,1,0:T(8,128)(2,1)S(1)}, u32[]{:S(2)}, u32[]{:S(2)}) async-start(bf16[16,16,128]{2,1,0:T(8,128)(2,1)} %shard_map.102._), calls=%async_computation.1 | async-start | bytes 131072 | tf_op jit(solution)/shard_map/all_to_all | solution.py:336
  27.8 0.0 collective-permute-done.1.sibling_ref
  27.8 0.0 collective-permute-done.2.cross_ref
  27.9 0.0 copy-start.2
  27.9 5.9 %shard_map.103 = (f32[64,512]{1,0:T(8,128)S(1)}, bf16[1024,256]{1,0:T(8,128)(2,1)S(1)}) custom-call(bf16[64,512]{1,0:T(8,128)(2,1)S(1)} %copy-done.3, bf16[64,512]{1,0:T(8,128)(2,1)S(1)} %collective-permute-done.1.sibling_ref, bf16[64,512]{1,0:T(8,128)(2,1)S(1)} %collective-permute-done.2.cross_ref, s32[64,32]{1,0:T(8,128)S(1)} %get-tuple-element.21.col_ref, ...), custom_call_target="tpu_custom_call" | custom-call | flops 1132462080 | bytes 15728640 | tf_op jit(solution)/shard_map/pallas_call | solution.py:22
  33.7 0.0 all-to-all-done.1.inc_ref
  33.7 0.0 copy-done.2
  33.8 4.7 %shard_map.104 = f32[64,512]{1,0:T(8,128)} custom-call(bf16[16,16,128]{2,1,0:T(8,128)(2,1)S(1)} %all-to-all-done.1.inc_ref, f32[8,2048]{1,0:T(8,128)S(1)} %get-tuple-element.15.cos_ref, f32[8,2048]{1,0:T(8,128)S(1)} %get-tuple-element.16.sin_ref, f32[64,512]{1,0:T(8,128)S(1)} %get-tuple-element.22.near_ref, bf16[1024,512]{1,0:T(8,128)(2,1)S(1)} %copy-done.2, ...), custom_call_target="tpu_custom_call" | custom-call | flops 805306368 | bytes 10485760 | tf_op jit(solution)/shard_map/pallas_call | solution.py:22
Async XLA Ops:
  0.0 4.7 %collective-permute-start = (bf16[64,512]{1,0:T(8,128)(2,1)}, bf16[64,512]{1,0:T(8,128)(2,1)S(1)}, u32[]{:S(2)}, u32[]{:S(2)}) collective-permute-start(bf16[64,512]{1,0:T(8,128)(2,1)} %own_ref.3), channel_id=1, source_target_pairs={{0,12},{1,13},{2,14},{3,15},{4,8},{5,9},{6,10},{7,11},{8,26},{9,27... | collective-permute-start | bytes 196616 | tf_op jit(solution)/shard_map/ppermute | solution.py:270
  1.5 3.6 %copy-start = (bf16[1024,4096]{1,0:T(8,128)(2,1)S(1)}, bf16[1024,4096]{1,0:T(8,128)(2,1)}, u32[]{:S(2)}) copy-start(bf16[1024,4096]{1,0:T(8,128)(2,1)} %interp.5) | copy-start | bytes 25165828
  1.5 3.8 %copy-start.1 = (bf16[512,1024]{1,0:T(8,128)(2,1)S(1)}, bf16[512,1024]{1,0:T(8,128)(2,1)}, u32[]{:S(2)}) copy-start(bf16[512,1024]{1,0:T(8,128)(2,1)} %agg_ref.1) | copy-start | bytes 3145732
  1.5 3.8 %copy-start.3 = (bf16[64,512]{1,0:T(8,128)(2,1)S(1)}, bf16[64,512]{1,0:T(8,128)(2,1)}, u32[]{:S(2)}) copy-start(bf16[64,512]{1,0:T(8,128)(2,1)} %own_ref.3) | copy-start | bytes 196612
  8.0 12.8 %all-to-all-start = ((bf16[16,32,128]{2,1,0:T(8,128)(2,1)}), bf16[16,32,128]{2,1,0:T(8,128)(2,1)S(1)}, u32[]{:S(2)}, u32[]{:S(2)}) async-start(bf16[16,32,128]{2,1,0:T(8,128)(2,1)} %get-tuple-element.17), calls=%async_computation | async-start | bytes 262144 | tf_op jit(solution)/shard_map/all_to_all | solution.py:322
  15.6 12.3 %collective-permute-start.1 = (bf16[64,512]{1,0:T(8,128)(2,1)S(1)}, bf16[64,512]{1,0:T(8,128)(2,1)S(1)}, u32[]{:S(2)}, u32[]{:S(2)}) collective-permute-start(bf16[64,512]{1,0:T(8,128)(2,1)S(1)} %copy-done.3), channel_id=1, source_target_pairs={{0,1},{1,0},{2,3},{3,2},{4,5},{5,4},{6,7},{7,6},{8,9},{9,8},{10,11... | collective-permute-start | bytes 196616 | tf_op jit(solution)/shard_map/ppermute | solution.py:271
  15.9 11.9 %collective-permute-start.2 = (bf16[64,512]{1,0:T(8,128)(2,1)S(1)}, bf16[64,512]{1,0:T(8,128)(2,1)S(1)}, u32[]{:S(2)}, u32[]{:S(2)}) collective-permute-start(bf16[64,512]{1,0:T(8,128)(2,1)S(1)} %get-tuple-element.20), channel_id=1, source_target_pairs={{0,0},{1,2},{2,1},{3,4},{4,3},{5,6},{6,5},{7,8},{8,7},{9,10},{10,9... | collective-permute-start | bytes 196616 | tf_op jit(solution)/shard_map/ppermute | solution.py:325
  22.2 11.5 %all-to-all-start.1 = ((bf16[16,16,128]{2,1,0:T(8,128)(2,1)}), bf16[16,16,128]{2,1,0:T(8,128)(2,1)S(1)}, u32[]{:S(2)}, u32[]{:S(2)}) async-start(bf16[16,16,128]{2,1,0:T(8,128)(2,1)} %shard_map.102._), calls=%async_computation.1 | async-start | bytes 131072 | tf_op jit(solution)/shard_map/all_to_all | solution.py:336
  27.9 5.9 %copy-start.2 = (bf16[1024,512]{1,0:T(8,128)(2,1)S(1)}, bf16[1024,512]{1,0:T(8,128)(2,1)}, u32[]{:S(2)}) copy-start(bf16[1024,512]{1,0:T(8,128)(2,1)} %receive_ref.1) | copy-start | bytes 3145732

commit v12 on v11

--- a/solution.py
+++ b/solution.py
@@ -10,7 +10,8 @@
 BF16, F32, I32 = jnp.bfloat16, jnp.float32, jnp.int32
 BOTH = ("box", "dir")
 VMEM = pltpu.VMEM
-KEPT = 2
+MORE = 2
+KEPT = 1
 AHEAD = 5 * 10**9
 
 
@@ -181,7 +182,7 @@
     chunks = buf.shape[1] // width
     copies = []
     for j in range(chunks):
-        source = interp.at[:, pl.ds((KEPT + 1 + j) * width, width)]
+        source = interp.at[:, pl.ds((KEPT + MORE + j) * width, width)]
         target = buf.at[:, pl.ds(j * width, width)]
         copies.append(pltpu.make_async_copy(source, target, sems.at[j]))
     for copy in copies:
@@ -200,9 +201,9 @@
             (im * cosine - re * sine).reshape(leaves, 128).astype(BF16)
         )
     back = dot(received[:, : KEPT * width], kept[...], 1, 1)
-    back += dot(received[:, KEPT * width : (KEPT + 1) * width], more[...], 1, 1)
+    back += dot(received[:, KEPT * width : (KEPT + MORE) * width], more[...], 1, 1)
     for j in range(chunks):
-        at = (KEPT + 1 + j) * width
+        at = (KEPT + MORE + j) * width
         copies[j].wait()
         back += dot(received[:, at : at + width], buf[:, j * width : (j + 1) * width], 1, 1)
     out_ref[...] = near_ref[...] + dot(back.astype(BF16), receive_ref[...])
@@ -339,7 +340,7 @@
         near_kernel,
         (
             jax.ShapeDtypeStruct((leaves, width), F32),
-            pltpu.VMEM((interp.shape[0], 256), BF16),
+            pltpu.VMEM((interp.shape[0], MORE * 256), BF16),
         ),
         (currents, from_sibling, from_cross, column, *in_hbm(near_matrix, interp), local),
         [whole()] * 4 + [whole(pltpu.HBM)] * 2 + [whole(pl.ANY)],
@@ -359,7 +360,7 @@
         (incoming, cosine, sine, near, in_vmem(receive), in_vmem(kept), in_vmem(more), *in_hbm(interp)),
         [whole()] * 7 + [whole(pltpu.HBM)],
         [
-            pltpu.VMEM((interp.shape[0], interp.shape[1] - (KEPT + 1) * 256), BF16),
+            pltpu.VMEM((interp.shape[0], interp.shape[1] - (KEPT + MORE) * 256), BF16),
             pltpu.VMEM((leaves, interp.shape[1]), BF16),
             pltpu.SemaphoreType.DMA((interp.shape[1] // 256,)),
         ],

time: 38.7 us -> 38.8 us (level)
  no operation moved by 1% of the time
where the time goes in v12:
time: 38.8 us; the launch traced here: 38.6 us
  starting transfers between devices  18.1 us (47%)
  Pallas kernels  18 us (46%)
  waiting for transfers between devices  1.77 us (5%)
  local copies, waits for them, and re-layouts  0.57 us (1%)
    pallas_call x5, Pallas kernels, call(): pl.pallas_call(body, out_shape=out, in_specs=specs, out_specs=jax.tree.ma...  18 us
    all_to_all x1, starting transfers between devices, on_device(): upper = lax.all_to_all(up, 'dir', split_axis=0, concat_axis=0, tiled=True)  7.57 us
    all_to_all x1, starting transfers between devices, on_device(): lax.all_to_all(local, 'dir', split_axis=0, concat_axis=0, tiled=True)  5.65 us
    ppermute x1, starting transfers between devices, on_device(): from_cross = lax.ppermute(relay, BOTH, cross)  3.11 us
    all_to_all x1, waiting for transfers between devices, on_device(): upper = lax.all_to_all(up, 'dir', split_axis=0, concat_axis=0, tiled=True)  1.76 us
    ppermute x1, starting transfers between devices, on_device(): lax.ppermute(currents, BOTH, [(i, halo_target(i, boxes, dirs)) for i in r...  1.39 us
  transfers between devices with their start and end apart: 5, of which 1 were waited for; matrix products, arithmetic and copies ran while one was open for 0% of the time, Pallas kernels for 27%

profile of v12, /device:TPU:27, one launch (start us, length us, event | category | flops | bytes accessed | tf_op | source)
XLA Modules:
  0.0 38.6 jit_solution(11279720312792880233)
XLA Ops:
  0.0 1.4 %collective-permute-start = (bf16[64,512]{1,0:T(8,128)(2,1)}, bf16[64,512]{1,0:T(8,128)(2,1)S(1)}, u32[]{:S(2)}, u32[]{:S(2)}) collective-permute-start(bf16[64,512]{1,0:T(8,128)(2,1)} %own_ref.3), channel_id=1, source_target_pairs={{0,12},{1,13},{2,14},{3,15},{4,8},{5,9},{6,10},{7,11},{8,26},{9,27... | collective-permute-start | bytes 196616 | tf_op jit(solution)/shard_map/ppermute | solution.py:271
  1.4 0.1 pad_add_fusion.place_ref
  1.5 0.0 copy-start
  1.5 0.0 copy-start.1
  1.5 0.0 copy-start.3
  1.5 3.2 %shard_map.100 = (bf16[20,128,256]{2,1,0:T(8,128)(2,1)S(1)}, s32[128,32]{1,0:T(8,128)S(1)}, s32[64,32]{1,0:T(8,128)S(1)}, f32[8,2048]{1,0:T(8,128)S(1)}, f32[8,2048]{1,0:T(8,128)S(1)}) custom-call(s32[2]{0:T(128)S(1)} %pad_add_fusion.place_ref, s32[20,1024]{1,0:T(8,128)} %bitcast.7, s32[20,1024]{1,0:T(8,128)} %bitcast.8, f32[8,2048]{1,0:T(8,128)} %angle_hbm.1, ...), custom_call_target="tpu_custom_call" | custom-call | flops 5000000000 | bytes 11534336 | tf_op jit(solution)/shard_map/pallas_call | solution.py:23
  4.7 0.0 collective-permute-done.far_ref
  4.7 0.3 copy-done
  5.0 0.2 copy-done.1
  5.3 0.0 copy-done.3
  5.3 2.7 %shard_map.101 = (bf16[16,32,128]{2,1,0:T(8,128)(2,1)}, bf16[64,512]{1,0:T(8,128)(2,1)S(1)}, bf16[1024,256]{1,0:T(8,128)(2,1)S(1)}) custom-call(bf16[64,512]{1,0:T(8,128)(2,1)S(1)} %copy-done.3, bf16[64,512]{1,0:T(8,128)(2,1)S(1)} %collective-permute-done.far_ref, bf16[512,1024]{1,0:T(8,128)(2,1)S(1)} %copy-done.1, f32[8,2048]{1,0:T(8,128)S(1)} %get-tuple-element.15.cos_ref, ...), custom_call_target="tpu_custom_call" | custom-call | flops 1207959552 | bytes 10485760 | tf_op jit(solution)/shard_map/pallas_call | solution.py:23
  7.9 7.6 %all-to-all-start = ((bf16[16,32,128]{2,1,0:T(8,128)(2,1)}), bf16[16,32,128]{2,1,0:T(8,128)(2,1)S(1)}, u32[]{:S(2)}, u32[]{:S(2)}) async-start(bf16[16,32,128]{2,1,0:T(8,128)(2,1)} %get-tuple-element.17), calls=%async_computation | async-start | bytes 262144 | tf_op jit(solution)/shard_map/all_to_all | solution.py:323
  15.5 0.4 collective-permute-start.1
  15.9 3.1 %collective-permute-start.2 = (bf16[64,512]{1,0:T(8,128)(2,1)S(1)}, bf16[64,512]{1,0:T(8,128)(2,1)S(1)}, u32[]{:S(2)}, u32[]{:S(2)}) collective-permute-start(bf16[64,512]{1,0:T(8,128)(2,1)S(1)} %get-tuple-element.20), channel_id=1, source_target_pairs={{0,0},{1,2},{2,1},{3,4},{4,3},{5,6},{6,5},{7,8},{8,7},{9,10},{10,9... | collective-permute-start | bytes 196616 | tf_op jit(solution)/shard_map/ppermute | solution.py:326
  19.0 1.8 %all-to-all-done.upper_ref = bf16[16,32,128]{2,1,0:T(8,128)(2,1)S(1)} async-done(((bf16[16,32,128]{2,1,0:T(8,128)(2,1)}), bf16[16,32,128]{2,1,0:T(8,128)(2,1)S(1)}, u32[]{:S(2)}, u32[]{:S(2)}) %all-to-all-start) | async-done | bytes 131104 | tf_op jit(solution)/shard_map/all_to_all | solution.py:323
  20.7 1.4 %shard_map.102._ = bf16[16,16,128]{2,1,0:T(8,128)(2,1)} custom-call(bf16[16,32,128]{2,1,0:T(8,128)(2,1)S(1)} %all-to-all-done.upper_ref, s32[128,32]{1,0:T(8,128)S(1)} %get-tuple-element.18.index_ref, bf16[20,128,256]{2,1,0:T(8,128)(2,1)S(1)} %get-tuple-element.19.operator_ref), custom_call_target="tpu_custom_call" | custom-call | flops 335544320 | bytes 2097152 | tf_op jit(solution)/shard_map/pallas_call | solution.py:23
  22.1 5.7 %all-to-all-start.1 = ((bf16[16,16,128]{2,1,0:T(8,128)(2,1)}), bf16[16,16,128]{2,1,0:T(8,128)(2,1)S(1)}, u32[]{:S(2)}, u32[]{:S(2)}) async-start(bf16[16,16,128]{2,1,0:T(8,128)(2,1)} %shard_map.102._), calls=%async_computation.1 | async-start | bytes 131072 | tf_op jit(solution)/shard_map/all_to_all | solution.py:337
  27.8 0.0 collective-permute-done.1.sibling_ref
  27.8 0.0 collective-permute-done.2.cross_ref
  27.8 0.0 copy-start.2
  27.8 6.0 %shard_map.103 = (f32[64,512]{1,0:T(8,128)S(1)}, bf16[1024,512]{1,0:T(8,128)(2,1)S(1)}) custom-call(bf16[64,512]{1,0:T(8,128)(2,1)S(1)} %copy-done.3, bf16[64,512]{1,0:T(8,128)(2,1)S(1)} %collective-permute-done.1.sibling_ref, bf16[64,512]{1,0:T(8,128)(2,1)S(1)} %collective-permute-done.2.cross_ref, s32[64,32]{1,0:T(8,128)S(1)} %get-tuple-element.21.col_ref, ...), custom_call_target="tpu_custom_call" | custom-call | flops 1132462080 | bytes 15728640 | tf_op jit(solution)/shard_map/pallas_call | solution.py:23
  33.8 0.0 all-to-all-done.1.inc_ref
  33.8 0.0 copy-done.2
  33.8 4.8 %shard_map.104 = f32[64,512]{1,0:T(8,128)} custom-call(bf16[16,16,128]{2,1,0:T(8,128)(2,1)S(1)} %all-to-all-done.1.inc_ref, f32[8,2048]{1,0:T(8,128)S(1)} %get-tuple-element.15.cos_ref, f32[8,2048]{1,0:T(8,128)S(1)} %get-tuple-element.16.sin_ref, f32[64,512]{1,0:T(8,128)S(1)} %get-tuple-element.22.near_ref, bf16[1024,512]{1,0:T(8,128)(2,1)S(1)} %copy-done.2, ...), custom_call_target="tpu_custom_call" | custom-call | flops 805306368 | bytes 10485760 | tf_op jit(solution)/shard_map/pallas_call | solution.py:23
Async XLA Ops:
  0.0 4.7 %collective-permute-start = (bf16[64,512]{1,0:T(8,128)(2,1)}, bf16[64,512]{1,0:T(8,128)(2,1)S(1)}, u32[]{:S(2)}, u32[]{:S(2)}) collective-permute-start(bf16[64,512]{1,0:T(8,128)(2,1)} %own_ref.3), channel_id=1, source_target_pairs={{0,12},{1,13},{2,14},{3,15},{4,8},{5,9},{6,10},{7,11},{8,26},{9,27... | collective-permute-start | bytes 196616 | tf_op jit(solution)/shard_map/ppermute | solution.py:271
  1.5 3.6 %copy-start = (bf16[1024,4096]{1,0:T(8,128)(2,1)S(1)}, bf16[1024,4096]{1,0:T(8,128)(2,1)}, u32[]{:S(2)}) copy-start(bf16[1024,4096]{1,0:T(8,128)(2,1)} %interp.5) | copy-start | bytes 25165828
  1.5 3.8 %copy-start.1 = (bf16[512,1024]{1,0:T(8,128)(2,1)S(1)}, bf16[512,1024]{1,0:T(8,128)(2,1)}, u32[]{:S(2)}) copy-start(bf16[512,1024]{1,0:T(8,128)(2,1)} %agg_ref.1) | copy-start | bytes 3145732
  1.5 3.8 %copy-start.3 = (bf16[64,512]{1,0:T(8,128)(2,1)S(1)}, bf16[64,512]{1,0:T(8,128)(2,1)}, u32[]{:S(2)}) copy-start(bf16[64,512]{1,0:T(8,128)(2,1)} %own_ref.3) | copy-start | bytes 196612
  7.9 12.8 %all-to-all-start = ((bf16[16,32,128]{2,1,0:T(8,128)(2,1)}), bf16[16,32,128]{2,1,0:T(8,128)(2,1)S(1)}, u32[]{:S(2)}, u32[]{:S(2)}) async-start(bf16[16,32,128]{2,1,0:T(8,128)(2,1)} %get-tuple-element.17), calls=%async_computation | async-start | bytes 262144 | tf_op jit(solution)/shard_map/all_to_all | solution.py:323
  15.5 12.3 %collective-permute-start.1 = (bf16[64,512]{1,0:T(8,128)(2,1)S(1)}, bf16[64,512]{1,0:T(8,128)(2,1)S(1)}, u32[]{:S(2)}, u32[]{:S(2)}) collective-permute-start(bf16[64,512]{1,0:T(8,128)(2,1)S(1)} %copy-done.3), channel_id=1, source_target_pairs={{0,1},{1,0},{2,3},{3,2},{4,5},{5,4},{6,7},{7,6},{8,9},{9,8},{10,11... | collective-permute-start | bytes 196616 | tf_op jit(solution)/shard_map/ppermute | solution.py:272
  15.9 11.9 %collective-permute-start.2 = (bf16[64,512]{1,0:T(8,128)(2,1)S(1)}, bf16[64,512]{1,0:T(8,128)(2,1)S(1)}, u32[]{:S(2)}, u32[]{:S(2)}) collective-permute-start(bf16[64,512]{1,0:T(8,128)(2,1)S(1)} %get-tuple-element.20), channel_id=1, source_target_pairs={{0,0},{1,2},{2,1},{3,4},{4,3},{5,6},{6,5},{7,8},{8,7},{9,10},{10,9... | collective-permute-start | bytes 196616 | tf_op jit(solution)/shard_map/ppermute | solution.py:326
  22.1 11.7 %all-to-all-start.1 = ((bf16[16,16,128]{2,1,0:T(8,128)(2,1)}), bf16[16,16,128]{2,1,0:T(8,128)(2,1)S(1)}, u32[]{:S(2)}, u32[]{:S(2)}) async-start(bf16[16,16,128]{2,1,0:T(8,128)(2,1)} %shard_map.102._), calls=%async_computation.1 | async-start | bytes 131072 | tf_op jit(solution)/shard_map/all_to_all | solution.py:337
  27.8 6.0 %copy-start.2 = (bf16[1024,512]{1,0:T(8,128)(2,1)S(1)}, bf16[1024,512]{1,0:T(8,128)(2,1)}, u32[]{:S(2)}) copy-start(bf16[1024,512]{1,0:T(8,128)(2,1)} %receive_ref.1) | copy-start | bytes 3145732

commit v13 on v12

--- a/solution.py
+++ b/solution.py
@@ -117,7 +117,7 @@
     copy = pltpu.make_async_copy(interp.at[:, pl.ds(0, KEPT * 256)], kept, sem)
     copy.start()
     relay_ref[...] = own_ref[...]
-    width = 256
+    width = 512
     directions = cos_ref.shape[1]
     leaves = own_ref.shape[0]
     rows = 2 * leaves
@@ -132,18 +132,20 @@
     for j in range(directions // width):
         re = dot(pattern, interp[:, j * width : (j + 1) * width])
         im = dot(pattern, interp[:, directions + j * width : directions + (j + 1) * width])
-        acc_re = jnp.zeros((parents, width), F32)
-        acc_im = jnp.zeros((parents, width), F32)
-        for k in range(8):
-            cosine = cos_ref[pl.ds(k, 1), pl.ds(j * width, width)]
-            sine = sin_ref[pl.ds(k, 1), pl.ds(j * width, width)]
-            a, b = re[k * parents : (k + 1) * parents], im[k * parents : (k + 1) * parents]
-            acc_re += a * cosine - b * sine
-            acc_im += a * sine + b * cosine
         for h in range(width // 128):
-            s = slice(h * 128, (h + 1) * 128)
-            out_ref[j * (width // 128) + h, 0:parents, :] = acc_re[:, s].astype(BF16)
-            out_ref[j * (width // 128) + h, parents : 2 * parents, :] = acc_im[:, s].astype(BF16)
+            lanes = slice(h * 128, (h + 1) * 128)
+            acc_re = jnp.zeros((parents, 128), F32)
+            acc_im = jnp.zeros((parents, 128), F32)
+            for k in range(8):
+                cosine = cos_ref[pl.ds(k, 1), pl.ds(j * width + h * 128, 128)]
+                sine = sin_ref[pl.ds(k, 1), pl.ds(j * width + h * 128, 128)]
+                a = re[k * parents : (k + 1) * parents, lanes]
+                b = im[k * parents : (k + 1) * parents, lanes]
+                acc_re += a * cosine - b * sine
+                acc_im += a * sine + b * cosine
+            block = j * (width // 128) + h
+            out_ref[block, 0:parents, :] = acc_re.astype(BF16)
+            out_ref[block, parents : 2 * parents, :] = acc_im.astype(BF16)
     copy.wait()
 
 

time: 38.8 us -> 38.7 us (level)
  transfers between devices with their start and end apart: 5 -> 5, of which waited for: 1 -> 1; matrix products, arithmetic and copies ran while one was open for 0% -> 0% of each run, Pallas kernels for 27% -> 28%
where the time goes in v13:
time: 38.7 us; the launch traced here: 38.4 us
  starting transfers between devices  18.1 us (47%)
  Pallas kernels  17.8 us (46%)
  waiting for transfers between devices  1.77 us (5%)
  local copies, waits for them, and re-layouts  0.57 us (1%)
    pallas_call x5, Pallas kernels, call(): pl.pallas_call(body, out_shape=out, in_specs=specs, out_specs=jax.tree.ma...  17.8 us
    all_to_all x1, starting transfers between devices, on_device(): upper = lax.all_to_all(up, 'dir', split_axis=0, concat_axis=0, tiled=True)  7.56 us
    all_to_all x1, starting transfers between devices, on_device(): lax.all_to_all(local, 'dir', split_axis=0, concat_axis=0, tiled=True)  5.66 us
    ppermute x1, starting transfers between devices, on_device(): from_cross = lax.ppermute(relay, BOTH, cross)  3.11 us
    all_to_all x1, waiting for transfers between devices, on_device(): upper = lax.all_to_all(up, 'dir', split_axis=0, concat_axis=0, tiled=True)  1.76 us
    ppermute x1, starting transfers between devices, on_device(): lax.ppermute(currents, BOTH, [(i, halo_target(i, boxes, dirs)) for i in r...  1.39 us
  transfers between devices with their start and end apart: 5, of which 1 were waited for; matrix products, arithmetic and copies ran while one was open for 0% of the time, Pallas kernels for 28%

profile of v13, /device:TPU:27, one launch (start us, length us, event | category | flops | bytes accessed | tf_op | source)
XLA Modules:
  0.0 38.4 jit_solution(1201930347307148832)
XLA Ops:
  0.0 1.4 %collective-permute-start = (bf16[64,512]{1,0:T(8,128)(2,1)}, bf16[64,512]{1,0:T(8,128)(2,1)S(1)}, u32[]{:S(2)}, u32[]{:S(2)}) collective-permute-start(bf16[64,512]{1,0:T(8,128)(2,1)} %own_ref.3), channel_id=1, source_target_pairs={{0,12},{1,13},{2,14},{3,15},{4,8},{5,9},{6,10},{7,11},{8,26},{9,27... | collective-permute-start | bytes 196616 | tf_op jit(solution)/shard_map/ppermute | solution.py:273
  1.4 0.1 pad_add_fusion.place_ref
  1.5 0.0 copy-start
  1.5 0.0 copy-start.1
  1.5 0.0 copy-start.3
  1.5 3.2 %shard_map.100 = (bf16[20,128,256]{2,1,0:T(8,128)(2,1)S(1)}, s32[128,32]{1,0:T(8,128)S(1)}, s32[64,32]{1,0:T(8,128)S(1)}, f32[8,2048]{1,0:T(8,128)S(1)}, f32[8,2048]{1,0:T(8,128)S(1)}) custom-call(s32[2]{0:T(128)S(1)} %pad_add_fusion.place_ref, s32[20,1024]{1,0:T(8,128)} %bitcast.7, s32[20,1024]{1,0:T(8,128)} %bitcast.8, f32[8,2048]{1,0:T(8,128)} %angle_hbm.1, ...), custom_call_target="tpu_custom_call" | custom-call | flops 5000000000 | bytes 11534336 | tf_op jit(solution)/shard_map/pallas_call | solution.py:23
  4.7 0.0 collective-permute-done.far_ref
  4.7 0.3 copy-done
  5.0 0.2 copy-done.1
  5.3 0.0 copy-done.3
  5.3 2.5 %shard_map.101 = (bf16[16,32,128]{2,1,0:T(8,128)(2,1)}, bf16[64,512]{1,0:T(8,128)(2,1)S(1)}, bf16[1024,256]{1,0:T(8,128)(2,1)S(1)}) custom-call(bf16[64,512]{1,0:T(8,128)(2,1)S(1)} %copy-done.3, bf16[64,512]{1,0:T(8,128)(2,1)S(1)} %collective-permute-done.far_ref, bf16[512,1024]{1,0:T(8,128)(2,1)S(1)} %copy-done.1, f32[8,2048]{1,0:T(8,128)S(1)} %get-tuple-element.15.cos_ref, ...), custom_call_target="tpu_custom_call" | custom-call | flops 1207959552 | bytes 10485760 | tf_op jit(solution)/shard_map/pallas_call | solution.py:23
  7.8 7.6 %all-to-all-start = ((bf16[16,32,128]{2,1,0:T(8,128)(2,1)}), bf16[16,32,128]{2,1,0:T(8,128)(2,1)S(1)}, u32[]{:S(2)}, u32[]{:S(2)}) async-start(bf16[16,32,128]{2,1,0:T(8,128)(2,1)} %get-tuple-element.17), calls=%async_computation | async-start | bytes 262144 | tf_op jit(solution)/shard_map/all_to_all | solution.py:325
  15.3 0.4 collective-permute-start.1
  15.7 3.1 %collective-permute-start.2 = (bf16[64,512]{1,0:T(8,128)(2,1)S(1)}, bf16[64,512]{1,0:T(8,128)(2,1)S(1)}, u32[]{:S(2)}, u32[]{:S(2)}) collective-permute-start(bf16[64,512]{1,0:T(8,128)(2,1)S(1)} %get-tuple-element.20), channel_id=1, source_target_pairs={{0,0},{1,2},{2,1},{3,4},{4,3},{5,6},{6,5},{7,8},{8,7},{9,10},{10,9... | collective-permute-start | bytes 196616 | tf_op jit(solution)/shard_map/ppermute | solution.py:328
  18.8 1.8 %all-to-all-done.upper_ref = bf16[16,32,128]{2,1,0:T(8,128)(2,1)S(1)} async-done(((bf16[16,32,128]{2,1,0:T(8,128)(2,1)}), bf16[16,32,128]{2,1,0:T(8,128)(2,1)S(1)}, u32[]{:S(2)}, u32[]{:S(2)}) %all-to-all-start) | async-done | bytes 131104 | tf_op jit(solution)/shard_map/all_to_all | solution.py:325
  20.6 1.4 %shard_map.102._ = bf16[16,16,128]{2,1,0:T(8,128)(2,1)} custom-call(bf16[16,32,128]{2,1,0:T(8,128)(2,1)S(1)} %all-to-all-done.upper_ref, s32[128,32]{1,0:T(8,128)S(1)} %get-tuple-element.18.index_ref, bf16[20,128,256]{2,1,0:T(8,128)(2,1)S(1)} %get-tuple-element.19.operator_ref), custom_call_target="tpu_custom_call" | custom-call | flops 335544320 | bytes 2097152 | tf_op jit(solution)/shard_map/pallas_call | solution.py:23
  21.9 5.7 %all-to-all-start.1 = ((bf16[16,16,128]{2,1,0:T(8,128)(2,1)}), bf16[16,16,128]{2,1,0:T(8,128)(2,1)S(1)}, u32[]{:S(2)}, u32[]{:S(2)}) async-start(bf16[16,16,128]{2,1,0:T(8,128)(2,1)} %shard_map.102._), calls=%async_computation.1 | async-start | bytes 131072 | tf_op jit(solution)/shard_map/all_to_all | solution.py:339
  27.6 0.0 collective-permute-done.1.sibling_ref
  27.6 0.0 collective-permute-done.2.cross_ref
  27.6 0.0 copy-start.2
  27.6 6.0 %shard_map.103 = (f32[64,512]{1,0:T(8,128)S(1)}, bf16[1024,512]{1,0:T(8,128)(2,1)S(1)}) custom-call(bf16[64,512]{1,0:T(8,128)(2,1)S(1)} %copy-done.3, bf16[64,512]{1,0:T(8,128)(2,1)S(1)} %collective-permute-done.1.sibling_ref, bf16[64,512]{1,0:T(8,128)(2,1)S(1)} %collective-permute-done.2.cross_ref, s32[64,32]{1,0:T(8,128)S(1)} %get-tuple-element.21.col_ref, ...), custom_call_target="tpu_custom_call" | custom-call | flops 1132462080 | bytes 15728640 | tf_op jit(solution)/shard_map/pallas_call | solution.py:23
  33.6 0.0 all-to-all-done.1.inc_ref
  33.6 0.0 copy-done.2
  33.6 4.8 %shard_map.104 = f32[64,512]{1,0:T(8,128)} custom-call(bf16[16,16,128]{2,1,0:T(8,128)(2,1)S(1)} %all-to-all-done.1.inc_ref, f32[8,2048]{1,0:T(8,128)S(1)} %get-tuple-element.15.cos_ref, f32[8,2048]{1,0:T(8,128)S(1)} %get-tuple-element.16.sin_ref, f32[64,512]{1,0:T(8,128)S(1)} %get-tuple-element.22.near_ref, bf16[1024,512]{1,0:T(8,128)(2,1)S(1)} %copy-done.2, ...), custom_call_target="tpu_custom_call" | custom-call | flops 805306368 | bytes 10485760 | tf_op jit(solution)/shard_map/pallas_call | solution.py:23
Async XLA Ops:
  0.0 4.7 %collective-permute-start = (bf16[64,512]{1,0:T(8,128)(2,1)}, bf16[64,512]{1,0:T(8,128)(2,1)S(1)}, u32[]{:S(2)}, u32[]{:S(2)}) collective-permute-start(bf16[64,512]{1,0:T(8,128)(2,1)} %own_ref.3), channel_id=1, source_target_pairs={{0,12},{1,13},{2,14},{3,15},{4,8},{5,9},{6,10},{7,11},{8,26},{9,27... | collective-permute-start | bytes 196616 | tf_op jit(solution)/shard_map/ppermute | solution.py:273
  1.5 3.6 %copy-start = (bf16[1024,4096]{1,0:T(8,128)(2,1)S(1)}, bf16[1024,4096]{1,0:T(8,128)(2,1)}, u32[]{:S(2)}) copy-start(bf16[1024,4096]{1,0:T(8,128)(2,1)} %interp.5) | copy-start | bytes 25165828
  1.5 3.8 %copy-start.1 = (bf16[512,1024]{1,0:T(8,128)(2,1)S(1)}, bf16[512,1024]{1,0:T(8,128)(2,1)}, u32[]{:S(2)}) copy-start(bf16[512,1024]{1,0:T(8,128)(2,1)} %agg_ref.1) | copy-start | bytes 3145732
  1.5 3.8 %copy-start.3 = (bf16[64,512]{1,0:T(8,128)(2,1)S(1)}, bf16[64,512]{1,0:T(8,128)(2,1)}, u32[]{:S(2)}) copy-start(bf16[64,512]{1,0:T(8,128)(2,1)} %own_ref.3) | copy-start | bytes 196612
  7.8 12.8 %all-to-all-start = ((bf16[16,32,128]{2,1,0:T(8,128)(2,1)}), bf16[16,32,128]{2,1,0:T(8,128)(2,1)S(1)}, u32[]{:S(2)}, u32[]{:S(2)}) async-start(bf16[16,32,128]{2,1,0:T(8,128)(2,1)} %get-tuple-element.17), calls=%async_computation | async-start | bytes 262144 | tf_op jit(solution)/shard_map/all_to_all | solution.py:325
  15.3 12.3 %collective-permute-start.1 = (bf16[64,512]{1,0:T(8,128)(2,1)S(1)}, bf16[64,512]{1,0:T(8,128)(2,1)S(1)}, u32[]{:S(2)}, u32[]{:S(2)}) collective-permute-start(bf16[64,512]{1,0:T(8,128)(2,1)S(1)} %copy-done.3), channel_id=1, source_target_pairs={{0,1},{1,0},{2,3},{3,2},{4,5},{5,4},{6,7},{7,6},{8,9},{9,8},{10,11... | collective-permute-start | bytes 196616 | tf_op jit(solution)/shard_map/ppermute | solution.py:274
  15.7 11.9 %collective-permute-start.2 = (bf16[64,512]{1,0:T(8,128)(2,1)S(1)}, bf16[64,512]{1,0:T(8,128)(2,1)S(1)}, u32[]{:S(2)}, u32[]{:S(2)}) collective-permute-start(bf16[64,512]{1,0:T(8,128)(2,1)S(1)} %get-tuple-element.20), channel_id=1, source_target_pairs={{0,0},{1,2},{2,1},{3,4},{4,3},{5,6},{6,5},{7,8},{8,7},{9,10},{10,9... | collective-permute-start | bytes 196616 | tf_op jit(solution)/shard_map/ppermute | solution.py:328
  21.9 11.7 %all-to-all-start.1 = ((bf16[16,16,128]{2,1,0:T(8,128)(2,1)}), bf16[16,16,128]{2,1,0:T(8,128)(2,1)S(1)}, u32[]{:S(2)}, u32[]{:S(2)}) async-start(bf16[16,16,128]{2,1,0:T(8,128)(2,1)} %shard_map.102._), calls=%async_computation.1 | async-start | bytes 131072 | tf_op jit(solution)/shard_map/all_to_all | solution.py:339
  27.6 6.0 %copy-start.2 = (bf16[1024,512]{1,0:T(8,128)(2,1)S(1)}, bf16[1024,512]{1,0:T(8,128)(2,1)}, u32[]{:S(2)}) copy-start(bf16[1024,512]{1,0:T(8,128)(2,1)} %receive_ref.1) | copy-start | bytes 3145732

commit v14 on v13

--- a/solution.py
+++ b/solution.py
@@ -44,7 +44,6 @@
 
 
 def prepare_kernel(
-    place_ref,
     far_hbm,
     kind_hbm,
     angle_hbm,
@@ -64,7 +63,7 @@
     sems,
 ):
     slots, parents = far_ref.shape
-    box, me = place_ref[0], place_ref[1]
+    box, me = lax.axis_index("box"), lax.axis_index(BOTH)
     mine = pl.ds(pl.multiple_of(box * parents, parents), parents)
     copies = [
         pltpu.make_async_copy(
@@ -265,15 +264,12 @@
 ):
     leaves, width = currents.shape
     n = boxes * dirs
-    me = lax.axis_index(BOTH)
-    box = lax.axis_index("box")
     parents = leaves // 8 * dirs
     slots, near_slots = far_list.shape[1], near_list.shape[1]
 
     far_half = lax.ppermute(currents, BOTH, [(i, halo_target(i, boxes, dirs)) for i in range(n)])
     from_sibling = lax.ppermute(currents, BOTH, [(i, i ^ 1) for i in range(n)])
 
-    place = jnp.stack([box, me]).astype(I32)
     operators, index, column, cosine, sine = call(
         prepare_kernel,
         (
@@ -283,17 +279,14 @@
             pltpu.VMEM(shift_angle.shape, F32),
             pltpu.VMEM(shift_angle.shape, F32),
         ),
-        (
-            place,
-            *in_hbm(
-                far_list.T,
-                far_kind.T,
-                shift_angle,
-                translation.reshape(-1, translation.shape[2]),
-                near_list.T,
-            ),
-        ),
-        [whole(pltpu.SMEM)] + [whole(pltpu.HBM)] * 5,
+        in_hbm(
+            far_list.T,
+            far_kind.T,
+            shift_angle,
+            translation.reshape(-1, translation.shape[2]),
+            near_list.T,
+        ),
+        [whole(pltpu.HBM)] * 5,
         [
             pltpu.VMEM((slots, parents), I32),
             pltpu.VMEM((slots, parents), I32),

time: 38.7 us -> 38.7 us (level)
  local copies, waits for them, and re-layouts: 0.57 us -> 1.18 us
  Pallas kernels: 17.8 us -> 17.2 us
    pallas_call x5, Pallas kernels: 17.8 us -> 17.2 us  [call(): pl.pallas_call(body, out_shape=out, in_specs=specs, out_specs=jax.tree.ma...]
    unnamed x8, local copies, waits for them, and re-layouts: 0.57 us -> 1.18 us
  transfers between devices with their start and end apart: 5 -> 5, of which waited for: 1 -> 1; matrix products, arithmetic and copies ran while one was open for 0% -> 0% of each run, Pallas kernels for 28% -> 26%
where the time goes in v14:
time: 38.7 us; the launch traced here: 38.4 us
  starting transfers between devices  18.2 us (47%)
  Pallas kernels  17.2 us (44%)
  waiting for transfers between devices  1.77 us (5%)
  local copies, waits for them, and re-layouts  1.18 us (3%)
    pallas_call x5, Pallas kernels, call(): pl.pallas_call(body, out_shape=out, in_specs=specs, out_specs=jax.tree.ma...  17.2 us
    all_to_all x1, starting transfers between devices, on_device(): upper = lax.all_to_all(up, 'dir', split_axis=0, concat_axis=0, tiled=True)  7.59 us
    all_to_all x1, starting transfers between devices, on_device(): lax.all_to_all(local, 'dir', split_axis=0, concat_axis=0, tiled=True)  5.71 us
    ppermute x1, starting transfers between devices, on_device(): from_cross = lax.ppermute(relay, BOTH, cross)  3.11 us
    all_to_all x1, waiting for transfers between devices, on_device(): upper = lax.all_to_all(up, 'dir', split_axis=0, concat_axis=0, tiled=True)  1.76 us
    ppermute x1, starting transfers between devices, on_device(): lax.ppermute(currents, BOTH, [(i, halo_target(i, boxes, dirs)) for i in r...  1.39 us
    unnamed x8, local copies, waits for them, and re-layouts  1.18 us
  transfers between devices with their start and end apart: 5, of which 1 were waited for; matrix products, arithmetic and copies ran while one was open for 0% of the time, Pallas kernels for 26%

profile of v14, /device:TPU:27, one launch (start us, length us, event | category | flops | bytes accessed | tf_op | source)
XLA Modules:
  0.0 38.4 jit_solution(13398945958723302427)
XLA Ops:
  0.0 1.4 %collective-permute-start = (bf16[64,512]{1,0:T(8,128)(2,1)}, bf16[64,512]{1,0:T(8,128)(2,1)S(1)}, u32[]{:S(2)}, u32[]{:S(2)}) collective-permute-start(bf16[64,512]{1,0:T(8,128)(2,1)} %own_ref.3), channel_id=1, source_target_pairs={{0,12},{1,13},{2,14},{3,15},{4,8},{5,9},{6,10},{7,11},{8,26},{9,27... | collective-permute-start | bytes 196616 | tf_op jit(solution)/shard_map/ppermute | solution.py:270
  1.4 0.0 copy-start
  1.4 0.0 copy-start.1
  1.4 0.0 copy-start.3
  1.4 2.6 %shard_map.100 = (bf16[20,128,256]{2,1,0:T(8,128)(2,1)S(1)}, s32[128,32]{1,0:T(8,128)S(1)}, s32[64,32]{1,0:T(8,128)S(1)}, f32[8,2048]{1,0:T(8,128)S(1)}, f32[8,2048]{1,0:T(8,128)S(1)}) custom-call(s32[20,1024]{1,0:T(8,128)} %bitcast.5, s32[20,1024]{1,0:T(8,128)} %bitcast.6, f32[8,2048]{1,0:T(8,128)} %angle_hbm.1, f32[632,128]{1,0:T(8,128)} %bitcast.4, ...), custom_call_target="tpu_custom_call" | custom-call | flops 5000000000 | bytes 11534336 | tf_op jit(solution)/shard_map/pallas_call | solution.py:23
  4.0 0.0 collective-permute-done.far_ref
  4.0 0.9 %copy-done = bf16[1024,4096]{1,0:T(8,128)(2,1)S(1)} copy-done((bf16[1024,4096]{1,0:T(8,128)(2,1)S(1)}, bf16[1024,4096]{1,0:T(8,128)(2,1)}, u32[]{:S(2)}) %copy-start) | copy-done | bytes 8388632
  5.0 0.2 copy-done.1
  5.2 0.0 copy-done.3
  5.2 2.5 %shard_map.101 = (bf16[16,32,128]{2,1,0:T(8,128)(2,1)}, bf16[64,512]{1,0:T(8,128)(2,1)S(1)}, bf16[1024,256]{1,0:T(8,128)(2,1)S(1)}) custom-call(bf16[64,512]{1,0:T(8,128)(2,1)S(1)} %copy-done.3, bf16[64,512]{1,0:T(8,128)(2,1)S(1)} %collective-permute-done.far_ref, bf16[512,1024]{1,0:T(8,128)(2,1)S(1)} %copy-done.1, f32[8,2048]{1,0:T(8,128)S(1)} %get-tuple-element.15.cos_ref, ...), custom_call_target="tpu_custom_call" | custom-call | flops 1207959552 | bytes 10485760 | tf_op jit(solution)/shard_map/pallas_call | solution.py:23
  7.7 7.6 %all-to-all-start = ((bf16[16,32,128]{2,1,0:T(8,128)(2,1)}), bf16[16,32,128]{2,1,0:T(8,128)(2,1)S(1)}, u32[]{:S(2)}, u32[]{:S(2)}) async-start(bf16[16,32,128]{2,1,0:T(8,128)(2,1)} %get-tuple-element.17), calls=%async_computation | async-start | bytes 262144 | tf_op jit(solution)/shard_map/all_to_all | solution.py:318
  15.3 0.4 collective-permute-start.1
  15.6 3.1 %collective-permute-start.2 = (bf16[64,512]{1,0:T(8,128)(2,1)S(1)}, bf16[64,512]{1,0:T(8,128)(2,1)S(1)}, u32[]{:S(2)}, u32[]{:S(2)}) collective-permute-start(bf16[64,512]{1,0:T(8,128)(2,1)S(1)} %get-tuple-element.20), channel_id=1, source_target_pairs={{0,0},{1,2},{2,1},{3,4},{4,3},{5,6},{6,5},{7,8},{8,7},{9,10},{10,9... | collective-permute-start | bytes 196616 | tf_op jit(solution)/shard_map/ppermute | solution.py:321
  18.8 1.8 %all-to-all-done.upper_ref = bf16[16,32,128]{2,1,0:T(8,128)(2,1)S(1)} async-done(((bf16[16,32,128]{2,1,0:T(8,128)(2,1)}), bf16[16,32,128]{2,1,0:T(8,128)(2,1)S(1)}, u32[]{:S(2)}, u32[]{:S(2)}) %all-to-all-start) | async-done | bytes 131104 | tf_op jit(solution)/shard_map/all_to_all | solution.py:318
  20.5 1.4 %shard_map.102._ = bf16[16,16,128]{2,1,0:T(8,128)(2,1)} custom-call(bf16[16,32,128]{2,1,0:T(8,128)(2,1)S(1)} %all-to-all-done.upper_ref, s32[128,32]{1,0:T(8,128)S(1)} %get-tuple-element.18.index_ref, bf16[20,128,256]{2,1,0:T(8,128)(2,1)S(1)} %get-tuple-element.19.operator_ref), custom_call_target="tpu_custom_call" | custom-call | flops 335544320 | bytes 2097152 | tf_op jit(solution)/shard_map/pallas_call | solution.py:23
  21.9 5.7 %all-to-all-start.1 = ((bf16[16,16,128]{2,1,0:T(8,128)(2,1)}), bf16[16,16,128]{2,1,0:T(8,128)(2,1)S(1)}, u32[]{:S(2)}, u32[]{:S(2)}) async-start(bf16[16,16,128]{2,1,0:T(8,128)(2,1)} %shard_map.102._), calls=%async_computation.1 | async-start | bytes 131072 | tf_op jit(solution)/shard_map/all_to_all | solution.py:332
  27.6 0.0 collective-permute-done.1.sibling_ref
  27.6 0.0 collective-permute-done.2.cross_ref
  27.6 0.0 copy-start.2
  27.6 6.0 %shard_map.103 = (f32[64,512]{1,0:T(8,128)S(1)}, bf16[1024,512]{1,0:T(8,128)(2,1)S(1)}) custom-call(bf16[64,512]{1,0:T(8,128)(2,1)S(1)} %copy-done.3, bf16[64,512]{1,0:T(8,128)(2,1)S(1)} %collective-permute-done.1.sibling_ref, bf16[64,512]{1,0:T(8,128)(2,1)S(1)} %collective-permute-done.2.cross_ref, s32[64,32]{1,0:T(8,128)S(1)} %get-tuple-element.21.col_ref, ...), custom_call_target="tpu_custom_call" | custom-call | flops 1132462080 | bytes 15728640 | tf_op jit(solution)/shard_map/pallas_call | solution.py:23
  33.6 0.0 all-to-all-done.1.inc_ref
  33.6 0.0 copy-done.2
  33.6 4.8 %shard_map.104 = f32[64,512]{1,0:T(8,128)} custom-call(bf16[16,16,128]{2,1,0:T(8,128)(2,1)S(1)} %all-to-all-done.1.inc_ref, f32[8,2048]{1,0:T(8,128)S(1)} %get-tuple-element.15.cos_ref, f32[8,2048]{1,0:T(8,128)S(1)} %get-tuple-element.16.sin_ref, f32[64,512]{1,0:T(8,128)S(1)} %get-tuple-element.22.near_ref, bf16[1024,512]{1,0:T(8,128)(2,1)S(1)} %copy-done.2, ...), custom_call_target="tpu_custom_call" | custom-call | flops 805306368 | bytes 10485760 | tf_op jit(solution)/shard_map/pallas_call | solution.py:23
Async XLA Ops:
  0.0 4.0 %collective-permute-start = (bf16[64,512]{1,0:T(8,128)(2,1)}, bf16[64,512]{1,0:T(8,128)(2,1)S(1)}, u32[]{:S(2)}, u32[]{:S(2)}) collective-permute-start(bf16[64,512]{1,0:T(8,128)(2,1)} %own_ref.3), channel_id=1, source_target_pairs={{0,12},{1,13},{2,14},{3,15},{4,8},{5,9},{6,10},{7,11},{8,26},{9,27... | collective-permute-start | bytes 196616 | tf_op jit(solution)/shard_map/ppermute | solution.py:270
  1.4 3.6 %copy-start = (bf16[1024,4096]{1,0:T(8,128)(2,1)S(1)}, bf16[1024,4096]{1,0:T(8,128)(2,1)}, u32[]{:S(2)}) copy-start(bf16[1024,4096]{1,0:T(8,128)(2,1)} %interp.5) | copy-start | bytes 25165828
  1.4 3.8 %copy-start.1 = (bf16[512,1024]{1,0:T(8,128)(2,1)S(1)}, bf16[512,1024]{1,0:T(8,128)(2,1)}, u32[]{:S(2)}) copy-start(bf16[512,1024]{1,0:T(8,128)(2,1)} %agg_ref.1) | copy-start | bytes 3145732
  1.4 3.8 %copy-start.3 = (bf16[64,512]{1,0:T(8,128)(2,1)S(1)}, bf16[64,512]{1,0:T(8,128)(2,1)}, u32[]{:S(2)}) copy-start(bf16[64,512]{1,0:T(8,128)(2,1)} %own_ref.3) | copy-start | bytes 196612
  7.7 12.8 %all-to-all-start = ((bf16[16,32,128]{2,1,0:T(8,128)(2,1)}), bf16[16,32,128]{2,1,0:T(8,128)(2,1)S(1)}, u32[]{:S(2)}, u32[]{:S(2)}) async-start(bf16[16,32,128]{2,1,0:T(8,128)(2,1)} %get-tuple-element.17), calls=%async_computation | async-start | bytes 262144 | tf_op jit(solution)/shard_map/all_to_all | solution.py:318
  15.3 12.3 %collective-permute-start.1 = (bf16[64,512]{1,0:T(8,128)(2,1)S(1)}, bf16[64,512]{1,0:T(8,128)(2,1)S(1)}, u32[]{:S(2)}, u32[]{:S(2)}) collective-permute-start(bf16[64,512]{1,0:T(8,128)(2,1)S(1)} %copy-done.3), channel_id=1, source_target_pairs={{0,1},{1,0},{2,3},{3,2},{4,5},{5,4},{6,7},{7,6},{8,9},{9,8},{10,11... | collective-permute-start | bytes 196616 | tf_op jit(solution)/shard_map/ppermute | solution.py:271
  15.6 12.0 %collective-permute-start.2 = (bf16[64,512]{1,0:T(8,128)(2,1)S(1)}, bf16[64,512]{1,0:T(8,128)(2,1)S(1)}, u32[]{:S(2)}, u32[]{:S(2)}) collective-permute-start(bf16[64,512]{1,0:T(8,128)(2,1)S(1)} %get-tuple-element.20), channel_id=1, source_target_pairs={{0,0},{1,2},{2,1},{3,4},{4,3},{5,6},{6,5},{7,8},{8,7},{9,10},{10,9... | collective-permute-start | bytes 196616 | tf_op jit(solution)/shard_map/ppermute | solution.py:321
  21.9 11.7 %all-to-all-start.1 = ((bf16[16,16,128]{2,1,0:T(8,128)(2,1)}), bf16[16,16,128]{2,1,0:T(8,128)(2,1)S(1)}, u32[]{:S(2)}, u32[]{:S(2)}) async-start(bf16[16,16,128]{2,1,0:T(8,128)(2,1)} %shard_map.102._), calls=%async_computation.1 | async-start | bytes 131072 | tf_op jit(solution)/shard_map/all_to_all | solution.py:332
  27.6 6.0 %copy-start.2 = (bf16[1024,512]{1,0:T(8,128)(2,1)S(1)}, bf16[1024,512]{1,0:T(8,128)(2,1)}, u32[]{:S(2)}) copy-start(bf16[1024,512]{1,0:T(8,128)(2,1)} %receive_ref.1) | copy-start | bytes 3145732

commit v15 on v13

--- a/solution.py
+++ b/solution.py
@@ -19,12 +19,12 @@
     return pl.BlockSpec(memory_space=space)
 
 
-def call(body, out, args, specs, scratch, mib, flops, moved):
+def call(body, out, args, specs, scratch, mib, flops, moved, place=VMEM):
     return pl.pallas_call(
         body,
         out_shape=out,
         in_specs=specs,
-        out_specs=jax.tree.map(lambda _: whole(), out),
+        out_specs=jax.tree.map(lambda _: whole(place), out),
         scratch_shapes=scratch,
         compiler_params=pltpu.CompilerParams(vmem_limit_bytes=mib << 20),
         cost_estimate=pl.CostEstimate(flops=flops, bytes_accessed=moved, transcendentals=0),
@@ -149,9 +149,9 @@
     copy.wait()
 
 
-def translate_kernel(upper_ref, index_ref, operator_ref, out_ref):
+def translate_kernel(upper_ref, index_ref, operator_ref, out, part_ref, sems):
     sources = upper_ref.shape[0] * 16
-    slots, rows = operator_ref.shape[:2]
+    slots, parents = operator_ref.shape[:2]
     field = jnp.concatenate(
         [
             upper_ref[:, 0:16, :].reshape(sources, 128),
@@ -159,24 +159,35 @@
         ],
         axis=1,
     )
+    rows = parents // 2
+    blocks = rows // 8
     lane = lax.broadcasted_iota(I32, (rows, sources), 1).astype(BF16)
-    index = index_ref[...].astype(BF16)
     one, zero = jnp.ones((), BF16), jnp.zeros((), BF16)
-    acc_re = jnp.zeros((rows, 128), F32)
-    acc_im = jnp.zeros((rows, 128), F32)
-    for first in range(0, slots, 4):
-        hot = [jnp.where(lane == index[:, j : j + 1], one, zero) for j in range(first, first + 4)]
-        picked = dot(jnp.concatenate(hot, axis=0), field)
-        for k in range(4):
-            x = picked[k * rows : (k + 1) * rows]
-            op = operator_ref[first + k].astype(F32)
-            xr, xi = x[:, :128], x[:, 128:]
-            tr, ti = op[:, :128], op[:, 128:]
-            acc_re += tr * xr - ti * xi
-            acc_im += tr * xi + ti * xr
-    blocks = out_ref.shape[0]
-    out_ref[:, 0:8, :] = acc_re.reshape(blocks, 8, 128).astype(BF16)
-    out_ref[:, 8:16, :] = acc_im.reshape(blocks, 8, 128).astype(BF16)
+    copies = []
+    for part in range(2):
+        low = part * rows
+        index = index_ref[low : low + rows].astype(BF16)
+        acc_re = jnp.zeros((rows, 128), F32)
+        acc_im = jnp.zeros((rows, 128), F32)
+        for first in range(0, slots, 4):
+            hot = [
+                jnp.where(lane == index[:, j : j + 1], one, zero) for j in range(first, first + 4)
+            ]
+            picked = dot(jnp.concatenate(hot, axis=0), field)
+            for k in range(4):
+                x = picked[k * rows : (k + 1) * rows]
+                op = operator_ref[first + k, low : low + rows].astype(F32)
+                xr, xi = x[:, :128], x[:, 128:]
+                tr, ti = op[:, :128], op[:, 128:]
+                acc_re += tr * xr - ti * xi
+                acc_im += tr * xi + ti * xr
+        part_ref[part, :, 0:8, :] = acc_re.reshape(blocks, 8, 128).astype(BF16)
+        part_ref[part, :, 8:16, :] = acc_im.reshape(blocks, 8, 128).astype(BF16)
+        target = out.at[pl.ds(part * blocks, blocks)]
+        copies.append(pltpu.make_async_copy(part_ref.at[part], target, sems.at[part]))
+        copies[part].start()
+    for copy in copies:
+        copy.wait()
 
 
 def down_kernel(inc_ref, cos_ref, sin_ref, near_ref, receive_ref, kept, more, interp, out_ref, buf, received, sems):
@@ -328,13 +339,17 @@
     from_cross = lax.ppermute(relay, BOTH, cross)
     local = call(
         translate_kernel,
-        jax.ShapeDtypeStruct((dirs, 2 * leaves // 8, 128), BF16),
+        pltpu.HBM((dirs, 2 * leaves // 8, 128), BF16),
         (upper, index, operators),
         [whole()] * 3,
-        [],
+        [
+            pltpu.VMEM((2, dirs // 2, 2 * leaves // 8, 128), BF16),
+            pltpu.SemaphoreType.DMA((2,)),
+        ],
         8,
         2 * slots * parents * 256 * 256,
         2 << 20,
+        pltpu.HBM,
     )
     incoming = lax.all_to_all(local, "dir", split_axis=0, concat_axis=0, tiled=True)
 

time: 38.7 us -> 39.6 us (1.023)
  local copies, waits for them, and re-layouts: 0.57 us -> 1.41 us
    unnamed x8 -> x10, local copies, waits for them, and re-layouts: 0.57 us -> 1.41 us
  transfers between devices with their start and end apart: 5 -> 5, of which waited for: 1 -> 1; matrix products, arithmetic and copies ran while one was open for 0% -> 0% of each run, Pallas kernels for 28% -> 27%
where the time goes in v15:
time: 39.6 us; the launch traced here: 39.3 us
  starting transfers between devices  18.1 us (46%)
  Pallas kernels  17.8 us (45%)
  waiting for transfers between devices  1.77 us (4%)
  local copies, waits for them, and re-layouts  1.41 us (4%)
    pallas_call x5, Pallas kernels, call(): pl.pallas_call(body, out_shape=out, in_specs=specs, out_specs=jax.tree.ma...  17.8 us
    all_to_all x1, starting transfers between devices, on_device(): upper = lax.all_to_all(up, 'dir', split_axis=0, concat_axis=0, tiled=True)  7.56 us
    all_to_all x1, starting transfers between devices, on_device(): lax.all_to_all(local, 'dir', split_axis=0, concat_axis=0, tiled=True)  5.67 us
    ppermute x1, starting transfers between devices, on_device(): from_cross = lax.ppermute(relay, BOTH, cross)  3.11 us
    all_to_all x1, waiting for transfers between devices, on_device(): upper = lax.all_to_all(up, 'dir', split_axis=0, concat_axis=0, tiled=True)  1.76 us
    unnamed x10, local copies, waits for them, and re-layouts  1.41 us
    ppermute x1, starting transfers between devices, on_device(): lax.ppermute(currents, BOTH, [(i, halo_target(i, boxes, dirs)) for i in r...  1.39 us
  transfers between devices with their start and end apart: 5, of which 1 were waited for; matrix products, arithmetic and copies ran while one was open for 0% of the time, Pallas kernels for 27%

profile of v15, /device:TPU:27, one launch (start us, length us, event | category | flops | bytes accessed | tf_op | source)
XLA Modules:
  0.0 39.3 jit_solution(4514450269068798064)
XLA Ops:
  0.0 1.4 %collective-permute-start = (bf16[64,512]{1,0:T(8,128)(2,1)}, bf16[64,512]{1,0:T(8,128)(2,1)S(1)}, u32[]{:S(2)}, u32[]{:S(2)}) collective-permute-start(bf16[64,512]{1,0:T(8,128)(2,1)} %own_ref.3), channel_id=1, source_target_pairs={{0,12},{1,13},{2,14},{3,15},{4,8},{5,9},{6,10},{7,11},{8,26},{9,27... | collective-permute-start | bytes 196616 | tf_op jit(solution)/shard_map/ppermute | solution.py:284
  1.4 0.1 pad_add_fusion.place_ref
  1.5 0.0 copy-start
  1.5 0.0 copy-start.1
  1.5 0.0 copy-start.4
  1.5 3.2 %shard_map.100 = (bf16[20,128,256]{2,1,0:T(8,128)(2,1)S(1)}, s32[128,32]{1,0:T(8,128)S(1)}, s32[64,32]{1,0:T(8,128)S(1)}, f32[8,2048]{1,0:T(8,128)S(1)}, f32[8,2048]{1,0:T(8,128)S(1)}) custom-call(s32[2]{0:T(128)S(1)} %pad_add_fusion.place_ref, s32[20,1024]{1,0:T(8,128)} %bitcast.7, s32[20,1024]{1,0:T(8,128)} %bitcast.8, f32[8,2048]{1,0:T(8,128)} %angle_hbm.1, ...), custom_call_target="tpu_custom_call" | custom-call | flops 5000000000 | bytes 11534336 | tf_op jit(solution)/shard_map/pallas_call | solution.py:23
  4.7 0.0 collective-permute-done.far_ref
  4.7 0.3 copy-done
  5.0 0.2 copy-done.1
  5.3 0.0 copy-done.4
  5.3 2.5 %shard_map.101 = (bf16[16,32,128]{2,1,0:T(8,128)(2,1)}, bf16[64,512]{1,0:T(8,128)(2,1)S(1)}, bf16[1024,256]{1,0:T(8,128)(2,1)S(1)}) custom-call(bf16[64,512]{1,0:T(8,128)(2,1)S(1)} %copy-done.4, bf16[64,512]{1,0:T(8,128)(2,1)S(1)} %collective-permute-done.far_ref, bf16[512,1024]{1,0:T(8,128)(2,1)S(1)} %copy-done.1, f32[8,2048]{1,0:T(8,128)S(1)} %get-tuple-element.15.cos_ref, ...), custom_call_target="tpu_custom_call" | custom-call | flops 1207959552 | bytes 10485760 | tf_op jit(solution)/shard_map/pallas_call | solution.py:23
  7.8 7.6 %all-to-all-start = ((bf16[16,32,128]{2,1,0:T(8,128)(2,1)}), bf16[16,32,128]{2,1,0:T(8,128)(2,1)S(1)}, u32[]{:S(2)}, u32[]{:S(2)}) async-start(bf16[16,32,128]{2,1,0:T(8,128)(2,1)} %get-tuple-element.17), calls=%async_computation | async-start | bytes 262144 | tf_op jit(solution)/shard_map/all_to_all | solution.py:336
  15.3 0.4 collective-permute-start.1
  15.7 3.1 %collective-permute-start.2 = (bf16[64,512]{1,0:T(8,128)(2,1)S(1)}, bf16[64,512]{1,0:T(8,128)(2,1)S(1)}, u32[]{:S(2)}, u32[]{:S(2)}) collective-permute-start(bf16[64,512]{1,0:T(8,128)(2,1)S(1)} %get-tuple-element.20), channel_id=1, source_target_pairs={{0,0},{1,2},{2,1},{3,4},{4,3},{5,6},{6,5},{7,8},{8,7},{9,10},{10,9... | collective-permute-start | bytes 196616 | tf_op jit(solution)/shard_map/ppermute | solution.py:339
  18.8 1.8 %all-to-all-done.upper_ref = bf16[16,32,128]{2,1,0:T(8,128)(2,1)S(1)} async-done(((bf16[16,32,128]{2,1,0:T(8,128)(2,1)}), bf16[16,32,128]{2,1,0:T(8,128)(2,1)S(1)}, u32[]{:S(2)}, u32[]{:S(2)}) %all-to-all-start) | async-done | bytes 131104 | tf_op jit(solution)/shard_map/all_to_all | solution.py:336
  20.6 1.3 %shard_map.102._ = bf16[16,16,128]{2,1,0:T(8,128)(2,1)} custom-call(bf16[16,32,128]{2,1,0:T(8,128)(2,1)S(1)} %all-to-all-done.upper_ref, s32[128,32]{1,0:T(8,128)S(1)} %get-tuple-element.18.index_ref, bf16[20,128,256]{2,1,0:T(8,128)(2,1)S(1)} %get-tuple-element.19.operator_ref), custom_call_target="tpu_custom_call" | custom-call | flops 335544320 | bytes 2097152 | tf_op jit(solution)/shard_map/pallas_call | solution.py:23
  21.9 5.7 %all-to-all-start.1 = ((bf16[16,16,128]{2,1,0:T(8,128)(2,1)}), bf16[16,16,128]{2,1,0:T(8,128)(2,1)S(1)}, u32[]{:S(2)}, u32[]{:S(2)}) async-start(bf16[16,16,128]{2,1,0:T(8,128)(2,1)} %shard_map.102._), calls=%async_computation.1 | async-start | bytes 131072 | tf_op jit(solution)/shard_map/all_to_all | solution.py:354
  27.6 0.0 collective-permute-done.1.sibling_ref
  27.6 0.0 collective-permute-done.2.cross_ref
  27.6 0.0 copy-start.3
  27.6 0.8 %copy-done.3 = bf16[16,16,128]{2,1,0:T(8,128)(2,1)S(1)} copy-done((bf16[16,16,128]{2,1,0:T(8,128)(2,1)S(1)}, bf16[16,16,128]{2,1,0:T(8,128)(2,1)}, u32[]{:S(2)}) %copy-start.3) | copy-done | bytes 65560
  28.5 0.0 copy-start.2
  28.5 6.0 %shard_map.103 = (f32[64,512]{1,0:T(8,128)S(1)}, bf16[1024,512]{1,0:T(8,128)(2,1)S(1)}) custom-call(bf16[64,512]{1,0:T(8,128)(2,1)S(1)} %copy-done.4, bf16[64,512]{1,0:T(8,128)(2,1)S(1)} %collective-permute-done.1.sibling_ref, bf16[64,512]{1,0:T(8,128)(2,1)S(1)} %collective-permute-done.2.cross_ref, s32[64,32]{1,0:T(8,128)S(1)} %get-tuple-element.21.col_ref, ...), custom_call_target="tpu_custom_call" | custom-call | flops 1132462080 | bytes 15728640 | tf_op jit(solution)/shard_map/pallas_call | solution.py:23
  34.5 0.0 all-to-all-done.1.inc_ref
  34.5 0.0 copy-done.2
  34.5 4.8 %shard_map.104 = f32[64,512]{1,0:T(8,128)} custom-call(bf16[16,16,128]{2,1,0:T(8,128)(2,1)S(1)} %all-to-all-done.1.inc_ref, f32[8,2048]{1,0:T(8,128)S(1)} %get-tuple-element.15.cos_ref, f32[8,2048]{1,0:T(8,128)S(1)} %get-tuple-element.16.sin_ref, f32[64,512]{1,0:T(8,128)S(1)} %get-tuple-element.22.near_ref, bf16[1024,512]{1,0:T(8,128)(2,1)S(1)} %copy-done.2, ...), custom_call_target="tpu_custom_call" | custom-call | flops 805306368 | bytes 10485760 | tf_op jit(solution)/shard_map/pallas_call | solution.py:23
Async XLA Ops:
  0.0 4.7 %collective-permute-start = (bf16[64,512]{1,0:T(8,128)(2,1)}, bf16[64,512]{1,0:T(8,128)(2,1)S(1)}, u32[]{:S(2)}, u32[]{:S(2)}) collective-permute-start(bf16[64,512]{1,0:T(8,128)(2,1)} %own_ref.3), channel_id=1, source_target_pairs={{0,12},{1,13},{2,14},{3,15},{4,8},{5,9},{6,10},{7,11},{8,26},{9,27... | collective-permute-start | bytes 196616 | tf_op jit(solution)/shard_map/ppermute | solution.py:284
  1.5 3.6 %copy-start = (bf16[1024,4096]{1,0:T(8,128)(2,1)S(1)}, bf16[1024,4096]{1,0:T(8,128)(2,1)}, u32[]{:S(2)}) copy-start(bf16[1024,4096]{1,0:T(8,128)(2,1)} %interp.5) | copy-start | bytes 25165828
  1.5 3.8 %copy-start.1 = (bf16[512,1024]{1,0:T(8,128)(2,1)S(1)}, bf16[512,1024]{1,0:T(8,128)(2,1)}, u32[]{:S(2)}) copy-start(bf16[512,1024]{1,0:T(8,128)(2,1)} %agg_ref.1) | copy-start | bytes 3145732
  1.5 3.8 %copy-start.4 = (bf16[64,512]{1,0:T(8,128)(2,1)S(1)}, bf16[64,512]{1,0:T(8,128)(2,1)}, u32[]{:S(2)}) copy-start(bf16[64,512]{1,0:T(8,128)(2,1)} %own_ref.3) | copy-start | bytes 196612
  7.8 12.8 %all-to-all-start = ((bf16[16,32,128]{2,1,0:T(8,128)(2,1)}), bf16[16,32,128]{2,1,0:T(8,128)(2,1)S(1)}, u32[]{:S(2)}, u32[]{:S(2)}) async-start(bf16[16,32,128]{2,1,0:T(8,128)(2,1)} %get-tuple-element.17), calls=%async_computation | async-start | bytes 262144 | tf_op jit(solution)/shard_map/all_to_all | solution.py:336
  15.3 12.3 %collective-permute-start.1 = (bf16[64,512]{1,0:T(8,128)(2,1)S(1)}, bf16[64,512]{1,0:T(8,128)(2,1)S(1)}, u32[]{:S(2)}, u32[]{:S(2)}) collective-permute-start(bf16[64,512]{1,0:T(8,128)(2,1)S(1)} %copy-done.4), channel_id=1, source_target_pairs={{0,1},{1,0},{2,3},{3,2},{4,5},{5,4},{6,7},{7,6},{8,9},{9,8},{10,11... | collective-permute-start | bytes 196616 | tf_op jit(solution)/shard_map/ppermute | solution.py:285
  15.7 11.9 %collective-permute-start.2 = (bf16[64,512]{1,0:T(8,128)(2,1)S(1)}, bf16[64,512]{1,0:T(8,128)(2,1)S(1)}, u32[]{:S(2)}, u32[]{:S(2)}) collective-permute-start(bf16[64,512]{1,0:T(8,128)(2,1)S(1)} %get-tuple-element.20), channel_id=1, source_target_pairs={{0,0},{1,2},{2,1},{3,4},{4,3},{5,6},{6,5},{7,8},{8,7},{9,10},{10,9... | collective-permute-start | bytes 196616 | tf_op jit(solution)/shard_map/ppermute | solution.py:339
  21.9 12.5 %all-to-all-start.1 = ((bf16[16,16,128]{2,1,0:T(8,128)(2,1)}), bf16[16,16,128]{2,1,0:T(8,128)(2,1)S(1)}, u32[]{:S(2)}, u32[]{:S(2)}) async-start(bf16[16,16,128]{2,1,0:T(8,128)(2,1)} %shard_map.102._), calls=%async_computation.1 | async-start | bytes 131072 | tf_op jit(solution)/shard_map/all_to_all | solution.py:354
  27.6 0.9 %copy-start.3 = (bf16[16,16,128]{2,1,0:T(8,128)(2,1)S(1)}, bf16[16,16,128]{2,1,0:T(8,128)(2,1)}, u32[]{:S(2)}) copy-start(bf16[16,16,128]{2,1,0:T(8,128)(2,1)} %shard_map.102._) | copy-start | bytes 196612
  28.5 6.0 %copy-start.2 = (bf16[1024,512]{1,0:T(8,128)(2,1)S(1)}, bf16[1024,512]{1,0:T(8,128)(2,1)}, u32[]{:S(2)}) copy-start(bf16[1024,512]{1,0:T(8,128)(2,1)} %receive_ref.1) | copy-start | bytes 3145732
